TPU v7x, 32 devices: a whole 2x2x4 slice. The times are simulated.
32 devices in a mesh: grp: 2 (over y), fsdp: 16 (over z, x, core).
Axes of the slice: x: 2, y: 2, z: 4, core: 2. Of those that a mesh axis runs over, the one named last changes fastest.
Arguments:
- hidden_in: bfloat16 [65536, 768], P(('grp', 'fsdp')), may hold values from -6 to 6
- out_grad: bfloat16 [65536, 768], P(('grp', 'fsdp')), may hold values from -6 to 6
- pooled_gradient: float32 [128, 2, 768], P(('grp', 'fsdp')), may hold values from -384 to 384
- gain_attn: bfloat16 [768], P('fsdp'), may hold values from 0.5 to 1.5
- w_query: bfloat16 [768, 768], P('fsdp'), may hold values from -0.0546875 to 0.0546875
- w_key: bfloat16 [768, 768], P('fsdp'), may hold values from -0.21875 to 0.21875
- w_value: bfloat16 [768, 768], P('fsdp'), may hold values from -0.21875 to 0.21875
- w_output: bfloat16 [768, 768], P('fsdp'), may hold values from -0.4375 to 0.4375
- rel_table: bfloat16 [384], P('fsdp'), may hold values from -4 to 4
- gain_ffn: bfloat16 [768], P('fsdp'), may hold values from 0.5 to 1.5
- w_in: bfloat16 [768, 3072], P('fsdp'), may hold values from -0.21875 to 0.21875
- w_out: bfloat16 [3072, 768], P('fsdp'), may hold values from -0.109375 to 0.109375
- pair_flags: int32 [65536], P(('grp', 'fsdp')), may hold values from 0 to 1, as said below
- instruction_mask: int32 [65536], P(('grp', 'fsdp')), may hold values from 0 to 1, as said below
Outputs:
- output: bfloat16 [65536, 768], P(('grp', 'fsdp'))
- pooled: float32 [128, 2, 768], P(('grp', 'fsdp'))
- input_grad: bfloat16 [65536, 768], P(('grp', 'fsdp'))
- grad_gain_attn: float32 [768], P('fsdp')
- grad_w_query: float32 [768, 768], P('fsdp')
- grad_w_key: float32 [768, 768], P('fsdp')
- grad_w_value: float32 [768, 768], P('fsdp')
- grad_w_output: float32 [768, 768], P('fsdp')
- grad_rel_table: float32 [384], P('fsdp')
- grad_gain_ffn: float32 [768], P('fsdp')
- grad_w_in: float32 [768, 3072], P('fsdp')
- grad_w_out: float32 [3072, 768], P('fsdp')
Inputs may be any that keep to these rules, and one draw needn't show every extreme that they name: `pair_flags`: in each sequence of 512 tokens, 0 on a first run and 1 on the rest; each run has 128 tokens or more. `instruction_mask`: 1 on a prefix of 1 to 64 tokens of each run of pair_flags, 0 elsewhere.
All inputs are finite; a program needn't handle non-finite values.
Results may differ from a plain program's by a relative error of at most 0.015.
Values may be sent and summed in bfloat16 or wider, within the bound.
A program may use at most 256 MiB of HBM per device.

v0:
```python
from functools import partial

import jax
import jax.numpy as jnp
from jax import lax
from jax.sharding import PartitionSpec as P

HEADS = 12
HEAD_DIM = 64
BUCKETS = 32
SEQUENCE_LENGTH = 512


EPS = 1e-06
NEG = -1e30
HIGH_PRECISION = lax.Precision.HIGHEST
LIMITS = (12, 16, 23, 32, 46, 64, 91)


def bucket_of(offset):
    distance = jnp.abs(offset)
    far_bucket = jnp.full(offset.shape, 8, jnp.int32)
    for threshold in LIMITS:
        far_bucket = far_bucket + (distance >= threshold).astype(jnp.int32)
    near_bucket = jnp.where(distance < 8, distance, far_bucket)
    return near_bucket + BUCKETS // 2 * (offset > 0).astype(jnp.int32)


def matmul(matrix, operand):
    return jnp.dot(matrix, operand, preferred_element_type=jnp.float32)


def left_product(matrix, operand):
    return lax.dot_general(
        matrix, operand, (((0,), (0,)), ((), ())), preferred_element_type=jnp.float32
    )


def right_product(matrix, operand):
    return lax.dot_general(
        matrix, operand, (((1,), (1,)), ((), ())), preferred_element_type=jnp.float32
    )


def rms_norm(tensor, scale_vec):
    return tensor * lax.rsqrt(jnp.mean(tensor * tensor, axis=-1, keepdims=True) + EPS) * scale_vec


def norm_back(tensor, scale_vec, cotangent):
    outcome, pullback = jax.vjp(rms_norm, tensor, scale_vec)
    return pullback(cotangent)


def pooling_weight_rows(flag_values, instruction_tokens):
    kept_tokens = (instruction_tokens.reshape(-1, SEQUENCE_LENGTH) == 0).astype(jnp.float32)
    which_part = (
        flag_values.reshape(-1, SEQUENCE_LENGTH)[:, None, :]
        == jnp.arange(2, dtype=jnp.int32)[None, :, None]
    ).astype(jnp.float32)
    chosen = which_part * kept_tokens[:, None, :]
    return chosen / jnp.sum(chosen, axis=-1, keepdims=True)


def toeplitz_rows(vector, length):
    tiled = jnp.tile(vector, length)[: length * (2 * length - 2)]
    return tiled.reshape(length, 2 * length - 2)[:, :length]


def diagonal_sums(matrix, length):
    padded = jnp.pad(jnp.flip(matrix, axis=1), ((0, 0), (0, length)))
    skewed = padded.reshape(-1)[: length * (2 * length - 1)].reshape(length, 2 * length - 1)
    return jnp.sum(skewed, axis=0)


def split_heads(matrix):
    return matrix.reshape(-1, SEQUENCE_LENGTH, HEADS, HEAD_DIM).transpose(2, 0, 1, 3)


def join_heads(stacked):
    return stacked.transpose(1, 2, 0, 3).reshape(-1, HEADS * HEAD_DIM)


def shards(
    hidden_in,
    out_grad,
    pooled_gradient,
    gain_attn,
    w_query,
    w_key,
    w_value,
    w_output,
    rel_table,
    gain_ffn,
    w_in,
    w_out,
    pair_flags,
    instruction_mask,
):
    query_all, key_all, value_all, output_all, gain_one, table_all = (
        lax.all_gather(w_query, "fsdp", axis=0, tiled=True),
        lax.all_gather(w_key, "fsdp", axis=0, tiled=True),
        lax.all_gather(w_value, "fsdp", axis=0, tiled=True),
        lax.all_gather(w_output, "fsdp", axis=0, tiled=True),
        lax.all_gather(gain_attn, "fsdp", axis=0, tiled=True),
        lax.all_gather(rel_table, "fsdp", axis=0, tiled=True),
    )
    position = jnp.arange(2 * SEQUENCE_LENGTH - 1, dtype=jnp.int32)
    circle_offset = jnp.where(
        position < SEQUENCE_LENGTH, position, position - (2 * SEQUENCE_LENGTH - 1)
    )
    bucket_ids = jnp.arange(BUCKETS, dtype=jnp.int32)[None, :]
    forward_table = (bucket_of(circle_offset)[:, None] == bucket_ids).astype(jnp.bfloat16)
    back_table = (bucket_of(SEQUENCE_LENGTH - 1 - position)[:, None] == bucket_ids).astype(
        jnp.float32
    )
    flag_rows = pair_flags.reshape(-1, SEQUENCE_LENGTH)
    same_part = flag_rows[:, :, None] == flag_rows[:, None, :]

    def head_scores(head_query, head_key, head_bias):
        scores = jnp.einsum(
            "sid,sjd->sij", head_query, head_key, preferred_element_type=jnp.float32
        )
        scores = scores + toeplitz_rows(head_bias, SEQUENCE_LENGTH)[None]
        return jnp.where(same_part, scores, NEG)

    def attend_head(pieces):
        head_query, head_key, head_value, head_bias = pieces
        scores = head_scores(head_query, head_key, head_bias)
        highest = jnp.max(scores, axis=-1, keepdims=True)
        exponent = jnp.exp(scores - highest)
        total = jnp.sum(exponent, axis=-1, keepdims=True)
        probabilities = exponent / total
        mixture = jnp.einsum(
            "sij,sjd->sid",
            probabilities.astype(jnp.bfloat16),
            head_value,
            preferred_element_type=jnp.float32,
        )
        return (mixture.astype(jnp.bfloat16), highest + jnp.log(total))

    def attend_back(pieces):
        head_query, head_key, head_value, head_bias, head_total, head_grad = pieces
        scores = head_scores(head_query, head_key, head_bias)
        probabilities = jnp.exp(scores - head_total)
        grad_value = jnp.einsum(
            "sij,sid->sjd",
            probabilities.astype(jnp.bfloat16),
            head_grad,
            preferred_element_type=jnp.float32,
        )
        grad_prob = jnp.einsum(
            "sid,sjd->sij", head_grad, head_value, preferred_element_type=jnp.float32
        )
        grad_scores = probabilities * (
            grad_prob - jnp.sum(probabilities * grad_prob, axis=-1, keepdims=True)
        )
        grad_low = grad_scores.astype(jnp.bfloat16)
        grad_query = jnp.einsum(
            "sij,sjd->sid", grad_low, head_key, preferred_element_type=jnp.float32
        )
        grad_key = jnp.einsum(
            "sij,sid->sjd", grad_low, head_query, preferred_element_type=jnp.float32
        )
        diagonal = diagonal_sums(jnp.sum(grad_low.astype(jnp.float32), axis=0), SEQUENCE_LENGTH)
        return (
            grad_query.astype(jnp.bfloat16),
            grad_key.astype(jnp.bfloat16),
            grad_value.astype(jnp.bfloat16),
            diagonal,
        )

    hidden = hidden_in.astype(jnp.float32)
    gain_first = gain_one.astype(jnp.float32)
    normed = rms_norm(hidden, gain_first).astype(jnp.bfloat16)
    queries = matmul(normed, query_all).astype(jnp.bfloat16)
    keys_proj = matmul(normed, key_all).astype(jnp.bfloat16)
    values_proj = matmul(normed, value_all).astype(jnp.bfloat16)
    bias_rows = matmul(forward_table, table_all.reshape(BUCKETS, HEADS)).T
    mixture, log_total = lax.map(
        attend_head,
        (split_heads(queries), split_heads(keys_proj), split_heads(values_proj), bias_rows),
    )
    mixed_rows = join_heads(mixture)
    middle = hidden + matmul(mixed_rows, output_all)
    inner_all, outer_all, gain_two = (
        lax.all_gather(w_in, "fsdp", axis=0, tiled=True),
        lax.all_gather(w_out, "fsdp", axis=0, tiled=True),
        lax.all_gather(gain_ffn, "fsdp", axis=0, tiled=True),
    )
    gain_second = gain_two.astype(jnp.float32)
    normed_two = rms_norm(middle, gain_second).astype(jnp.bfloat16)
    inner_value = matmul(normed_two, inner_all)
    activation = jax.nn.gelu(inner_value, approximate=True).astype(jnp.bfloat16)
    final_output = middle + matmul(activation, outer_all)
    weight_pooling_matrix = pooling_weight_rows(pair_flags, instruction_mask)
    pooled = jnp.einsum(
        "qgu,quv->qgv",
        weight_pooling_matrix,
        final_output.reshape(-1, SEQUENCE_LENGTH, final_output.shape[1]),
        precision=HIGH_PRECISION,
    )
    inner_all, outer_all, gain_two = (
        lax.all_gather(w_in, "fsdp", axis=0, tiled=True),
        lax.all_gather(w_out, "fsdp", axis=0, tiled=True),
        lax.all_gather(gain_ffn, "fsdp", axis=0, tiled=True),
    )
    grad_result = out_grad.astype(jnp.float32) + jnp.einsum(
        "hkx,hkw->hxw", weight_pooling_matrix, pooled_gradient, precision=HIGH_PRECISION
    ).reshape(final_output.shape)
    branch_grad = grad_result.astype(jnp.bfloat16)
    grad_outer = left_product(activation, branch_grad)
    grad_act = right_product(branch_grad, outer_all)
    gelu_value, gelu_pull = jax.vjp(partial(jax.nn.gelu, approximate=True), inner_value)
    inner_low = gelu_pull(grad_act)[0].astype(jnp.bfloat16)
    grad_inner_w = left_product(normed_two, inner_low)
    grad_normed_two = right_product(inner_low, inner_all)
    grad_middle_part, grad_gain_two = norm_back(
        middle, gain_two.astype(jnp.float32), grad_normed_two
    )
    grad_middle = grad_result + grad_middle_part
    ffn_shards = (
        lax.psum_scatter(grad_inner_w, "fsdp", scatter_dimension=0, tiled=True),
        lax.psum_scatter(grad_outer, "fsdp", scatter_dimension=0, tiled=True),
        lax.psum_scatter(grad_gain_two, "fsdp", scatter_dimension=0, tiled=True),
    )
    query_all, key_all, value_all, output_all, gain_one, table_all = (
        lax.all_gather(w_query, "fsdp", axis=0, tiled=True),
        lax.all_gather(w_key, "fsdp", axis=0, tiled=True),
        lax.all_gather(w_value, "fsdp", axis=0, tiled=True),
        lax.all_gather(w_output, "fsdp", axis=0, tiled=True),
        lax.all_gather(gain_attn, "fsdp", axis=0, tiled=True),
        lax.all_gather(rel_table, "fsdp", axis=0, tiled=True),
    )
    out_low = grad_middle.astype(jnp.bfloat16)
    grad_output_w = left_product(mixed_rows, out_low)
    grad_mixture = right_product(out_low, output_all).astype(jnp.bfloat16)
    bias_back = matmul(forward_table, table_all.reshape(BUCKETS, HEADS)).T
    grad_heads_q, grad_heads_k, grad_heads_v, diagonals = lax.map(
        attend_back,
        (
            split_heads(queries),
            split_heads(keys_proj),
            split_heads(values_proj),
            bias_back,
            log_total,
            split_heads(grad_mixture),
        ),
    )
    grad_table = jnp.dot(diagonals, back_table, precision=HIGH_PRECISION).T.reshape(-1)
    grad_queries = join_heads(grad_heads_q)
    grad_keys = join_heads(grad_heads_k)
    grad_values = join_heads(grad_heads_v)
    grad_query_w = left_product(normed, grad_queries)
    grad_key_w = left_product(normed, grad_keys)
    grad_value_w = left_product(normed, grad_values)
    grad_normed = (
        right_product(grad_queries, query_all)
        + right_product(grad_keys, key_all)
        + right_product(grad_values, value_all)
    )
    grad_hidden_part, grad_gain_one = norm_back(hidden, gain_one.astype(jnp.float32), grad_normed)
    input_grad = (grad_middle + grad_hidden_part).astype(jnp.bfloat16)
    attn_shards = (
        lax.psum_scatter(grad_gain_one, "fsdp", scatter_dimension=0, tiled=True),
        lax.psum_scatter(grad_query_w, "fsdp", scatter_dimension=0, tiled=True),
        lax.psum_scatter(grad_key_w, "fsdp", scatter_dimension=0, tiled=True),
        lax.psum_scatter(grad_value_w, "fsdp", scatter_dimension=0, tiled=True),
        lax.psum_scatter(grad_output_w, "fsdp", scatter_dimension=0, tiled=True),
        lax.psum_scatter(grad_table, "fsdp", scatter_dimension=0, tiled=True),
    )
    shard_set = attn_shards + (ffn_shards[2], ffn_shards[0], ffn_shards[1])
    summed = (
        lax.psum(shard_set[0].astype(jnp.bfloat16), "grp").astype(jnp.float32),
        lax.psum(shard_set[1].astype(jnp.bfloat16), "grp").astype(jnp.float32),
        lax.psum(shard_set[2].astype(jnp.bfloat16), "grp").astype(jnp.float32),
        lax.psum(shard_set[3].astype(jnp.bfloat16), "grp").astype(jnp.float32),
        lax.psum(shard_set[4].astype(jnp.bfloat16), "grp").astype(jnp.float32),
        lax.psum(shard_set[5].astype(jnp.bfloat16), "grp").astype(jnp.float32),
        lax.psum(shard_set[6].astype(jnp.bfloat16), "grp").astype(jnp.float32),
        lax.psum(shard_set[7].astype(jnp.bfloat16), "grp").astype(jnp.float32),
        lax.psum(shard_set[8].astype(jnp.bfloat16), "grp").astype(jnp.float32),
    )
    return (
        final_output.astype(jnp.bfloat16),
        pooled,
        input_grad,
        summed[0],
        summed[1],
        summed[2],
        summed[3],
        summed[4],
        summed[5],
        summed[6],
        summed[7],
        summed[8],
    )


def solution(mesh):
    placed = (
        P(("grp", "fsdp"), None),
        P(("grp", "fsdp"), None),
        P(("grp", "fsdp"), None, None),
        P("fsdp"),
        P("fsdp", None),
        P("fsdp", None),
        P("fsdp", None),
        P("fsdp", None),
        P("fsdp"),
        P("fsdp"),
        P("fsdp", None),
        P("fsdp", None),
        P(("grp", "fsdp")),
        P(("grp", "fsdp")),
    )
    return jax.shard_map(
        shards,
        mesh=mesh,
        in_specs=placed,
        out_specs=(
            P(("grp", "fsdp"), None),
            P(("grp", "fsdp"), None, None),
            P(("grp", "fsdp"), None),
            P("fsdp"),
            P("fsdp", None),
            P("fsdp", None),
            P("fsdp", None),
            P("fsdp", None),
            P("fsdp"),
            P("fsdp"),
            P("fsdp", None),
            P("fsdp", None),
        ),
        check_vma=False,
    )
```

profile of v0, /device:TPU:0, one launch (start us, length us, event | category | flops | bytes accessed | tf_op | source)
XLA Modules:
  0.0 1477.2 jit_solution(5024421882680148349)
XLA Ops:
  16.4 35.6 %all-reduce.8 = (bf16[768]{0:T(1024)(128)(2,1)S(1)}, bf16[384]{0:T(512)(128)(2,1)S(1)}, bf16[768]{0:T(1024)(128)(2,1)S(1)}) all-reduce(bf16[768]{0:T(1024)(128)(2,1)S(1)} %dynamic-update-slice, bf16[384]{0:T(512)(128)(2,1)S(1)} %dynamic-update-slice.1, bf16[768]{0:T(1024)(128)(2,1)S(1)} %dynamic-update-slice.2), channel_id=1, replica_groups=mesh['grp'=2,'fsdp'=16] {'fsdp'}, use_global_device_ids=true, to_apply=%add.1 | all-reduce | flops 1920 | bytes 7680
  58.5 6.0 fusion.100
  82.5 6.2 reshape.231
  103.2 6.3 reshape.232
  114.0 16.9 %all-gather.11.cloned.1.call-done = bf16[768,768]{1,0:T(8,128)(2,1)} async-done(((bf16[48,768]{1,0:T(8,128)(2,1)}), bf16[768,768]{1,0:T(8,128)(2,1)}) %all-gather.11.cloned.1.call-update) | async-done | bytes 1179664 | tf_op jit(solution)/shard_map/all_gather | solution.py:102
  150.0 203.7 %while.32 = (s32[]{:T(128)}, bf16[12,4,512,64]{2,3,1,0:T(8,128)(2,1)}, f32[12,4,512,1]{2,1,3,0:T(4,128)}, bf16[12,4,512,64]{2,3,1,0:T(8,128)(2,1)}, bf16[12,4,51...) while((s32[]{:T(128)}, ...), condition=%wide.region_4.5_spmd.clone, body=%wide.region_1.4_spmd.clone.sunk | while | flops 284293120 | bytes 37843564 | solution.py:179
  360.8 7.8 multiply_reduce_fusion.3
  368.6 18.2 %fusion.105 = f32[2048,3072]{1,0:T(8,128)} fusion(bf16[768,3072]{1,0:T(8,128)(2,1)} %all-gather.15.cloned.1.call-done, f32[2048,768]{1,0:T(8,128)} %get-tuple-element.407, f32[768]{0:T(1024)S(1)} %convert_element_type.276, f32[2048]{0:T(1024)S(1)} %fusion.79), kind=kOutput, calls=%fused_computation.146 | convolution fusion | flops 9668395008 | bytes 36187136 | tf_op jit(solution)/shard_map/dot_general | solution.py:30
  386.8 27.6 %fusion.56 = bf16[2048,3072]{1,0:T(8,128)(2,1)} fusion(f32[2048,3072]{1,0:T(8,128)} %fusion.105, bf16[2048,768]{1,0:T(8,128)(2,1)S(1)} %copy-done.18, bf16[3072,768]{1,0:T(8,128)(2,1)} %all-gather.17.cloned.1.call-done), kind=kOutput, calls=%fused_computation.66 | convolution fusion | flops 9789505536 | bytes 45613056 | tf_op jit(solution)/shard_map/dot_general | solution.py:40
  414.4 17.4 %multiply_reduce_fusion.1 = (f32[768]{0:T(1024)}, f32[2048]{0:T(1024)S(1)}, f32[2048,768]{1,0:T(8,128)}) fusion(f32[2048,768]{1,0:T(8,128)S(1)} %copy-done.13, f32[2048]{0:T(1024)S(1)} %fusion.79, f32[768]{0:T(1024)S(1)} %convert_element_type.276, bf16[2048,3072]{1,0:T(8,128)(2,1)} %fusion.56, bf16[768,3072]{1,0:T(8,128)(2,1)} %all-gather.15.cloned.1.call-done), kind=kOutput, calls=%fused_computation.85 | convolution fusion | flops 9673110528 | bytes 29906944 | tf_op jit(solution)/shard_map/dot_general | solution.py:40
  431.8 5.9 fusion.61
  444.5 7.1 convolution_convert_fusion.2
  465.2 517.6 %while.33 = (s32[]{:T(128)}, bf16[12,4,512,64]{2,3,1,0:T(8,128)(2,1)}, bf16[12,4,512,64]{2,3,1,0:T(8,128)(2,1)}, bf16[12,4,512,64]{2,3,1,0:T(8,128)(2,1)}, f32[1...) while((s32[]{:T(128)}, ...), condition=%wide.region_12.13_spmd.clone, body=%wide.region_8.12_spmd.clone.sunk | while | flops 684323328 | bytes 125882608 | solution.py:238
  1018.4 17.5 %fusion.104 = f32[768,3072]{1,0:T(8,128)} fusion(bf16[2048,3072]{1,0:T(8,128)(2,1)} %fusion.56, f32[2048,768]{1,0:T(8,128)} %get-tuple-element.407, f32[768]{0:T(1024)S(1)} %convert_element_type.276, f32[2048]{0:T(1024)S(1)} %fusion.79), kind=kOutput, calls=%fused_computation.145 | convolution fusion | flops 9668395008 | bytes 28322816 | tf_op jit(solution)/shard_map/dot_general | solution.py:34
  1036.5 21.5 %fusion.106 = f32[3072,768]{1,0:T(8,128)} fusion(bf16[2048,768]{1,0:T(8,128)(2,1)} %fusion.66, f32[2048,3072]{1,0:T(8,128)} %fusion.105), kind=kOutput, calls=%fused_computation.147 | convolution fusion | flops 9720299520 | bytes 37748736 | tf_op jit(solution)/shard_map/dot_general | solution.py:34
  1068.2 6.5 fusion.60
  1074.8 60.7 %all-reduce.7 = (bf16[768]{0:T(1024)(128)(2,1)S(1)}, bf16[384]{0:T(512)(128)(2,1)S(1)}, bf16[768]{0:T(1024)(128)(2,1)S(1)}) all-reduce(f32[768]{0:T(1024)S(1)} %get-tuple-element.341, f32[384]{0:T(512)S(1)} %reshape.242, f32[768]{0:T(1024)S(1)} %copy-done.30), channel_id=2, replica_groups=mesh['grp'=2,'fsdp'=16] {'fsdp'}, use_global_device_ids=true, to_apply=%region_15.16.clone | all-reduce | flops 1920 | bytes 11520
  1142.4 24.0 %fusion.117 = (bf16[2048,768]{1,0:T(8,128)(2,1)}, f32[2048,768]{1,0:T(8,128)}) fusion(f32[2048,768]{1,0:T(8,128)} %get-tuple-element.407, bf16[3072,768]{1,0:T(8,128)(2,1)} %all-gather.17.cloned.1.call-done, f32[2048,3072]{1,0:T(8,128)} %fusion.105), kind=kOutput, calls=%fused_computation.152 | convolution fusion | flops 9723445248 | bytes 45613056 | tf_op jit(solution)/shard_map/dot_general | solution.py:30
  1166.4 6.5 fusion.102
  1177.6 11.9 reduce-scatter.11.cloned.1.call-done
  1191.0 113.0 %reduce-scatter.15.cloned.1.call-done = f32[48,3072]{1,0:T(8,128)} async-done(((f32[768,3072]{1,0:T(8,128)}), f32[48,3072]{1,0:T(8,128)}) %reduce-scatter.15.cloned.1.call-update) | async-done | bytes 589840 | tf_op jit(solution)/shard_map/reduce_scatter | solution.py:222
  1305.8 113.9 %reduce-scatter.17.cloned.1.call-done = f32[192,768]{1,0:T(8,128)} async-done(((f32[3072,768]{1,0:T(8,128)}), f32[192,768]{1,0:T(8,128)}) %reduce-scatter.17.cloned.1.call-update) | async-done | bytes 589840 | tf_op jit(solution)/shard_map/reduce_scatter | solution.py:223
  1421.5 6.7 fusion.63
  1428.2 32.5 %all-reduce.13.cloned.1.call-done = (bf16[48,768]{1,0:T(8,128)(2,1)}, bf16[48,768]{1,0:T(8,128)(2,1)}, bf16[48,768]{1,0:T(8,128)(2,1)}, bf16[48,768]{1,0:T(8,128...) async-done(((bf16[48,768]{1,0:T(8,128)(2,1)}, bf16[48,768]{1,0:T(8,128)(2,1)}, bf16[48,768]{1,0:T(8,128)(2,1)}, bf16[48,768]{1,0:T(8,128)(2,1)}, ...) | async-done | bytes 884752 | tf_op jit(solution)/shard_map/psum | solution.py:274
  (664 shorter events, 888.5 us)
Async XLA Ops:
  7.2 51.4 %copy-start = (f32[4,2,768]{2,1,0:T(2,128)S(1)}, f32[4,2,768]{2,1,0:T(2,128)}, u32[]{:S(2)}) copy-start(f32[4,2,768]{2,1,0:T(2,128)} %param.20) | copy-start | bytes 73732
  7.2 65.3 %all-gather.7.cloned.1.call-start = ((), (), s32[]{:S(2)}) async-start(), calls=%async_computation.6 | async-start | bytes 1253376 | tf_op jit(solution)/shard_map/all_gather | solution.py:100
  7.9 85.2 %all-gather.9.cloned.1.call-start = ((), (), s32[]{:S(2)}) async-start(), calls=%async_computation.7 | async-start | bytes 1253376 | tf_op jit(solution)/shard_map/all_gather | solution.py:101
  8.7 122.2 %all-gather.11.cloned.1.call-start = ((), (), s32[]{:S(2)}) async-start(), calls=%async_computation.8 | async-start | bytes 1253376 | tf_op jit(solution)/shard_map/all_gather | solution.py:102
  9.4 351.3 %all-gather.13.cloned.1.call-start = ((), (), s32[]{:S(2)}) async-start(), calls=%async_computation.9 | async-start | bytes 1253376 | tf_op jit(solution)/shard_map/all_gather | solution.py:103
  10.0 358.6 %all-gather.15.cloned.1.call-start = ((), (), s32[]{:S(2)}) async-start(), calls=%async_computation.10 | async-start | bytes 5013504 | tf_op jit(solution)/shard_map/all_gather | solution.py:186
  10.6 376.2 %all-gather.17.cloned.1.call-start = ((), (), s32[]{:S(2)}) async-start(), calls=%async_computation.11 | async-start | bytes 5013504 | tf_op jit(solution)/shard_map/all_gather | solution.py:187
  11.2 1161.8 %reduce-scatter.13.cloned.1.call-start = ((), (), s32[]{:S(2)}) async-start(), calls=%async_computation.15 | async-start | bytes 2506752 | tf_op jit(solution)/shard_map/reduce_scatter | solution.py:268
  52.1 78.8 %copy-start.26 = (f32[768]{0:T(1024)}, f32[768]{0:T(1024)S(1)}, u32[]{:S(2)}) copy-start(f32[768]{0:T(1024)S(1)} %convert_element_type.264) | copy-start | bytes 9220
  55.3 75.6 %copy-start.22 = (f32[2048]{0:T(1024)}, f32[2048]{0:T(1024)S(1)}, u32[]{:S(2)}) copy-start(f32[2048]{0:T(1024)S(1)} %fusion.78) | copy-start | bytes 24580
  58.5 14.0 copy-start.28
  368.6 18.2 %copy-start.18 = (bf16[2048,768]{1,0:T(8,128)(2,1)S(1)}, bf16[2048,768]{1,0:T(8,128)(2,1)}, u32[]{:S(2)}) copy-start(bf16[2048,768]{1,0:T(8,128)(2,1)} %fusion.66) | copy-start | bytes 9437188
  386.8 27.6 %copy-start.13 = (f32[2048,768]{1,0:T(8,128)S(1)}, f32[2048,768]{1,0:T(8,128)}, u32[]{:S(2)}) copy-start(f32[2048,768]{1,0:T(8,128)} %get-tuple-element.407) | copy-start | bytes 18874372
  414.4 17.5 %copy-start.10 = (bf16[2048,768]{1,0:T(8,128)(2,1)S(1)}, bf16[2048,768]{1,0:T(8,128)(2,1)}, u32[]{:S(2)}) copy-start(bf16[2048,768]{1,0:T(8,128)(2,1)} %param.19) | copy-start | bytes 9437188
  444.4 730.1 %reduce-scatter.7.cloned.1.call-start = ((), (), s32[]{:S(2)}) async-start(), calls=%async_computation.12 | async-start | bytes 2506752 | tf_op jit(solution)/shard_map/reduce_scatter | solution.py:265
  994.6 181.5 %reduce-scatter.9.cloned.1.call-start = ((), (), s32[]{:S(2)}) async-start(), calls=%async_computation.13 | async-start | bytes 2506752 | tf_op jit(solution)/shard_map/reduce_scatter | solution.py:266
  1006.4 183.1 %reduce-scatter.11.cloned.1.call-start = ((), (), s32[]{:S(2)}) async-start(), calls=%async_computation.14 | async-start | bytes 2506752 | tf_op jit(solution)/shard_map/reduce_scatter | solution.py:267
  1018.4 285.6 %reduce-scatter.15.cloned.1.call-start = ((), (), s32[]{:S(2)}) async-start(), calls=%async_computation.16 | async-start | bytes 10027008 | tf_op jit(solution)/shard_map/reduce_scatter | solution.py:222
  1036.0 383.6 %reduce-scatter.17.cloned.1.call-start = ((), (), s32[]{:S(2)}) async-start(), calls=%async_computation.17 | async-start | bytes 10027008 | tf_op jit(solution)/shard_map/reduce_scatter | solution.py:223
  1058.0 402.6 %all-reduce.13.cloned.1.call-start = ((), (), s32[]{:S(2)}) async-start(), calls=%async_computation.18 | async-start | bytes 1769472 | tf_op jit(solution)/shard_map/psum | solution.py:274
  1068.2 74.2 %copy-start.25 = (f32[2048]{0:T(1024)S(1)}, f32[2048]{0:T(1024)}, u32[]{:S(2)}) copy-start(f32[2048]{0:T(1024)} %copy-done.24) | copy-start | bytes 24580
  1142.4 24.0 %copy-start.21 = (f32[4,512]{1,0:T(4,128)S(1)}, f32[4,512]{1,0:T(4,128)}, u32[]{:S(2)}) copy-start(f32[4,512]{1,0:T(4,128)} %copy-done.20) | copy-start | bytes 24580
  1142.4 24.0 %copy-start.29 = (f32[4,2]{1,0:T(4,128)S(1)}, f32[4,2]{1,0:T(4,128)}, u32[]{:S(2)}) copy-start(f32[4,2]{1,0:T(4,128)} %copy-done.28) | copy-start | bytes 100
  1421.5 49.0 %copy-start.1 = (f32[4,2,768]{2,1,0:T(2,128)S(1)}, f32[4,2,768]{2,1,0:T(2,128)}, u32[]{:S(2)}) copy-start(f32[4,2,768]{2,1,0:T(2,128)} %param.20) | copy-start | bytes 73732
  (80 other events, 234.2 us)
Sparse Core Ops, SparseCore 0:
  10.3 41.1 all-gather.6
  53.8 37.3 all-gather.8
  93.5 37.3 all-gather.10
  133.0 37.3 all-gather.12
  172.5 52.2 all-gather.14
  226.9 51.7 all-gather.16
  444.5 62.3 reduce-scatter.12
  994.7 62.5 reduce-scatter.6
  1061.1 62.3 reduce-scatter.8
  1127.6 61.8 reduce-scatter.10
  1193.6 110.3 reduce-scatter.14
  1308.5 111.1 reduce-scatter.16
  1423.5 37.1 all-reduce.12
where the time goes:
time: 1490 us; the launch traced here: 1480 us
  local copies, waits for them, and re-layouts  519 us (35%)
  matrix products  435 us (29%)
  waiting for transfers between devices  292 us (20%)
  other arithmetic  110 us (7%)
  blocking collectives  101 us (7%)
  between operations  17.2 us (1%)
    reduce_scatter x1, waiting for transfers between devices, shards(): lax.psum_scatter(grad_outer, 'fsdp', scatter_dimension=0, tiled=True)  114 us
    reduce_scatter x1, waiting for transfers between devices, shards(): lax.psum_scatter(grad_inner_w, 'fsdp', scatter_dimension=0, tiled=True)  113 us
    unnamed x2, blocking collectives  96.4 us
    dot_general x24, matrix products, head_scores(): jnp.einsum('sid,sjd->sij', head_query, head_key, preferred_element_type=j...  77.6 us
    another operation x48, local copies, waits for them, and re-layouts, toeplitz_rows(): tiled = jnp.tile(vector, length)[:length * (2 * length - 2)]  69.2 us
    reshape x24, local copies, waits for them, and re-layouts, toeplitz_rows(): return tiled.reshape(length, 2 * length - 2)[:, :length]  68.9 us
    dot_general x6, matrix products, right_product(): lax.dot_general(matrix, operand, (((1,), (1,)), ((), ())), preferred_elem...  66.5 us
    dot_general x7, matrix products, matmul(): return jnp.dot(matrix, operand, preferred_element_type=jnp.float32)  66.4 us
  transfers between devices with their start and end apart: 13, of which 5 were waited for; matrix products, arithmetic and copies ran while one was open for 64% of the time, Pallas kernels for 0%

commit v1 on v0

v1 whole, which is shorter than its diff:
```python
from functools import partial

import jax
import jax.numpy as jnp
from jax import lax
from jax.experimental import pallas as pl
from jax.experimental.pallas import tpu as pltpu
from jax.sharding import PartitionSpec as P

HEADS = 12
HEAD_DIM = 64
BUCKETS = 32
LENGTH = 512
BLOCK = 128
BLOCKS = LENGTH // BLOCK
PAIRS = HEADS // 2
BAND = 5 * BLOCK
EPS = 1e-06
NEG = -1e30
LIMITS = (12, 16, 23, 32, 46, 64, 91)
ROOT = 0.7978845608028654
CUBE = 0.044715
F32 = jnp.float32
BF16 = jnp.bfloat16
ANY = pl.BlockSpec(memory_space=pl.ANY)
VMEM_LIMIT = 62 * 1024 * 1024


def bucket_of(offset):
    distance = jnp.abs(offset)
    far_bucket = jnp.full(offset.shape, 8, jnp.int32)
    for threshold in LIMITS:
        far_bucket = far_bucket + (distance >= threshold).astype(jnp.int32)
    near_bucket = jnp.where(distance < 8, distance, far_bucket)
    return near_bucket + BUCKETS // 2 * (offset > 0).astype(jnp.int32)


def dot(a, b):
    return lax.dot_general(a, b, (((1,), (0,)), ((), ())), preferred_element_type=F32)


def dot_nt(a, b):
    return lax.dot_general(a, b, (((1,), (1,)), ((), ())), preferred_element_type=F32)


def dot_tn(a, b):
    return lax.dot_general(a, b, (((0,), (0,)), ((), ())), preferred_element_type=F32)


def iota(shape, axis):
    return lax.broadcasted_iota(jnp.int32, shape, axis)


def whole(shape):
    zeros = (0,) * len(shape)
    return pl.BlockSpec(shape, lambda *_: zeros, pipeline_mode=pl.Buffered(1))


def columns_of(row):
    return (0, BLOCKS - 1) if row == 0 else (1, BLOCKS) if row == BLOCKS - 1 else (0, BLOCKS)


def span(first, last):
    return slice(first * BLOCK, last * BLOCK)


def half_mask(half):
    return (iota((1, BLOCK), 1) // HEAD_DIM == half).astype(F32).astype(BF16)


def pool_terms(flags, instruction):
    kept = (instruction == 0).astype(F32)
    chosen = [kept * (flags == part).astype(F32) for part in range(2)]
    counts = [jnp.sum(one, axis=1, keepdims=True) for one in chosen]
    return chosen, counts


def pool_gradient(chosen, counts, pooled_grad):
    row = iota((16, LENGTH), 0)
    picks = jnp.where(row % 2 == 0, chosen[0], chosen[1])
    picks = jnp.where(row < 6, picks, 0.0).astype(BF16)
    scaled = [pooled_grad[part : part + 1, :] / counts[part] for part in range(2)]
    width = pooled_grad.shape[1]
    line = iota((16, width), 0)
    both = jnp.where(line % 2 == 0, scaled[0], scaled[1])
    high = both.astype(BF16).astype(F32)
    rest = both - high
    middle = rest.astype(BF16).astype(F32)
    low = rest - middle
    parts = jnp.where(line < 2, high, jnp.where(line < 4, middle, jnp.where(line < 6, low, 0.0)))
    return dot_tn(picks, parts.astype(BF16))


def attend_kernel(
    x_ref, og_ref, pg_ref, flags_ref, instr_ref, gain1_ref, gain2_ref, table_ref, wq_ref, wk_ref, wv_ref, wo_ref,
    q_ref, k_ref, v_ref, p_ref, mix_ref, mid_ref, n2_ref, bg_ref,
    band_ref, auxq_ref, auxk_ref,
):
    @pl.when(pl.program_id(0) == 0)
    def _():
        table = table_ref[...]

        def one_head(head, _):
            line = jnp.sum(jnp.where(iota((16, 2 * LENGTH), 0) == head, table, 0.0), axis=0, keepdims=True)
            turned = pltpu.roll(jnp.broadcast_to(line, (BLOCK, 2 * LENGTH)), 0, 1, stride=1, stride_axis=0)
            band_ref[head] = turned[:, BLOCK : BLOCK + BAND]
            return 0

        lax.fori_loop(0, HEADS, one_head, 0)

    flags, instruction = flags_ref[0], instr_ref[0]
    chosen, counts = pool_terms(flags, instruction)
    grad_result = og_ref[...].astype(F32) + pool_gradient(chosen, counts, pg_ref[0])
    bg_ref[...] = grad_result.astype(BF16)

    row = iota((16, LENGTH), 0)
    which = jnp.where(row == 0, 1 - flags, jnp.where(row == 1, flags, 0)).astype(F32).astype(BF16)
    lane, line = iota((16, BLOCK), 1), iota((16, BLOCK), 0)
    own = jnp.where((lane == line) & (line < 2), 1.0, 0.0).astype(BF16)
    other = jnp.where((lane == 1 - line) & (line < 2), NEG, 0.0).astype(BF16)
    auxq_ref[...] = dot_tn(which, own).astype(BF16)
    auxk_ref[...] = dot_tn(which, other).astype(BF16)

    hidden = x_ref[...].astype(F32)
    scale = lax.rsqrt(jnp.mean(hidden * hidden, axis=1, keepdims=True) + EPS)
    normed = (hidden * scale * gain1_ref[...]).astype(BF16)
    q_ref[...] = dot(normed, wq_ref[...]).astype(BF16)
    k_ref[...] = dot(normed, wk_ref[...]).astype(BF16)
    v_ref[...] = dot(normed, wv_ref[...]).astype(BF16)

    def one_pair(pair, _):
        lanes = pl.ds(pl.multiple_of(pair * BLOCK, BLOCK), BLOCK)
        keys = jnp.concatenate([k_ref[:, lanes], auxk_ref[...]], axis=1)
        values = v_ref[:, lanes]
        for index in range(BLOCKS):
            first, last = columns_of(index)
            shift = 2 - index
            total = None
            for half in range(2):
                head = pair * 2 + half
                query = q_ref[span(index, index + 1), lanes] * half_mask(half)
                query = jnp.concatenate([query, auxq_ref[span(index, index + 1), :]], axis=1)
                scores = dot_nt(query, keys[span(first, last)]) + band_ref[head, :, span(first + shift, last + shift)]
                exponent = jnp.exp(scores - jnp.max(scores, axis=1, keepdims=True))
                probability = exponent * (1.0 / jnp.sum(exponent, axis=1, keepdims=True))
                probability = probability.astype(BF16)
                p_ref[0, head, span(index, index + 1), span(first, last)] = probability
                part = dot(probability, values[span(first, last)] * half_mask(half))
                total = part if total is None else total + part
            mix_ref[span(index, index + 1), lanes] = total.astype(BF16)
        return 0

    lax.fori_loop(0, PAIRS, one_pair, 0)

    middle = hidden + dot(mix_ref[...], wo_ref[...])
    mid_ref[...] = middle
    scale = lax.rsqrt(jnp.mean(middle * middle, axis=1, keepdims=True) + EPS)
    n2_ref[...] = (middle * scale * gain2_ref[...]).astype(BF16)


def attend(x, og, pg, flags, instr, gain1, gain2, table, wq, wk, wv, wo):
    tokens, width = x.shape
    seqs = tokens // LENGTH
    rows = pl.BlockSpec((LENGTH, width), lambda s: (s, 0))
    flag_rows = pl.BlockSpec((1, 1, LENGTH), lambda s: (s, 0, 0))
    low = jax.ShapeDtypeStruct((tokens, width), BF16)
    return pl.pallas_call(
        attend_kernel,
        name="attend",
        grid=(seqs,),
        in_specs=[
            rows, rows, pl.BlockSpec((1, 2, width), lambda s: (s, 0, 0)), flag_rows, flag_rows,
            whole((1, width)), whole((1, width)), whole((16, 2 * LENGTH)),
            whole((width, width)), whole((width, width)), whole((width, width)), whole((width, width)),
        ],
        out_specs=[
            rows, rows, rows, pl.BlockSpec((1, HEADS, LENGTH, LENGTH), lambda s: (s, 0, 0, 0)), rows, rows, rows, rows,
        ],
        out_shape=[
            low, low, low, jax.ShapeDtypeStruct((seqs, HEADS, LENGTH, LENGTH), BF16), low,
            jax.ShapeDtypeStruct((tokens, width), F32), low, low,
        ],
        scratch_shapes=[
            pltpu.VMEM((HEADS, BLOCK, BAND), F32), pltpu.VMEM((LENGTH, BLOCK), BF16), pltpu.VMEM((LENGTH, BLOCK), BF16),
        ],
        compiler_params=pltpu.CompilerParams(vmem_limit_bytes=VMEM_LIMIT),
    )(x, og, pg, flags, instr, gain1, gain2, table, wq, wk, wv, wo)


FF_CHUNK = 512


def feed_kernel(
    n2_ref, bg_ref, mid_hbm, flags_ref, instr_ref, win_ref, wout_ref,
    out_ref, pooled_ref, dn2_ref, dwin_ref, dwout_ref,
    res_ref, act_ref, dinner_ref, sem,
):
    step, steps = pl.program_id(0), pl.num_programs(0)
    seqs = n2_ref.shape[0] // LENGTH

    @pl.when(step == 0)
    def _():
        copy = pltpu.make_async_copy(mid_hbm, res_ref, sem)
        copy.start()
        dn2_ref[...] = jnp.zeros_like(dn2_ref)
        copy.wait()

    def one_block(block, _):
        rows = pl.ds(pl.multiple_of(block * LENGTH, LENGTH), LENGTH)
        win, wout = win_ref[...], wout_ref[...]
        inner = dot(n2_ref[rows, :], win)
        square = inner * inner
        half = 0.5 * jnp.tanh(inner * (ROOT + (ROOT * CUBE) * square)) + 0.5
        active = inner * half
        slope = half + active * (1.0 - half) * (2.0 * ROOT + (6.0 * ROOT * CUBE) * square)
        active = active.astype(BF16)
        act_ref[rows, :] = active
        res_ref[rows, :] += dot(active, wout)
        dinner = (dot_nt(bg_ref[rows, :], wout) * slope).astype(BF16)
        dinner_ref[rows, :] = dinner
        dn2_ref[rows, :] += dot_nt(dinner, win)
        return 0

    lax.fori_loop(0, seqs, one_block, 0)
    dwin_ref[...] = dot_tn(n2_ref[...], dinner_ref[...]).astype(dwin_ref.dtype)
    dwout_ref[...] = dot_tn(act_ref[...], bg_ref[...]).astype(dwout_ref.dtype)

    @pl.when(step == steps - 1)
    def _():
        for seq in range(seqs):
            rows = slice(seq * LENGTH, (seq + 1) * LENGTH)
            result = res_ref[rows, :]
            out_ref[rows, :] = result.astype(BF16)
            chosen, counts = pool_terms(flags_ref[seq], instr_ref[seq])
            line = iota((8, LENGTH), 0)
            picks = jnp.where(line == 0, chosen[0], jnp.where(line == 1, chosen[1], 0.0)).astype(BF16)
            high = result.astype(BF16)
            low = (result - high.astype(F32)).astype(BF16)
            total = dot(picks, high) + dot(picks, low)
            side = iota((8, 1), 0)
            total = total / jnp.where(side == 0, counts[0], counts[1])
            pooled_ref[seq] = total[0:2, :]


def feed(n2, bg, mid, flags, instr, win, wout):
    tokens, width = n2.shape
    seqs = tokens // LENGTH
    ff = win.shape[1]
    chunk = FF_CHUNK
    return pl.pallas_call(
        feed_kernel,
        name="feed",
        grid=(ff // chunk,),
        in_specs=[
            whole((tokens, width)), whole((tokens, width)), ANY,
            whole((seqs, 1, LENGTH)), whole((seqs, 1, LENGTH)),
            pl.BlockSpec((width, chunk), lambda c: (0, c)), pl.BlockSpec((chunk, width), lambda c: (c, 0)),
        ],
        out_specs=[
            whole((tokens, width)), whole((seqs, 2, width)), whole((tokens, width)),
            pl.BlockSpec((width, chunk), lambda c: (0, c)), pl.BlockSpec((chunk, width), lambda c: (c, 0)),
        ],
        out_shape=[
            jax.ShapeDtypeStruct((tokens, width), BF16), jax.ShapeDtypeStruct((seqs, 2, width), F32),
            jax.ShapeDtypeStruct((tokens, width), F32),
            jax.ShapeDtypeStruct((width, ff), BF16), jax.ShapeDtypeStruct((ff, width), BF16),
        ],
        scratch_shapes=[
            pltpu.VMEM((tokens, width), F32), pltpu.VMEM((tokens, chunk), BF16), pltpu.VMEM((tokens, chunk), BF16),
            pltpu.SemaphoreType.DMA,
        ],
        compiler_params=pltpu.CompilerParams(vmem_limit_bytes=VMEM_LIMIT),
    )(n2, bg, mid, flags, instr, win, wout)


def norm_back(value, gain, cotangent):
    scale = lax.rsqrt(jnp.mean(value * value, axis=1, keepdims=True) + EPS)
    scaled = cotangent * gain
    inner = jnp.mean(scaled * value, axis=1, keepdims=True)
    unit = value * scale
    return scale * (scaled - unit * (scale * inner)), jnp.sum(cotangent * unit, axis=0, keepdims=True)


def back_kernel(
    x_ref, og_ref, pg_ref, flags_ref, instr_ref, mid_ref, dn2_ref, mix_ref, q_ref, k_ref, v_ref, p_hbm,
    gain1_ref, gain2_ref, wq_ref, wk_ref, wv_ref, wo_ref,
    ig_ref, dqkv_ref, dwo_ref, dgain_ref, diag_ref,
    band_ref, dwo_acc, normed_ref, grads_ref, dmix_ref, gm_ref, p_buf, ds_ref, sems,
):
    seq, seqs = pl.program_id(0), pl.num_programs(0)

    def p_copy(at):
        slot = lax.rem(at, 2)
        return pltpu.make_async_copy(
            p_hbm.at[lax.div(at, PAIRS), pl.ds(lax.rem(at, PAIRS) * 2, 2)], p_buf.at[slot], sems.at[slot]
        )

    @pl.when(seq == 0)
    def _():
        p_copy(0).start()
        band_ref[...] = jnp.zeros_like(band_ref)
        dwo_acc[...] = jnp.zeros_like(dwo_acc)
        dgain_ref[...] = jnp.zeros_like(dgain_ref)

    chosen, counts = pool_terms(flags_ref[0], instr_ref[0])
    grad_result = og_ref[...].astype(F32) + pool_gradient(chosen, counts, pg_ref[0])
    part, gain_part = norm_back(mid_ref[...], gain2_ref[...], dn2_ref[...])
    dgain_ref[1:2, :] += gain_part
    grad_middle = grad_result + part
    gm_ref[...] = grad_middle
    out_low = grad_middle.astype(BF16)
    dmix_ref[...] = dot_nt(out_low, wo_ref[...]).astype(BF16)
    dwo_acc[...] += dot_tn(mix_ref[...], out_low)

    rows = pl.ds(pl.multiple_of(seq * LENGTH, LENGTH), LENGTH)
    width = x_ref.shape[1]

    def one_pair(pair, _):
        at = seq * PAIRS + pair
        slot = lax.rem(at, 2)

        @pl.when(at + 1 < seqs * PAIRS)
        def _():
            p_copy(at + 1).start()

        p_copy(at).wait()
        lanes = pl.ds(pl.multiple_of(pair * BLOCK, BLOCK), BLOCK)
        queries, keys, grads = q_ref[:, lanes], k_ref[:, lanes], dmix_ref[:, lanes]
        values = jnp.concatenate([v_ref[:, lanes], jnp.full((LENGTH, BLOCK), -1.0, BF16)], axis=1)
        product = (grads.astype(F32) * mix_ref[:, lanes].astype(F32)).astype(BF16)
        dq = [None] * BLOCKS
        dk = [None] * BLOCKS
        dv = [None] * BLOCKS

        def add(total, index, part):
            total[index] = part if total[index] is None else total[index] + part

        for half in range(2):
            head = pair * 2 + half
            mask = half_mask(half)
            grad_half = grads * mask
            both = jnp.concatenate([grad_half, product * mask], axis=1)
            key_half, query_half = keys * mask, queries * mask
            for index in range(BLOCKS):
                first, last = columns_of(index)
                shift = 2 - index
                mine = span(index, index + 1)
                grad_prob = dot_nt(both[mine], values[span(first, last)])
                grad_scores = p_buf[slot, half, mine, span(first, last)].astype(F32) * grad_prob
                band_ref[head, :, span(first + shift, last + shift)] += grad_scores
                low = grad_scores.astype(BF16)
                ds_ref[half, mine, span(first, last)] = low
                add(dq, index, dot(low, key_half[span(first, last)]))
            for index in range(BLOCKS):
                first, last = columns_of(index)
                mine = span(index, index + 1)
                seen = span(first, last)
                add(dk, index, dot_tn(ds_ref[half, seen, mine], query_half[seen]))
                add(dv, index, dot_tn(p_buf[slot, half, seen, mine], grad_half[seen]))
        for which, total in enumerate((dq, dk, dv)):
            at_lane = pl.ds(pl.multiple_of(which * width + pair * BLOCK, BLOCK), BLOCK)
            for index in range(BLOCKS):
                at_row = pl.ds(pl.multiple_of(seq * LENGTH + index * BLOCK, BLOCK), BLOCK)
                grads_ref[at_row, at_lane] = total[index].astype(BF16)
        return 0

    lax.fori_loop(0, PAIRS, one_pair, 0)

    hidden = x_ref[...].astype(F32)
    scale = lax.rsqrt(jnp.mean(hidden * hidden, axis=1, keepdims=True) + EPS)
    normed_ref[rows, :] = (hidden * scale * gain1_ref[...]).astype(BF16)
    grad_normed = (
        dot_nt(grads_ref[rows, 0:width], wq_ref[...])
        + dot_nt(grads_ref[rows, width : 2 * width], wk_ref[...])
        + dot_nt(grads_ref[rows, 2 * width : 3 * width], wv_ref[...])
    )
    part, gain_part = norm_back(hidden, gain1_ref[...], grad_normed)
    dgain_ref[0:1, :] += gain_part
    ig_ref[...] = (gm_ref[...] + part).astype(BF16)

    @pl.when(seq == seqs - 1)
    def _():
        dwo_ref[...] = dwo_acc[...].astype(BF16)

        def one_part(part, _):
            lanes = pl.ds(pl.multiple_of(part * 256, 256), 256)
            dqkv_ref[:, lanes] = dot_tn(normed_ref[...], grads_ref[:, lanes]).astype(BF16)
            return 0

        lax.fori_loop(0, 3 * width // 256, one_part, 0)

        def one_head(head, _):
            total = jnp.zeros((8, 6 * BLOCK), F32)
            for group in range(BLOCK // 8):
                wide = band_ref[head, 8 * group : 8 * group + 8, :]
                wide = jnp.concatenate([wide, jnp.zeros((8, 6 * BLOCK - BAND), F32)], axis=1)
                total = total + pltpu.roll(wide, BLOCK - 8 * group, 1)
            line = iota((8, 6 * BLOCK), 0)
            turned = total
            for row in range(1, 8):
                turned = jnp.where(line == row, pltpu.roll(total, 6 * BLOCK - row, 1), turned)
            diag_ref[head] = jnp.broadcast_to(jnp.sum(turned, axis=0, keepdims=True), (8, 6 * BLOCK))
            return 0

        lax.fori_loop(0, HEADS, one_head, 0)


def back(x, og, pg, flags, instr, mid, dn2, mix, q, k, v, p, gain1, gain2, wq, wk, wv, wo):
    tokens, width = x.shape
    seqs = tokens // LENGTH
    rows = pl.BlockSpec((LENGTH, width), lambda s: (s, 0))
    flag_rows = pl.BlockSpec((1, 1, LENGTH), lambda s: (s, 0, 0))
    square = whole((width, width))
    return pl.pallas_call(
        back_kernel,
        name="back",
        grid=(seqs,),
        in_specs=[
            rows, rows, pl.BlockSpec((1, 2, width), lambda s: (s, 0, 0)), flag_rows, flag_rows,
            rows, rows, rows, rows, rows, rows, ANY,
            whole((1, width)), whole((1, width)), square, square, square, square,
        ],
        out_specs=[
            rows, whole((width, 3 * width)), square, whole((8, width)), whole((HEADS, 8, 6 * BLOCK)),
        ],
        out_shape=[
            jax.ShapeDtypeStruct((tokens, width), BF16), jax.ShapeDtypeStruct((width, 3 * width), BF16),
            jax.ShapeDtypeStruct((width, width), BF16), jax.ShapeDtypeStruct((8, width), F32),
            jax.ShapeDtypeStruct((HEADS, 8, 6 * BLOCK), F32),
        ],
        scratch_shapes=[
            pltpu.VMEM((HEADS, BLOCK, BAND), F32), pltpu.VMEM((width, width), F32), pltpu.VMEM((tokens, width), BF16),
            pltpu.VMEM((tokens, 3 * width), BF16), pltpu.VMEM((LENGTH, width), BF16), pltpu.VMEM((LENGTH, width), F32),
            pltpu.VMEM((2, 2, LENGTH, LENGTH), BF16), pltpu.VMEM((2, LENGTH, LENGTH), BF16), pltpu.SemaphoreType.DMA((2,)),
        ],
        compiler_params=pltpu.CompilerParams(vmem_limit_bytes=VMEM_LIMIT),
    )(x, og, pg, flags, instr, mid, dn2, mix, q, k, v, p, gain1, gain2, wq, wk, wv, wo)


DEPTH, WIDE, CORES = 4, 2, 2
MESH_ID = pl.DeviceIdType.MESH
GATHER_PHASES = 7
SCATTER_PHASES = 8
UP0, UP1, UP2, DOWN0, ACROSS_X, ACROSS_Y, ACROSS_C = range(7)


def place():
    grp, at = lax.axis_index("grp"), lax.axis_index("fsdp")
    z, x, core = lax.div(at, WIDE * CORES), lax.rem(lax.div(at, CORES), WIDE), lax.rem(at, CORES)

    def device(grp, z, x, core):
        return (grp, z * (WIDE * CORES) + x * CORES + core)

    edge = (z == 0) | (z == DEPTH - 1)
    low = z < DEPTH // 2
    return dict(
        y=grp, z=z, x=x, core=core, edge=edge, low=low,
        over_y=device(1 - grp, z, x, core),
        over_x=device(grp, z, 1 - x, core),
        over_core=device(grp, z, x, 1 - core),
        inward=device(grp, jnp.where(low, z + 1, z - 1), x, core),
        outward=device(grp, jnp.where(low, 0, DEPTH - 1), x, core),
    )


def greet(here):
    barrier = pltpu.get_barrier_semaphore()
    for name in ("over_y", "over_x", "over_core", "inward"):
        pl.semaphore_signal(barrier, inc=1, device_id=here[name], device_id_type=MESH_ID)

    @pl.when(jnp.logical_not(here["edge"]))
    def _():
        pl.semaphore_signal(barrier, inc=1, device_id=here["outward"], device_id_type=MESH_ID)
        pl.semaphore_wait(barrier, 5)

    @pl.when(here["edge"])
    def _():
        pl.semaphore_wait(barrier, 4)


def gather_phase(phase, piece, here, whole_ref, sent, got):
    y, z, x, core, edge, low = (here[name] for name in ("y", "z", "x", "core", "edge", "low"))
    inner = jnp.logical_not(edge)
    half = whole_ref.shape[-1] // 2
    mine = jnp.where(low, 0, DEPTH - 1)
    next_in = jnp.where(low, z + 1, z - 1)
    other_edge = DEPTH - 1 - mine

    def copy(where, channel, *target):
        ref = whole_ref.at[(piece, *where)]
        return pltpu.make_async_remote_copy(
            src_ref=ref, dst_ref=ref, send_sem=sent.at[channel, piece], recv_sem=got.at[channel, piece],
            device_id=target[0], device_id_type=MESH_ID,
        )

    line = lambda at: (at, x, core)
    x_half = (slice(None), x, core, slice(None), pl.ds(pl.multiple_of(y * half, half), half))
    x_half_in = (slice(None), 1 - x, core, slice(None), pl.ds(pl.multiple_of(y * half, half), half))
    y_half_in = (slice(None), 1 - x, core, slice(None), pl.ds(pl.multiple_of((1 - y) * half, half), half))
    inward, outward = here["inward"], here["outward"]
    if phase == 0:
        @pl.when(edge)
        def _():
            copy(line(z), 8, inward).start()

        @pl.when(inner)
        def _():
            copy(line(z), 0, inward).start()
            copy(line(z), 1, outward).start()
    elif phase == 1:
        @pl.when(inner)
        def _():
            copy(line(z), 0, inward).wait_send()
            copy(line(z), 1, outward).wait_send()
            copy(line(mine), 8, outward).wait_recv()
            copy(line(mine), 2, inward).start()
            copy(line(next_in), 0, inward).wait_recv()
            copy(line(next_in), 3, outward).start()

        @pl.when(edge)
        def _():
            copy(line(z), 8, inward).wait_send()
            copy(line(next_in), 1, inward).wait_recv()
    elif phase == 2:
        @pl.when(inner)
        def _():
            copy(line(mine), 2, inward).wait_send()
            copy(line(next_in), 3, outward).wait_send()
            copy(line(other_edge), 2, inward).wait_recv()
            copy(line(other_edge), 4, outward).start()

        @pl.when(edge)
        def _():
            copy(line(jnp.where(low, 2, 1)), 3, inward).wait_recv()
    elif phase == 3:
        @pl.when(inner)
        def _():
            copy(line(other_edge), 4, outward).wait_send()

        @pl.when(edge)
        def _():
            copy(line(other_edge), 4, inward).wait_recv()

        copy(x_half, 5, here["over_x"]).start()
    elif phase == 4:
        copy(x_half, 5, here["over_x"]).wait_send()
        copy(x_half_in, 5, here["over_x"]).wait_recv()
        copy(x_half_in, 6, here["over_y"]).start()
    elif phase == 5:
        copy(x_half_in, 6, here["over_y"]).wait_send()
        copy(y_half_in, 6, here["over_y"]).wait_recv()
        copy((slice(None), slice(None), core), 7, here["over_core"]).start()
    else:
        copy((slice(None), slice(None), core), 7, here["over_core"]).wait_send()
        copy((slice(None), slice(None), 1 - core), 7, here["over_core"]).wait_recv()


def scatter_phase(phase, piece, here, part_ref, out_ref, own, fromc, fromy, fromx, fromz, last, sent, got, own_sem):
    y, z, x, core, edge, low = (here[name] for name in ("y", "z", "x", "core", "edge", "low"))
    inner = jnp.logical_not(edge)
    half = part_ref.shape[-1] // 2
    slot = lax.rem(piece, 2)
    inward, outward = here["inward"], here["outward"]

    def remote(source, target, channel, device):
        return pltpu.make_async_remote_copy(
            src_ref=source, dst_ref=target, send_sem=sent.at[channel, piece], recv_sem=got.at[channel, piece],
            device_id=device, device_id_type=MESH_ID,
        )

    def lanes(which):
        return pl.ds(pl.multiple_of(which * half, half), half)

    def add(target, source):
        target[...] = (target[...].astype(F32) + source[...].astype(F32)).astype(BF16)

    total = fromc.at[piece]
    over_core = lambda: remote(part_ref.at[piece, :, :, 1 - core], fromc.at[piece], 0, here["over_core"])
    load = lambda: pltpu.make_async_copy(part_ref.at[piece, :, :, core], own.at[slot], own_sem.at[slot])
    over_y = lambda: remote(fromc.at[piece, :, 1 - x, :, lanes(1 - y)], fromy.at[piece], 1, here["over_y"])
    over_x = lambda: remote(fromc.at[piece, :, 1 - x, :, lanes(y)], fromx.at[piece], 2, here["over_x"])
    rest = pl.ds(jnp.where(low, 1, 0), 3)
    edge_in = lambda: remote(fromc.at[piece, rest, x], fromz.at[piece, pl.ds(0, 3)], 3, inward)
    far = pl.ds(jnp.where(low, 2, 0), 2)
    near = pl.ds(jnp.where(low, 0, 2), 2)
    across = lambda: remote(fromc.at[piece, far, x], fromz.at[piece, pl.ds(3, 2)], 4, inward)
    mine = jnp.where(low, 0, DEPTH - 1)
    back = lambda: remote(fromc.at[piece, mine, x], fromz.at[piece, 5], 5, outward)
    final = lambda: remote(fromc.at[piece, z, x], last.at[piece], 6, here["over_y"])

    if phase == 0:
        over_core().start()
        load().start()
    elif phase == 1:
        load().wait()
        over_core().wait()

        def one(at, _):
            for side in range(WIDE):
                add(total.at[at, side], own.at[slot, at, side])
            return 0

        lax.fori_loop(0, DEPTH, one, 0)
        over_y().start()
    elif phase == 2:
        over_y().wait()

        def one(at, _):
            add(total.at[at, 1 - x, :, lanes(y)], fromy.at[piece, at])
            return 0

        lax.fori_loop(0, DEPTH, one, 0)
        over_x().start()
    elif phase == 3:
        over_x().wait()

        def one(at, _):
            add(total.at[at, x, :, lanes(y)], fromx.at[piece, at])
            return 0

        lax.fori_loop(0, DEPTH, one, 0)

        @pl.when(edge)
        def _():
            edge_in().start()
    elif phase == 4:
        @pl.when(edge)
        def _():
            edge_in().wait_send()

        @pl.when(inner)
        def _():
            edge_in().wait_recv()
            for at in range(3):
                add(total.at[jnp.where(low, 1, 0) + at, x], fromz.at[piece, at])
            across().start()
    elif phase == 5:
        @pl.when(inner)
        def _():
            across().wait()
            for at in range(2):
                add(total.at[jnp.where(low, 0, 2) + at, x], fromz.at[piece, 3 + at])
            back().start()
    elif phase == 6:
        @pl.when(inner)
        def _():
            back().wait_send()

        @pl.when(edge)
        def _():
            back().wait_recv()
            add(total.at[z, x], fromz.at[piece, 5])

        final().start()
    else:
        final().wait()
        out_ref[piece] = fromc[piece, z, x].astype(F32) + last[piece].astype(F32)


def run_slot(slot, pieces, phases, stride, delay, act):
    for phase in reversed(range(phases)):
        since = slot - phase * delay
        piece = lax.div(since, stride)

        @pl.when((since >= 0) & (lax.rem(since, stride) == 0) & (piece < pieces))
        def _(phase=phase, piece=piece):
            act(phase, piece)


def gather_sems(pieces):
    return [pltpu.SemaphoreType.DMA((9, pieces)), pltpu.SemaphoreType.DMA((9, pieces))]


def scatter_scratch(pieces, rows, columns):
    return [
        pltpu.VMEM((2, DEPTH, WIDE, rows, columns), BF16),
        pltpu.VMEM((pieces, DEPTH, WIDE, rows, columns), BF16),
        pltpu.VMEM((pieces, DEPTH, rows, columns // 2), BF16),
        pltpu.VMEM((pieces, DEPTH, rows, columns // 2), BF16),
        pltpu.VMEM((pieces, 6, rows, columns), BF16),
        pltpu.VMEM((pieces, rows, columns), BF16),
        pltpu.SemaphoreType.DMA((7, pieces)),
        pltpu.SemaphoreType.DMA((7, pieces)),
        pltpu.SemaphoreType.DMA((2,)),
    ]


def gather_kernel(share_ref, whole_ref, sent, got, own_sem):
    here = place()
    pieces = share_ref.shape[0]
    own = [
        pltpu.make_async_copy(share_ref.at[piece], whole_ref.at[piece, here["z"], here["x"], here["core"]], own_sem.at[piece])
        for piece in range(pieces)
    ]
    for one in own:
        one.start()
    greet(here)
    for one in own:
        one.wait()

    def step(slot, _):
        run_slot(slot, pieces, GATHER_PHASES, 1, 1, lambda f, p: gather_phase(f, p, here, whole_ref, sent, got))
        return 0

    lax.fori_loop(0, pieces + GATHER_PHASES - 1, step, 0)


def gather_all(shares, collective_id):
    pieces, rows, columns = shares.shape
    return pl.pallas_call(
        gather_kernel,
        name="gather",
        in_specs=[ANY],
        out_specs=ANY,
        out_shape=jax.ShapeDtypeStruct((pieces, DEPTH, WIDE, CORES, rows, columns), shares.dtype),
        scratch_shapes=gather_sems(pieces) + [pltpu.SemaphoreType.DMA((pieces,))],
        compiler_params=pltpu.CompilerParams(collective_id=collective_id, has_side_effects=True),
    )(shares)


def scatter_kernel(part_ref, out_ref, *scratch):
    here = place()
    pieces = part_ref.shape[0]
    greet(here)

    def step(slot, _):
        run_slot(slot, pieces, SCATTER_PHASES, 1, 1, lambda f, p: scatter_phase(f, p, here, part_ref, out_ref, *scratch))
        return 0

    lax.fori_loop(0, pieces + SCATTER_PHASES - 1, step, 0)


def scatter_all(parts, collective_id):
    pieces, _, _, _, rows, columns = parts.shape
    return pl.pallas_call(
        scatter_kernel,
        name="scatter",
        in_specs=[ANY],
        out_specs=pl.BlockSpec(memory_space=pltpu.VMEM),
        out_shape=jax.ShapeDtypeStruct((pieces, rows, columns), F32),
        scratch_shapes=scatter_scratch(pieces, rows, columns),
        compiler_params=pltpu.CompilerParams(
            collective_id=collective_id, has_side_effects=True, vmem_limit_bytes=VMEM_LIMIT
        ),
    )(parts)


def shards(
    hidden_in, out_grad, pooled_gradient, gain_attn, w_query, w_key, w_value, w_output, rel_table, gain_ffn, w_in, w_out,
    pair_flags, instruction_mask, *, fast,
):
    width = hidden_in.shape[1]
    ff = w_in.shape[1]
    if fast:
        rows = w_query.shape[0]
        small = jnp.zeros((rows, width), BF16)
        small = small.at[:, 0].set(gain_attn).at[:, 1].set(gain_ffn).at[: rel_table.shape[0], 2].set(rel_table)
        pieces = jnp.concatenate(
            [
                jnp.stack([small, w_query, w_key, w_value, w_output]),
                w_in.reshape(rows, ff // width, width).transpose(1, 0, 2),
                w_out.reshape(ff // width, rows, width),
            ]
        )
        pieces = gather_all(pieces, 1).reshape(-1, width, width)
        small, wq, wk, wv, wo = (pieces[at] for at in range(5))
        win = pieces[5:9].transpose(1, 0, 2).reshape(width, ff)
        wout = pieces[9:13].reshape(ff // width, -1, rows, width).transpose(1, 0, 2, 3).reshape(ff, width)
        gain1, gain2 = small[:, 0], small[:, 1]
        rel = small[:, 2].reshape(-1, rows)[:, : rel_table.shape[0]].reshape(-1)
    else:
        gather = lambda one: lax.all_gather(one, "fsdp", axis=0, tiled=True)
        wq, wk, wv, wo, win, wout = map(gather, (w_query, w_key, w_value, w_output, w_in, w_out))
        gain1, gain2, rel = map(gather, (gain_attn, gain_ffn, rel_table))
    gain1, gain2 = gain1.astype(F32)[None, :], gain2.astype(F32)[None, :]
    position = jnp.arange(2 * LENGTH, dtype=jnp.int32)
    onehot = bucket_of(position - 3 * BLOCK)[None, :] == jnp.arange(BUCKETS, dtype=jnp.int32)[:, None]
    table = lax.dot_general(
        rel.reshape(BUCKETS, HEADS), onehot.astype(BF16), (((0,), (0,)), ((), ())), preferred_element_type=F32
    )
    table = jnp.pad(table, ((0, 16 - HEADS), (0, 0)))
    flags = pair_flags.reshape(-1, 1, LENGTH)
    instr = instruction_mask.reshape(-1, 1, LENGTH)
    q, k, v, p, mix, mid, n2, bg = attend(
        hidden_in, out_grad, pooled_gradient, flags, instr, gain1, gain2, table, wq, wk, wv, wo
    )
    output, pooled, dn2, dwin, dwout = feed(n2, bg, mid, flags, instr, win, wout)
    input_grad, dqkv, dwo, dgain, diag = back(
        hidden_in, out_grad, pooled_gradient, flags, instr, mid, dn2, mix, q, k, v, p, gain1, gain2, wq, wk, wv, wo
    )
    offset = jnp.arange(6 * BLOCK, dtype=jnp.int32) - 3 * BLOCK
    buckets = (bucket_of(offset)[:, None] == jnp.arange(BUCKETS, dtype=jnp.int32)[None, :]).astype(F32)
    grad_table = jnp.dot(diag[:, 0, :], buckets, precision=lax.Precision.HIGHEST).T.reshape(-1)
    if fast:
        devices = width // rows
        small = jnp.zeros((devices, rows, width), F32)
        small = small.at[:, :, 0].set(dgain[0].reshape(devices, rows)).at[:, :, 1].set(dgain[1].reshape(devices, rows))
        small = small.at[:, : rel_table.shape[0], 2].set(grad_table.reshape(devices, -1))
        parts = [small.astype(BF16)[None]]
        parts += [dqkv[:, at * width : (at + 1) * width].reshape(1, devices, rows, width) for at in range(3)]
        parts += [dwo.reshape(1, devices, rows, width)]
        parts += [dwin.reshape(devices, rows, ff // width, width).transpose(2, 0, 1, 3)]
        parts += [dwout.reshape(devices, ff // width, rows, width).transpose(1, 0, 2, 3)]
        sums = scatter_all(jnp.concatenate(parts).reshape(-1, DEPTH, WIDE, CORES, rows, width), 2)
        small = sums[0]
        return (
            output, pooled, input_grad,
            small[:, 0], sums[1], sums[2], sums[3], sums[4], small[: rel_table.shape[0], 2], small[:, 1],
            sums[5:9].transpose(1, 0, 2).reshape(rows, ff), sums[9:13].reshape(-1, width),
        )
    scatter = lambda one: lax.psum(lax.psum_scatter(one, "fsdp", scatter_dimension=0, tiled=True), "grp").astype(F32)
    return (
        output, pooled, input_grad,
        scatter(dgain[0]), scatter(dqkv[:, :width]), scatter(dqkv[:, width : 2 * width]), scatter(dqkv[:, 2 * width :]),
        scatter(dwo), scatter(grad_table), scatter(dgain[1]), scatter(dwin), scatter(dwout),
    )


def solution(mesh):
    tokens, square, line = P(("grp", "fsdp"), None), P("fsdp", None), P("fsdp")
    cube, flat = P(("grp", "fsdp"), None, None), P(("grp", "fsdp"))
    fast = mesh.shape["fsdp"] == DEPTH * WIDE * CORES and mesh.shape["grp"] == 2
    return jax.shard_map(
        partial(shards, fast=fast),
        mesh=mesh,
        in_specs=(tokens, tokens, cube, line, square, square, square, square, line, line, square, square, flat, flat),
        out_specs=(tokens, cube, tokens, line, square, square, square, square, line, line, square, square),
        check_vma=False,
    )
```

time: 1490 us -> 556 us (0.37)
  Pallas kernels: 0 us -> 471 us
  local copies, waits for them, and re-layouts: 519 us -> 71.6 us
  matrix products: 435 us -> 0.65 us
  waiting for transfers between devices: 292 us -> 0 us
  blocking collectives: 101 us -> 0 us
  other arithmetic: 110 us -> 10.6 us
  between operations: 17.2 us -> 0.88 us
    pallas_call x0 -> x5, Pallas kernels: none -> 471 us  [the longest x1 126 us: gather_all(): pl.pallas_call(gather_kernel, name='gather', in_specs=[ANY], out_specs=AN...]
    dot_general x106 -> x2, matrix products: 435 us -> 0.65 us  [the longest x1 0.48 us: shards(): jnp.dot(diag[:, 0, :], buckets, precision=lax.Precision.HIGHEST)]
    reduce_scatter x6 -> x0, waiting for transfers between devices: 239 us -> none  [the longest x1 114 us: shards(): lax.psum_scatter(grad_outer, 'fsdp', scatter_dimension=0, tiled=True)]
    reshape x42 -> x5, local copies, waits for them, and re-layouts: 141 us -> 16.8 us  [the longest x2 12.9 us: shards(): dwin.reshape(devices, rows, ff // width, width).transpose(2, 0, 1, 3)]
    unnamed x2 -> x0, blocking collectives: 96.4 us -> none
    another operation x52 -> x9, local copies, waits for them, and re-layouts: 77.3 us -> 2.55 us  [the longest x48 69.2 us: toeplitz_rows(): tiled = jnp.tile(vector, length)[:length * (2 * length - 2)]]
    rev x12 -> x0, local copies, waits for them, and re-layouts: 63.1 us -> none  [diagonal_sums(): padded = jnp.pad(jnp.flip(matrix, axis=1), ((0, 0), (0, length)))]
    reduce_sum x38 -> x0, other arithmetic: 62.9 us -> none  [the longest x12 23.6 us: attend_head(): total = jnp.sum(exponent, axis=-1, keepdims=True)]
  transfers between devices with their start and end apart: 13 -> 0, of which waited for: 5 -> 0; matrix products, arithmetic and copies ran while one was open for 64% -> 0% of each run, Pallas kernels for 0% -> 0%
where the time goes in v1:
time: 556 us; the launch traced here: 555 us
  Pallas kernels  471 us (85%)
  local copies, waits for them, and re-layouts  71.6 us (13%)
  other arithmetic  10.6 us (2%)
    pallas_call x1, Pallas kernels, gather_all(): pl.pallas_call(gather_kernel, name='gather', in_specs=[ANY], out_specs=AN...  126 us
    pallas_call x1, Pallas kernels, scatter_all(): pl.pallas_call(scatter_kernel, name='scatter', in_specs=[ANY], out_specs=...  100 us
    pallas_call x1, Pallas kernels, back(): pl.pallas_call(back_kernel, name='back', grid=(seqs,), in_specs=[rows, ro...  84.6 us
    pallas_call x1, Pallas kernels, feed(): pl.pallas_call(feed_kernel, name='feed', grid=(ff // chunk,), in_specs=[w...  83.1 us
    pallas_call x1, Pallas kernels, attend(): pl.pallas_call(attend_kernel, name='attend', grid=(seqs,), in_specs=[rows...  76.9 us
    unnamed x25, local copies, waits for them, and re-layouts  17 us
    reshape x2, local copies, waits for them, and re-layouts, shards(): dwin.reshape(devices, rows, ff // width, width).transpose(2, 0, 1, 3)  12.9 us

profile of v1, /device:TPU:0, one launch (start us, length us, event | category | flops | bytes accessed | tf_op | source)
XLA Modules:
  0.0 554.9 jit_solution(8171684570305832577)
XLA Ops:
  1.9 1.3 fusion.29
  3.9 1.3 fusion.30
  7.5 2.0 select_bitcast_fusion
  9.6 1.7 scatter.25
  17.8 126.2 %gather.1 = bf16[13,4,2,2,48,768]{5,4,3,2,1,0:T(8,128)(2,1)} custom-call(bf16[13,48,768]{2,1,0:T(8,128)(2,1)} %copy-done.1), custom_call_target="tpu_custom_call" | custom-call | tf_op jit(solution)/shard_map/gather/pallas_call | solution.py:710
  143.9 5.0 fusion.32
  151.1 76.9 %attend.1 = (bf16[2048,768]{1,0:T(8,128)(2,1)}, bf16[2048,768]{1,0:T(8,128)(2,1)}, bf16[2048,768]{1,0:T(8,128)(2,1)}, bf16[4,12,512,512]{3,2,1,0:T(8,128)(2,1)},...) custom-call(bf16[2048,768]{1,0:T(8,128)(2,1)} %x_ref.3, ...), custom_call_target="tpu_custom_call" | custom-call | tf_op jit(solution)/shard_map/attend/pallas_call | solution.py:167
  228.0 4.4 fusion.31
  232.4 3.6 copy.59
  236.1 3.2 copy.76
  239.3 2.6 copy.60
  241.9 83.1 %feed.1 = (bf16[2048,768]{1,0:T(8,128)(2,1)}, f32[4,2,768]{2,1,0:T(2,128)}, f32[2048,768]{1,0:T(8,128)}, bf16[768,3072]{1,0:T(8,128)(2,1)}, bf16[3072,768]{1,0:T(8,128)(2,1)}) custom-call(bf16[2048,768]{1,0:T(8,128)(2,1)} %get-tuple-element.102.n2_ref, bf16[2048,768]{1,0:T(8,128)(2,1)} %get-tuple-element.103.bg_ref, ...), custom_call_target="tpu_custom_call" | custom-call | tf_op jit(solution)/shard_map/feed/pallas_call | solution.py:250
  325.0 84.6 %back.1 = (bf16[2048,768]{1,0:T(8,128)(2,1)}, bf16[768,2304]{1,0:T(8,128)(2,1)}, bf16[768,768]{1,0:T(8,128)(2,1)}, f32[8,768]{1,0:T(8,128)}, f32[12,8,768]{2,1,0:T(8,128)}) custom-call(bf16[2048,768]{1,0:T(8,128)(2,1)} %x_ref.3, bf16[2048,768]{1,0:T(8,128)(2,1)} %og_ref.3, f32[4,2,768]{2,1,0:T(2,128)} %pg_ref.3, s32[4,1,512]{2,1,0:T(1,128)} %bitcast.112, ...), custom_call_target="tpu_custom_call" | custom-call | tf_op jit(solution)/shard_map/back/pallas_call | solution.py:414
  411.3 2.1 scatter.29
  415.8 2.0 dynamic-slice_select_fusion
  417.8 4.2 scatter.36
  423.1 2.2 fusion.33
  429.8 9.7 %reshape.372 = bf16[16,48,4,768]{3,2,1,0:T(4,128)(2,1)} reshape(bf16[768,3072]{1,0:T(8,128)(2,1)} %get-tuple-element.118) | data formatting | bytes 9437184 | tf_op jit(solution)/shard_map/reshape | solution.py:802
  439.6 3.1 copy.65
  442.7 2.5 constant_dynamic-update-slice_fusion.3
  445.6 2.5 constant_dynamic-update-slice_fusion.2.part_ref
  448.1 100.4 %scatter.37 = f32[13,48,768]{2,1,0:T(8,128)} custom-call(bf16[13,4,2,2,48,768]{5,4,3,2,1,0:T(8,128)(2,1)} %constant_dynamic-update-slice_fusion.2.part_ref), custom_call_target="tpu_custom_call" | custom-call | tf_op jit(solution)/shard_map/scatter/pallas_call | solution.py:735
  548.5 2.1 fusion.34
  551.5 2.0 slice_bitcast_fusion.1
  (55 shorter events, 25.0 us)
Async XLA Ops:
  16.8 0.9 copy-start.1
  325.0 90.0 %copy-start.2 = (s32[3]{0:T(128)S(1)}, s32[3]{0:T(128)}, u32[]{:S(2)}) copy-start(s32[3]{0:T(128)} %constant.188.clone.1) | copy-start | bytes 40
  425.4 3.3 copy-start
  439.6 5.6 %slice-start = ((s8[4718592]{0:T(1024)(128)(4,1)}), s8[4194304]{0:T(1024)(128)(4,1)S(1)}, s32[]{:S(2)}) async-start(s8[4718592]{0:T(1024)(128)(4,1)} %bitcast.100), calls=%async_computation | async-start | bytes 8388608
  442.7 2.5 slice-start.1

commit v2 on v0

v2 whole, which is shorter than its diff:
```python
from functools import partial

import jax
import jax.numpy as jnp
from jax import lax
from jax.experimental import pallas as pl
from jax.experimental.pallas import tpu as pltpu
from jax.sharding import PartitionSpec as P

HEADS = 12
HEAD_DIM = 64
BUCKETS = 32
LENGTH = 512
BLOCK = 128
BLOCKS = LENGTH // BLOCK
BAND_BLOCKS = 2 * BLOCKS - 1
BAND = BAND_BLOCKS * BLOCK
OFFSETS = BAND + BLOCK
GROUPS = 3
GROUP = HEADS // GROUPS
GROUP_ROWS = GROUP * HEAD_DIM
OWNERS, PARTS, SHARE = 16, 4, 48
TABLE_SHARE = HEADS * BUCKETS // OWNERS
SMALL = 256
EPS = 1e-06
NEG = -1e30
LIMITS = (12, 16, 23, 32, 46, 64, 91)
ROOT = 0.7978845608028654
CUBE = 0.044715
F32 = jnp.float32
BF16 = jnp.bfloat16
ANY = pl.BlockSpec(memory_space=pl.ANY)
VMEM_LIMIT = 63 * 1024 * 1024


def bucket_of(offset):
    distance = jnp.abs(offset)
    far_bucket = jnp.full(offset.shape, 8, jnp.int32)
    for threshold in LIMITS:
        far_bucket = far_bucket + (distance >= threshold).astype(jnp.int32)
    near_bucket = jnp.where(distance < 8, distance, far_bucket)
    return near_bucket + BUCKETS // 2 * (offset > 0).astype(jnp.int32)


def dot(a, b):
    return lax.dot_general(a, b, (((1,), (0,)), ((), ())), preferred_element_type=F32)


def dot_nt(a, b):
    return lax.dot_general(a, b, (((1,), (1,)), ((), ())), preferred_element_type=F32)


def dot_tn(a, b):
    return lax.dot_general(a, b, (((0,), (0,)), ((), ())), preferred_element_type=F32)


def dot_tt(a, b):
    return lax.dot_general(a, b, (((0,), (1,)), ((), ())), preferred_element_type=F32)


def iota(shape, axis):
    return lax.broadcasted_iota(jnp.int32, shape, axis)


def whole(shape):
    zeros = (0,) * len(shape)
    return pl.BlockSpec(shape, lambda *_: zeros, pipeline_mode=pl.Buffered(1))


def span(first, last):
    return slice(first * BLOCK, last * BLOCK)


def pool_terms(flags, instruction):
    kept = (instruction == 0).astype(F32)
    chosen = [kept * (flags == part).astype(F32) for part in range(2)]
    counts = [jnp.sum(one, axis=1, keepdims=True) for one in chosen]
    return chosen, counts


def pool_gradient(chosen, counts, pooled_grad):
    row = iota((16, LENGTH), 0)
    picks = jnp.where(row % 2 == 0, chosen[0], chosen[1])
    picks = jnp.where(row < 6, picks, 0.0).astype(BF16)
    scaled = [pooled_grad[part : part + 1, :] / counts[part] for part in range(2)]
    line = iota((16, pooled_grad.shape[1]), 0)
    both = jnp.where(line % 2 == 0, scaled[0], scaled[1])
    high = both.astype(BF16).astype(F32)
    rest = both - high
    middle = rest.astype(BF16).astype(F32)
    low = rest - middle
    parts = jnp.where(line < 2, high, jnp.where(line < 4, middle, jnp.where(line < 6, low, 0.0)))
    return dot_tn(picks, parts.astype(BF16))


def norm_back(value, gain, cotangent):
    scale = lax.rsqrt(jnp.mean(value * value, axis=1, keepdims=True) + EPS)
    scaled = cotangent * gain
    unit = value * scale
    inner = jnp.mean(scaled * unit, axis=1, keepdims=True)
    return scale * (scaled - unit * inner), jnp.sum(cotangent * unit, axis=0, keepdims=True)


def table_places():
    at = iota((1, OWNERS * SHARE), 1)
    owner = sum((at >= SHARE * one).astype(jnp.int32) for one in range(1, OWNERS))
    inside = at - SHARE * owner
    entry = owner * TABLE_SHARE + inside
    bucket = sum((entry >= HEADS * one).astype(jnp.int32) for one in range(1, BUCKETS))
    return entry - HEADS * bucket, jnp.where(inside < TABLE_SHARE, bucket, -1)


DEPTH, WIDE, CORES = 4, 2, 2
MESH_ID = pl.DeviceIdType.MESH


def place():
    grp, at = lax.axis_index("grp"), lax.axis_index("fsdp")
    z, x, core = lax.div(at, WIDE * CORES), lax.rem(lax.div(at, CORES), WIDE), lax.rem(at, CORES)

    def device(grp, z, x, core):
        return (grp, z * (WIDE * CORES) + x * CORES + core)

    return dict(
        z=z, x=x, core=core,
        over_y=device(1 - grp, z, x, core),
        over_x=device(grp, z, 1 - x, core),
        over_core=device(grp, z, x, 1 - core),
        over_z=[device(grp, lax.rem(z + one, DEPTH), x, core) for one in range(1, DEPTH)],
        ahead=[lax.rem(z + one, DEPTH) for one in range(1, DEPTH)],
        behind=[lax.rem(z + DEPTH - one, DEPTH) for one in range(1, DEPTH)],
    )


def greet(here):
    barrier = pltpu.get_barrier_semaphore()
    for device in (here["over_y"], here["over_x"], here["over_core"], *here["over_z"]):
        pl.semaphore_signal(barrier, inc=1, device_id=device, device_id_type=MESH_ID)
    pl.semaphore_wait(barrier, DEPTH + 2)


def gather_phase(phase, sem, here, share_ref, whole_ref, sent, got, own_sem):
    z, x, core = here["z"], here["x"], here["core"]

    def copy(source, where, channel, device):
        return pltpu.make_async_remote_copy(
            src_ref=source, dst_ref=whole_ref.at[where], send_sem=sent.at[channel, sem], recv_sem=got.at[channel, sem],
            device_id=device, device_id_type=MESH_ID,
        )

    own = lambda: pltpu.make_async_copy(share_ref, whole_ref.at[z, x, core], own_sem.at[sem])
    every = slice(None)
    line_out = lambda one: copy(share_ref, (z, x, core), one, here["over_z"][one])
    line_in = lambda one: copy(share_ref, (here["behind"][one], x, core), one, here["over_z"][one])
    side_out = lambda: copy(whole_ref.at[every, x, core], (every, x, core), 3, here["over_x"])
    side_in = lambda: copy(whole_ref.at[every, x, core], (every, 1 - x, core), 3, here["over_x"])
    core_out = lambda: copy(whole_ref.at[every, every, core], (every, every, core), 4, here["over_core"])
    core_in = lambda: copy(whole_ref.at[every, every, core], (every, every, 1 - core), 4, here["over_core"])
    if phase == 0:
        own().start()
        for one in range(DEPTH - 1):
            line_out(one).start()
    elif phase == 1:
        own().wait()
        for one in range(DEPTH - 1):
            line_in(one).wait_recv()
        side_out().start()
    elif phase == 2:
        side_in().wait_recv()
        core_out().start()
    else:
        for one in range(DEPTH - 1):
            line_out(one).wait_send()
        side_out().wait_send()
        core_out().wait_send()
        core_in().wait_recv()


def scatter_phase(phase, piece, here, part_ref, out_ref, own, fromc, fromx, fromz, last, sent, got, own_sem):
    z, x, core = here["z"], here["x"], here["core"]
    slot = lax.rem(piece, 2)

    def remote(source, target, channel, device):
        return pltpu.make_async_remote_copy(
            src_ref=source, dst_ref=target, send_sem=sent.at[channel, piece], recv_sem=got.at[channel, piece],
            device_id=device, device_id_type=MESH_ID,
        )

    total = fromc.at[piece]
    over_core = lambda: remote(part_ref.at[:, :, 1 - core], total, 0, here["over_core"])
    load = lambda: pltpu.make_async_copy(part_ref.at[:, :, core], own.at[slot], own_sem.at[slot])
    over_x = lambda: remote(fromc.at[piece, :, 1 - x], fromx.at[piece], 1, here["over_x"])
    line_out = lambda one: remote(fromc.at[piece, here["ahead"][one], x], fromz.at[piece, z], 2 + one, here["over_z"][one])
    line_in = lambda one: remote(
        fromc.at[piece, z, x], fromz.at[piece, here["behind"][one]], 2 + one, here["over_z"][one]
    )
    final = lambda: remote(fromc.at[piece, z, x], last.at[piece], 5, here["over_y"])

    if phase == 0:
        over_core().start()
        load().start()
    elif phase == 1:
        load().wait()
        over_core().wait()

        def one(at, _):
            for side in range(WIDE):
                mine = own[slot, at, side].astype(F32) + fromc[piece, at, side].astype(F32)
                fromc[piece, at, side] = mine.astype(BF16)
            return 0

        lax.fori_loop(0, DEPTH, one, 0)
        over_x().start()
    elif phase == 2:
        over_x().wait()

        def one(at, _):
            mine = fromc[piece, at, x].astype(F32) + fromx[piece, at].astype(F32)
            fromc[piece, at, x] = mine.astype(BF16)
            return 0

        lax.fori_loop(0, DEPTH, one, 0)
        for one in range(DEPTH - 1):
            line_out(one).start()
    elif phase == 3:
        mine = fromc[piece, z, x].astype(F32)
        for one in range(DEPTH - 1):
            line_in(one).wait_recv()
            mine = mine + fromz[piece, here["behind"][one]].astype(F32)
        fromc[piece, z, x] = mine.astype(BF16)
        final().start()
    else:
        for one in range(DEPTH - 1):
            line_out(one).wait_send()
        final().wait()
        out_ref[piece] = fromc[piece, z, x].astype(F32) + last[piece].astype(F32)


def run_slot(slot, table, act):
    for phase in reversed(range(max(map(len, table.values())))):
        due, found = False, 0
        for piece, slots in table.items():
            if slots[phase] is not None:
                now = slot == slots[phase]
                due, found = due | now, jnp.where(now, piece, found)
        if due is not False:

            @pl.when(due)
            def _(phase=phase, found=found):
                act(phase, found)


def run_rest(first, tables, travel):
    end = 1 + max(slot for table in tables for slots in table.values() for slot in slots if slot is not None)

    def one(slot, _):
        travel(slot)
        return 0

    if end > first:
        lax.fori_loop(first, end, one, 0)


def gather_sems(pieces):
    return [pltpu.SemaphoreType.DMA((5, pieces)), pltpu.SemaphoreType.DMA((5, pieces)), pltpu.SemaphoreType.DMA((pieces,))]


def scatter_scratch(pieces, rows, columns):
    return [
        pltpu.VMEM((2, DEPTH, WIDE, rows, columns), BF16),
        pltpu.VMEM((pieces, DEPTH, WIDE, rows, columns), BF16),
        pltpu.VMEM((pieces, DEPTH, rows, columns), BF16),
        pltpu.VMEM((pieces, DEPTH, rows, columns), BF16),
        pltpu.VMEM((pieces, rows, columns), BF16),
        pltpu.SemaphoreType.DMA((6, pieces)),
        pltpu.SemaphoreType.DMA((6, pieces)),
        pltpu.SemaphoreType.DMA((2,)),
    ]


ATTEND_PIECES, FEED_PIECES = 8, 4
ATTEND_TABLE = {
    1: (None, 0, 3, 5),
    2: (0, 4, 8, 10),
    3: (3, 8, 12, 14),
    4: (6, 11, 15, 17),
    5: (9, 14, 18, 20),
    6: (12, 17, 21, 23),
    7: (15, 20, 24, 25),
}
FEED_GATHER = {0: (0, 5, 10, 12), 1: (3, 8, 13, 15), 2: (6, 11, 16, 18), 3: (9, 14, 19, 21)}
FEED_SUMS = 5
FEED_SCATTER = {
    0: (8, 10, 15, 20, 23), 1: (11, 13, 18, 23, 26), 2: (16, 18, 23, 28, 31), 3: (19, 21, 26, 31, 34), 4: (24, 26, 31, 36, 39),
}
BACK_BEFORE, BACK_SUMS = 4, 6
BACK_SCATTER = {
    0: (0, 2, 7, 12, 15), 1: (3, 5, 10, 15, 18), 2: (6, 8, 13, 18, 21), 3: (9, 11, 16, 21, 24),
    4: (12, 14, 19, 24, 27), 5: (16, 18, 23, 27, 29),
}
TAIL_SUMS = 4
TAIL_SCATTER = {0: (24, 25, 26, 27, 28), 1: (25, 26, 27, 28, 29), 2: (26, 27, 28, 29, 30), 3: (27, 28, 29, 30, 31)}


def attend_kernel(
    x_ref, og_ref, pg_ref, flags_ref, instr_ref, shares_hbm, small_hbm,
    qkv_ref, p_ref, inv_ref, mix_ref, mid_ref, n2_ref, bg_ref, gains_ref, weights_hbm, smalls_hbm,
    band_ref, aux_ref, normed_ref, wg_ref, wo_ref, small_ref, table_ref, cur_ref, nxt_ref, sa_ref, sb_ref, sems,
    *comm, fast,
):
    group, seq = pl.program_id(0), pl.program_id(1)
    seqs = pl.num_programs(1)
    step = group * seqs + seq
    width = x_ref.shape[1]
    if fast:
        main_sems, first_sems, small_sems = comm[0:3], comm[3:6], comm[6:9]
        here = place()

        def main(phase, piece):
            gather_phase(phase, piece, here, shares_hbm.at[piece], weights_hbm.at[piece], *main_sems)

        def small(phase):
            gather_phase(phase, 0, here, small_hbm.at[0], smalls_hbm.at[0], *small_sems)

        def first(phase, which):
            lanes = pl.ds(which * GROUP_ROWS, GROUP_ROWS)
            every = slice(None)
            gather_phase(
                phase, which, here, shares_hbm.at[0, :, lanes], weights_hbm.at[0, every, every, every, every, lanes], *first_sems
            )

        def travel(slot):
            run_slot(slot, ATTEND_TABLE, main)

        point = lambda at: travel(2 * step + at)
    else:
        point = lambda at: None
    load_small = lambda: pltpu.make_async_copy(smalls_hbm.at[0], small_ref, sems.at[0])
    load_group = lambda at: pltpu.make_async_copy(weights_hbm.at[at], wg_ref, sems.at[1])
    load_output = lambda: pltpu.make_async_copy(weights_hbm.at[GROUPS], wo_ref, sems.at[2])
    square = lambda ref: ref[...].reshape(width, width)

    def prepare(at):
        flags = flags_ref[at]
        chosen, counts = pool_terms(flags, instr_ref[at])
        rows = pl.ds(pl.multiple_of(at * LENGTH, LENGTH), LENGTH)
        grad_result = og_ref[rows, :].astype(F32) + pool_gradient(chosen, counts, pg_ref[at])
        bg_ref[rows, :] = grad_result.astype(BF16)
        row = iota((16, LENGTH), 0)
        aux_ref[0, at] = jnp.where(row == 0, 1 - flags, jnp.where(row == 1, flags, 0)).astype(F32).astype(BF16)
        other = jnp.where(row == 0, flags, jnp.where(row == 1, 1 - flags, 0)).astype(F32) * NEG
        aux_ref[1, at] = other.astype(BF16)
        hidden = x_ref[rows, :].astype(F32)
        scale = lax.rsqrt(jnp.mean(hidden * hidden, axis=1, keepdims=True) + EPS)
        normed_ref[at] = (hidden * scale * gains_ref[0:1, :]).astype(BF16)

    def project(at, target):
        target[...] = dot_tt(square(wg_ref), normed_ref[at]).astype(BF16)

    def part(source, which, head):
        first = which * GROUP_ROWS + head * HEAD_DIM
        return source[first : first + HEAD_DIM, :]

    def score(source, at_group, at, head, target):
        queries = jnp.concatenate([part(source, 0, head), aux_ref[0, at]], axis=0)
        keys = jnp.concatenate([part(source, 1, head), aux_ref[1, at]], axis=0)
        scores = dot_tn(keys, queries)
        for row in range(BLOCKS):
            for column in range(BLOCKS):
                bias = band_ref[at_group * GROUP + head, span(row - column + BLOCKS - 1, row - column + BLOCKS), :]
                target[span(row, row + 1), span(column, column + 1)] = scores[span(row, row + 1), span(column, column + 1)] + bias

    def soften(head, source):
        scores = source[...]
        exponent = jnp.exp(scores - jnp.max(scores, axis=0, keepdims=True)).astype(BF16)
        p_ref[0, 0, head] = exponent
        values = jnp.concatenate([part(cur_ref, 2, head), jnp.ones((16, LENGTH), BF16)], axis=0)
        mixed = dot(values, exponent)
        inverse = 1.0 / mixed[HEAD_DIM : HEAD_DIM + 1, :]
        inv_ref[0, 0, head] = inverse
        mix_ref[group, seq, head * HEAD_DIM : (head + 1) * HEAD_DIM, :] = (mixed[0:HEAD_DIM, :] * inverse).astype(BF16)

    def read_small():
        load_small().start()
        load_small().wait()
        flipped = small_ref[...].reshape(width, SMALL)[:, 0:BLOCK].astype(F32).T
        gains_ref[...] = flipped[0:8, :]
        heads, buckets = table_places()
        entries = jnp.where((iota((16, width), 0) == heads) & (buckets >= 0), flipped[2:3, :], 0.0).astype(BF16)
        onehot = (bucket_of(iota((OFFSETS, 1), 0) - BLOCKS * BLOCK) == buckets).astype(F32).astype(BF16)
        table_ref[...] = dot_nt(entries, onehot)

    def make_bands():
        def one_head(head, _):
            table = table_ref[...]
            line = jnp.sum(jnp.where(iota(table.shape, 0) == head, table, 0.0), axis=0, keepdims=True)
            turned = pltpu.roll(jnp.broadcast_to(line, (BLOCK, OFFSETS)), 0, 1, stride=1, stride_axis=0)
            band_ref[head] = turned[:, BLOCK:].T
            return 0

        lax.fori_loop(0, HEADS, one_head, 0)

    def prepare_all():
        def one_seq(at, _):
            prepare(at)
            return 0

        lax.fori_loop(0, seqs, one_seq, 0)

    @pl.when(step == 0)
    def _():
        if fast:
            greet(here)
            small(0)
            for which in range(3):
                first(0, which)
            small(1)
            first(1, 0)
            small(2)
            first(1, 1)
            small(3)
            read_small()
            first(1, 2)
            main(0, 1)
            first(2, 0)
            prepare_all()
            first(2, 1)
            make_bands()
            first(2, 2)
            for which in range(3):
                first(3, which)
        else:
            read_small()
            prepare_all()
            make_bands()
        load_group(0).start()
        load_group(0).wait()
        project(0, nxt_ref)
        score(nxt_ref, 0, 0, 0, sa_ref)

    last_seq = seq == seqs - 1
    more = step + 1 < GROUPS * seqs
    cur_ref[...] = nxt_ref[...]
    qkv_ref[0, 0] = nxt_ref[...]

    @pl.when(last_seq & more)
    def _():
        load_group(group + 1).start()

    @pl.when((seq == 0) & (group == GROUPS - 1))
    def _():
        load_output().start()
        load_output().wait()

    next_seq = jnp.where(last_seq, 0, seq + 1)
    next_group = jnp.where(last_seq, jnp.minimum(group + 1, GROUPS - 1), group)
    point(0)
    score(cur_ref, group, seq, 1, sb_ref)
    soften(0, sa_ref)
    score(cur_ref, group, seq, 2, sa_ref)
    soften(1, sb_ref)
    point(1)
    score(cur_ref, group, seq, 3, sb_ref)
    soften(2, sa_ref)

    @pl.when(last_seq & more)
    def _():
        load_group(group + 1).wait()

    project(next_seq, nxt_ref)
    score(nxt_ref, next_group, next_seq, 0, sa_ref)
    soften(3, sb_ref)

    @pl.when(group == GROUPS - 1)
    def _():
        rows = pl.ds(pl.multiple_of(seq * LENGTH, LENGTH), LENGTH)
        middle = x_ref[rows, :].astype(F32)
        output = square(wo_ref)
        for one in range(GROUPS):
            middle = middle + dot_tn(mix_ref[one, seq], output[one * GROUP_ROWS : (one + 1) * GROUP_ROWS, :])
        mid_ref[...] = middle
        scale = lax.rsqrt(jnp.mean(middle * middle, axis=1, keepdims=True) + EPS)
        n2_ref[...] = (middle * scale * gains_ref[1:2, :]).astype(BF16)

    if fast:

        @pl.when(step == GROUPS * seqs - 1)
        def _():
            run_rest(2 * GROUPS * (x_ref.shape[0] // LENGTH), [ATTEND_TABLE], travel)


def attend(x, og, pg, flags, instr, shares, small, fast):
    tokens, width = x.shape
    seqs = tokens // LENGTH
    last_rows = pl.BlockSpec((LENGTH, width), lambda g, s: (jnp.where(g == GROUPS - 1, s, 0), 0))
    low = jax.ShapeDtypeStruct((tokens, width), BF16)
    out_specs = [
        pl.BlockSpec((1, 1, width, LENGTH), lambda g, s: (g, s, 0, 0)),
        pl.BlockSpec((1, 1, GROUP, LENGTH, LENGTH), lambda g, s: (g, s, 0, 0, 0)),
        pl.BlockSpec((1, 1, GROUP, 1, LENGTH), lambda g, s: (g, s, 0, 0, 0)),
        whole((GROUPS, seqs, GROUP_ROWS, LENGTH)), last_rows, last_rows, whole((tokens, width)), whole((8, width)),
    ]
    out_shape = [
        jax.ShapeDtypeStruct((GROUPS, seqs, width, LENGTH), BF16),
        jax.ShapeDtypeStruct((GROUPS, seqs, GROUP, LENGTH, LENGTH), BF16),
        jax.ShapeDtypeStruct((GROUPS, seqs, GROUP, 1, LENGTH), F32),
        jax.ShapeDtypeStruct((GROUPS, seqs, GROUP_ROWS, LENGTH), BF16),
        jax.ShapeDtypeStruct((tokens, width), F32), low, low, jax.ShapeDtypeStruct((8, width), F32),
    ]
    scratch = [
        pltpu.VMEM((HEADS, BAND, BLOCK), F32), pltpu.VMEM((2, seqs, 16, LENGTH), BF16),
        pltpu.VMEM((seqs, LENGTH, width), BF16), pltpu.VMEM((DEPTH, WIDE, CORES, SHARE, width), BF16),
        pltpu.VMEM((DEPTH, WIDE, CORES, SHARE, width), BF16), pltpu.VMEM((DEPTH, WIDE, CORES, SHARE, SMALL), BF16), pltpu.VMEM((16, OFFSETS), F32),
        pltpu.VMEM((width, LENGTH), BF16), pltpu.VMEM((width, LENGTH), BF16),
        pltpu.VMEM((LENGTH, LENGTH), F32), pltpu.VMEM((LENGTH, LENGTH), F32), pltpu.SemaphoreType.DMA((3,)),
    ]
    in_specs = [
        whole((tokens, width)), whole((tokens, width)), whole((seqs, 2, width)), whole((seqs, 1, LENGTH)),
        whole((seqs, 1, LENGTH)), ANY, ANY,
    ]
    if fast:
        kernel = partial(attend_kernel, fast=True)
        out_specs += [ANY, ANY]
        out_shape += [
            jax.ShapeDtypeStruct((ATTEND_PIECES, DEPTH, WIDE, CORES, SHARE, width), BF16),
            jax.ShapeDtypeStruct((1, DEPTH, WIDE, CORES, SHARE, SMALL), BF16),
        ]
        scratch += gather_sems(ATTEND_PIECES) + gather_sems(3) + gather_sems(1)
    else:

        def kernel(*refs):
            inputs, outputs, rest = refs[:7], refs[7:15], refs[15:]
            attend_kernel(*inputs, *outputs, inputs[5], inputs[6], *rest, fast=False)

    return pl.pallas_call(
        kernel,
        name="attend",
        grid=(GROUPS, seqs),
        in_specs=in_specs,
        out_specs=out_specs,
        out_shape=out_shape,
        scratch_shapes=scratch,
        compiler_params=pltpu.CompilerParams(
            vmem_limit_bytes=VMEM_LIMIT, collective_id=1 if fast else None, has_side_effects=fast
        ),
    )(x, og, pg, flags, instr, shares, small)


def feed_kernel(
    n2_ref, bg_ref, mid_hbm, flags_ref, instr_ref, pg_ref, gains_ref, og_ref, mid_ref, mix_ref, early_hbm, late_hbm,
    out_ref, pooled_ref, gm_ref, dmix_ref, parts_hbm, *rest, fast,
):
    if fast:
        sums_ref, gathered_hbm = rest[0:2]
        rest = rest[2:]
    res_ref, dn2_ref, act_ref, dinner_ref, win_ref, wout_ref, wo_ref, dwo_ref, staged_ref, sems = rest[:10]
    part, block = pl.program_id(0), pl.program_id(1)
    blocks = pl.num_programs(1)
    step = part * blocks + block
    width = n2_ref.shape[1]
    rows = pl.ds(pl.multiple_of(block * LENGTH, LENGTH), LENGTH)
    if fast:
        sems_of, scratch = rest[10:13], rest[13:]
        here = place()

        def travel(slot):
            def bring(phase, piece):
                share = late_hbm.at[ATTEND_PIECES + piece]
                gather_phase(phase, piece, here, share, gathered_hbm.at[piece], *sems_of)

            def add(phase, piece):
                scatter_phase(phase, piece, here, parts_hbm.at[piece], sums_ref, *scratch)

            run_slot(slot, FEED_GATHER, bring)
            run_slot(slot, FEED_SCATTER, add)

        point = lambda at: travel(2 * step + at)
    else:
        point = lambda at: None
    square = lambda ref: ref[...].reshape(width, width)

    def weights(at, start):
        def both(source, first):
            for which, target in enumerate((win_ref, wout_ref)):
                slot = lax.rem(at, 2)
                copy = pltpu.make_async_copy(source.at[first + which], target.at[slot], sems.at[slot, which])
                copy.start() if start else copy.wait()

        if start:
            pl.when(at < PARTS // 2)(lambda: both(early_hbm, 4 + 2 * at))
            pl.when(at >= PARTS // 2)(lambda: both(gathered_hbm if fast else late_hbm, 2 * at + (-PARTS if fast else 4)))
        else:
            both(early_hbm, 4)

    load_middle = lambda: pltpu.make_async_copy(mid_hbm, res_ref, sems.at[0, 2])
    load_output = lambda: pltpu.make_async_copy(early_hbm.at[GROUPS], wo_ref, sems.at[1, 2])
    keep = lambda at, which: pltpu.make_async_copy(staged_ref.at[which], parts_hbm.at[2 * at + which], sems.at[which, 3])

    @pl.when(step == 0)
    def _():
        load_middle().start()
        load_output().start()
        weights(0, True)
        if fast:
            greet(here)
        dn2_ref[...] = jnp.zeros_like(dn2_ref)
        dwo_ref[...] = jnp.zeros_like(dwo_ref)
        load_middle().wait()
        load_output().wait()

    @pl.when((part < PARTS) & (block == 0))
    def _():
        weights(part, False)

    @pl.when((part > 0) & (block == 0))
    def _():
        keep(part - 1, 0).wait()
        keep(part - 1, 1).wait()

    point(0)

    @pl.when(part < PARTS)
    def _():
        slot = lax.rem(part, 2)
        inner = dot(n2_ref[rows, :], square(win_ref.at[slot]))
        squared = inner * inner
        half = 0.5 * jnp.tanh(inner * (ROOT + (ROOT * CUBE) * squared)) + 0.5
        active = inner * half
        slope = half + active * (1.0 - half) * (2.0 * ROOT + (6.0 * ROOT * CUBE) * squared)
        active = active.astype(BF16)
        act_ref[rows, :] = active
        dinner = (dot_nt(bg_ref[rows, :], square(wout_ref.at[slot])) * slope).astype(BF16)
        dinner_ref[rows, :] = dinner
        res_ref[rows, :] += dot(active, square(wout_ref.at[slot]))
        dn2_ref[rows, :] += dot_nt(dinner, square(win_ref.at[slot]))

    point(1)

    @pl.when((part < PARTS - 1) & (block == blocks - 1))
    def _():
        weights(part + 1, True)

    def stage(which, first, value):
        for owner in range(OWNERS):
            z, x, core = owner // 4, owner // 2 % 2, owner % 2
            staged_ref[which, z, x, core, :, first : first + 256] = value[SHARE * owner : SHARE * (owner + 1), :]

    @pl.when((part < PARTS) & (block == blocks - 1))
    def _():
        for first in range(0, width, 256):
            stage(0, first, dot_tn(n2_ref[...], dinner_ref[:, first : first + 256]).astype(BF16))
        keep(part, 0).start()
        for first in range(0, width, 256):
            stage(1, first, dot_tn(act_ref[...], bg_ref[:, first : first + 256]).astype(BF16))
        keep(part, 1).start()

    @pl.when(part == PARTS)
    def _():
        result = res_ref[rows, :]
        out_ref[...] = result.astype(BF16)
        chosen, counts = pool_terms(flags_ref[block], instr_ref[block])
        line = iota((8, LENGTH), 0)
        picks = jnp.where(line == 0, chosen[0], jnp.where(line == 1, chosen[1], 0.0)).astype(BF16)
        high = result.astype(BF16)
        low = (result - high.astype(F32)).astype(BF16)
        total = dot(picks, high) + dot(picks, low)
        total = total / jnp.where(iota((8, 1), 0) == 0, counts[0], counts[1])
        pooled_ref[block] = total[0:2, :]
        grad_result = og_ref[...].astype(F32) + pool_gradient(chosen, counts, pg_ref[block])
        change, _ = norm_back(mid_ref[...], gains_ref[1:2, :], dn2_ref[rows, :])
        grad_middle = grad_result + change
        gm_ref[...] = grad_middle
        out_low = grad_middle.astype(BF16)
        output = square(wo_ref)
        for group in range(GROUPS):
            mine = slice(group * GROUP_ROWS, (group + 1) * GROUP_ROWS)
            dmix_ref[group, 0] = dot_nt(output[mine, :], out_low).astype(BF16)
            dwo_ref[mine, :] += dot(mix_ref[group, 0], out_low)

    @pl.when(step == (PARTS + 1) * blocks - 1)
    def _():
        for first in range(0, width, 256):
            stage(0, first, dwo_ref[:, first : first + 256].astype(BF16))
        keep(PARTS, 0).start()
        keep(PARTS, 0).wait()


def feed(n2, bg, mid, flags, instr, pg, gains, og, mix, early, late, fast):
    tokens, width = n2.shape
    seqs = tokens // LENGTH
    rows = pl.BlockSpec((LENGTH, width), lambda c, m: (jnp.where(c == PARTS, m, 0), 0))
    heads = pl.BlockSpec((GROUPS, 1, GROUP_ROWS, LENGTH), lambda c, m: (0, jnp.where(c == PARTS, m, 0), 0, 0))
    piece = (DEPTH, WIDE, CORES, SHARE, width)
    sums = FEED_SUMS
    out_specs = [rows, whole((seqs, 2, width)), rows, heads, ANY]
    out_shape = [
        jax.ShapeDtypeStruct((tokens, width), BF16), jax.ShapeDtypeStruct((seqs, 2, width), F32),
        jax.ShapeDtypeStruct((tokens, width), F32), jax.ShapeDtypeStruct((GROUPS, seqs, GROUP_ROWS, LENGTH), BF16),
        jax.ShapeDtypeStruct((2 * PARTS + 1, *piece), BF16),
    ]
    scratch = [
        pltpu.VMEM((tokens, width), F32), pltpu.VMEM((tokens, width), F32), pltpu.VMEM((tokens, width), BF16),
        pltpu.VMEM((tokens, width), BF16), pltpu.VMEM((2, *piece), BF16), pltpu.VMEM((2, *piece), BF16),
        pltpu.VMEM(piece, BF16), pltpu.VMEM((width, width), F32), pltpu.VMEM((2, *piece), BF16), pltpu.SemaphoreType.DMA((2, 4)),
    ]
    if fast:
        out_specs += [whole((sums, SHARE, width)), ANY]
        out_shape += [
            jax.ShapeDtypeStruct((sums, SHARE, width), F32), jax.ShapeDtypeStruct((FEED_PIECES, *piece), BF16)
        ]
        scratch += gather_sems(FEED_PIECES) + scatter_scratch(sums, SHARE, width)
    return pl.pallas_call(
        partial(feed_kernel, fast=fast),
        name="feed",
        grid=(PARTS + 1, seqs),
        in_specs=[
            whole((tokens, width)), whole((tokens, width)), ANY, whole((seqs, 1, LENGTH)), whole((seqs, 1, LENGTH)),
            whole((seqs, 2, width)), whole((8, width)), rows, rows, heads, ANY, ANY,
        ],
        out_specs=out_specs,
        out_shape=out_shape,
        scratch_shapes=scratch,
        compiler_params=pltpu.CompilerParams(
            vmem_limit_bytes=VMEM_LIMIT, collective_id=2 if fast else None, has_side_effects=fast
        ),
    )(n2, bg, mid, flags, instr, pg, gains, og, mid, mix, early, late)


def back_kernel(
    x_ref, gm_ref, gains_ref, wg_ref, qkv_ref, p_ref, inv_ref, mix_ref, dmix_ref, early_hbm,
    ig_ref, parts_hbm, small_ref, *rest, fast,
):
    if fast:
        sums_ref, tail_ref = rest[0:2]
        rest = rest[2:]
    band_ref, flipped_ref, grads_ref, normal_ref, diag_ref, staged_ref, ds_ref, sem = rest[:8]
    group, seq = pl.program_id(0), pl.program_id(1)
    seqs = pl.num_programs(1)
    step = group * seqs + seq
    width = x_ref.shape[1]
    if fast:
        extra = len(scatter_scratch(1, SHARE, width))
        scratch, tail_scratch = rest[8 : 8 + extra], rest[8 + extra :]
        here = place()

        def main(phase, piece):
            if phase > 0:
                scatter_phase(phase, piece, here, early_hbm.at[0], sums_ref, *scratch)
                return

            @pl.when(piece < BACK_BEFORE)
            def _():
                scatter_phase(phase, piece, here, early_hbm.at[FEED_SUMS + piece], sums_ref, *scratch)

            @pl.when(piece >= BACK_BEFORE)
            def _():
                scatter_phase(phase, piece, here, parts_hbm.at[piece - BACK_BEFORE], sums_ref, *scratch)

        def tail(phase, piece):
            if phase > 0:
                scatter_phase(phase, piece, here, small_ref, tail_ref, *tail_scratch)
                return
            for which in range(3):

                @pl.when(piece == which)
                def _(which=which):
                    lanes = slice(which * SMALL, (which + 1) * SMALL)
                    scatter_phase(phase, which, here, staged_ref.at[:, :, :, :, lanes], tail_ref, *tail_scratch)

            @pl.when(piece == 3)
            def _():
                scatter_phase(phase, 3, here, small_ref, tail_ref, *tail_scratch)

        def travel(slot):
            run_slot(slot, BACK_SCATTER, main)
            run_slot(slot, TAIL_SCATTER, tail)

        def point(at):
            ends = 2 * GROUPS * seqs
            travel(jnp.where(group < GROUPS, 2 * step + at, ends + seq + at * 10000))
    else:
        point = lambda at: None
    keep = lambda: pltpu.make_async_copy(staged_ref, parts_hbm.at[group], sem)
    lanes = pl.ds(pl.multiple_of(seq * LENGTH, LENGTH), LENGTH)

    def hidden_terms():
        hidden = x_ref[...].astype(F32)
        scale = lax.rsqrt(jnp.mean(hidden * hidden, axis=1, keepdims=True) + EPS)
        return hidden, scale

    if fast:

        @pl.when(step == 0)
        def _():
            greet(here)

    @pl.when(group == 0)
    def _():
        hidden, scale = hidden_terms()
        flipped_ref[:, lanes] = (hidden * scale * gains_ref[0:1, :]).astype(BF16).T
        normal_ref[seq] = jnp.zeros((width, LENGTH), F32)

    @pl.when((seq == 0) & (group < GROUPS))
    def _():
        band_ref[...] = jnp.zeros_like(band_ref)

    def one_head(head):
        at = head * HEAD_DIM
        rows = lambda which: qkv_ref[0, 0, which * GROUP_ROWS + at : which * GROUP_ROWS + at + HEAD_DIM, :]
        grads = dmix_ref[0, 0, at : at + HEAD_DIM, :].astype(F32) * inv_ref[0, 0, head]
        grads = grads.astype(BF16)
        delta = jnp.sum(grads.astype(F32) * mix_ref[0, 0, at : at + HEAD_DIM, :].astype(F32), axis=0, keepdims=True)
        grad_prob = dot_tn(rows(2), grads)
        for column in range(BLOCKS):
            mine = span(column, column + 1)
            for row in range(BLOCKS):
                seen = span(row, row + 1)
                value = p_ref[0, 0, head, seen, mine].astype(F32) * (grad_prob[seen, mine] - delta[:, mine])
                band_ref[head, span(row - column + BLOCKS - 1, row - column + BLOCKS), :] += value
                ds_ref[head % 2, seen, mine] = value.astype(BF16)
        scores = ds_ref[head % 2]
        grads_ref[at : at + HEAD_DIM, lanes] = dot(rows(1), scores).astype(BF16)
        grads_ref[GROUP_ROWS + at : GROUP_ROWS + at + HEAD_DIM, lanes] = dot_nt(rows(0), scores).astype(BF16)
        grads_ref[2 * GROUP_ROWS + at : 2 * GROUP_ROWS + at + HEAD_DIM, lanes] = dot_nt(grads, p_ref[0, 0, head]).astype(BF16)

    point(0)

    @pl.when(group < GROUPS)
    def _():
        one_head(0)
        one_head(1)

    point(1)

    @pl.when(group < GROUPS)
    def _():
        one_head(2)
        one_head(3)
        normal_ref[seq] += dot(wg_ref[...].reshape(width, width), grads_ref[:, lanes])

    @pl.when((seq == seqs - 1) & (group < GROUPS))
    def _():
        for first in range(0, width, 256):
            value = dot_nt(flipped_ref[...], grads_ref[first : first + 256, :]).astype(BF16)
            for owner in range(OWNERS):
                z, x, core = owner // 4, owner // 2 % 2, owner % 2
                staged_ref[z, x, core, :, first : first + 256] = value[SHARE * owner : SHARE * (owner + 1), :]
        keep().start()
        for head in range(GROUP):
            turned = band_ref[head].T
            total = jnp.zeros((8, OFFSETS), F32)
            for some in range(BLOCK // 8):
                wide = jnp.concatenate([turned[8 * some : 8 * some + 8, :], jnp.zeros((8, BLOCK), F32)], axis=1)
                total = total + pltpu.roll(wide, BLOCK - 8 * some, 1)
            line = iota((8, OFFSETS), 0)
            moved = total
            for row in range(1, 8):
                moved = jnp.where(line == row, pltpu.roll(total, OFFSETS - row, 1), moved)
            diag_ref[pl.ds(group * GROUP + head, 1)] = jnp.sum(moved, axis=0, keepdims=True)[None]
        keep().wait()

    @pl.when((seq == seqs - 1) & (group == GROUPS - 1))
    def _():
        heads, buckets = table_places()
        onehot = (bucket_of(iota((OFFSETS, 1), 0) - BLOCKS * BLOCK) == buckets).astype(F32).astype(BF16)
        row = iota((16, width), 0)
        sums = jnp.concatenate([diag_ref[head] for head in range(HEADS)] + [jnp.zeros((16 - HEADS, OFFSETS), F32)], axis=0)
        high = sums.astype(BF16)
        low = (sums - high.astype(F32)).astype(BF16)
        entries = dot(high, onehot) + dot(low, onehot)
        entries = jnp.sum(jnp.where((row == heads) & (buckets >= 0), entries, 0.0), axis=0, keepdims=True)
        column = jnp.broadcast_to(entries, (BLOCK, width)).T.astype(BF16)
        for owner in range(OWNERS):
            z, x, core = owner // 4, owner // 2 % 2, owner % 2
            mine = column[SHARE * owner : SHARE * (owner + 1), :]
            small_ref[z, x, core, :, 0:BLOCK] = mine
            small_ref[z, x, core, :, BLOCK:SMALL] = mine

    @pl.when(group == GROUPS)
    def _():
        hidden, scale = hidden_terms()
        cotangent = normal_ref[seq].T
        scaled = cotangent * gains_ref[0:1, :]
        unit = hidden * scale
        inner = jnp.mean(scaled * unit, axis=1, keepdims=True)
        ig_ref[...] = (gm_ref[...] + scale * (scaled - unit * inner)).astype(BF16)

    if fast:

        @pl.when(step == (GROUPS + 1) * seqs - 1)
        def _():
            run_rest((2 * GROUPS + 1) * (flipped_ref.shape[1] // LENGTH), [BACK_SCATTER, TAIL_SCATTER], travel)


def back(x, gm, gains, weights, qkv, p, inv, mix, dmix, early, fast):
    tokens, width = x.shape
    seqs = tokens // LENGTH
    piece = (DEPTH, WIDE, CORES, SHARE, width)
    last = GROUPS - 1
    group_at = lambda g: jnp.minimum(g, last)
    seq_at = lambda g, s: jnp.where(g <= last, s, seqs - 1)
    four = lambda rows: pl.BlockSpec((1, 1, rows, LENGTH), lambda g, s: (group_at(g), seq_at(g, s), 0, 0))
    x_rows = pl.BlockSpec((LENGTH, width), lambda g, s: (jnp.where((g == 0) | (g == GROUPS), s, 0), 0))
    end_rows = pl.BlockSpec((LENGTH, width), lambda g, s: (jnp.where(g == GROUPS, s, 0), 0))
    out_specs = [end_rows, ANY, whole((DEPTH, WIDE, CORES, SHARE, SMALL))]
    out_shape = [
        jax.ShapeDtypeStruct((tokens, width), BF16), jax.ShapeDtypeStruct((GROUPS, *piece), BF16),
        jax.ShapeDtypeStruct((DEPTH, WIDE, CORES, SHARE, SMALL), BF16),
    ]
    scratch = [
        pltpu.VMEM((GROUP, BAND, BLOCK), F32), pltpu.VMEM((width, tokens), BF16), pltpu.VMEM((width, tokens), BF16),
        pltpu.VMEM((seqs, width, LENGTH), F32), pltpu.VMEM((HEADS, 1, OFFSETS), F32), pltpu.VMEM(piece, BF16),
        pltpu.VMEM((2, LENGTH, LENGTH), BF16), pltpu.SemaphoreType.DMA,
    ]
    kernel = partial(back_kernel, fast=fast)
    if fast:
        sums = BACK_SUMS
        out_specs += [whole((sums, SHARE, width)), whole((TAIL_SUMS, SHARE, SMALL))]
        out_shape += [jax.ShapeDtypeStruct((sums, SHARE, width), F32), jax.ShapeDtypeStruct((TAIL_SUMS, SHARE, SMALL), F32)]
        scratch += scatter_scratch(sums, SHARE, width) + scatter_scratch(TAIL_SUMS, SHARE, SMALL)
    return pl.pallas_call(
        kernel,
        name="back",
        grid=(GROUPS + 1, seqs),
        in_specs=[
            x_rows, end_rows, whole((8, width)),
            pl.BlockSpec((1, *piece), lambda g, s: (group_at(g), 0, 0, 0, 0, 0)), four(width),
            pl.BlockSpec((1, 1, GROUP, LENGTH, LENGTH), lambda g, s: (group_at(g), seq_at(g, s), 0, 0, 0)),
            pl.BlockSpec((1, 1, GROUP, 1, LENGTH), lambda g, s: (group_at(g), seq_at(g, s), 0, 0, 0)),
            four(GROUP_ROWS), four(GROUP_ROWS), ANY,
        ],
        out_specs=out_specs,
        out_shape=out_shape,
        scratch_shapes=scratch,
        compiler_params=pltpu.CompilerParams(
            vmem_limit_bytes=VMEM_LIMIT, collective_id=3 if fast else None, has_side_effects=fast
        ),
    )(x, gm, gains, weights, qkv, p, inv, mix, dmix, early)


def ordered(rows, w_query, w_key, w_value, w_output, w_in, w_out):
    width = w_query.shape[1]
    groups = [
        jnp.concatenate([one[:, at * GROUP_ROWS : (at + 1) * GROUP_ROWS] for one in (w_query, w_key, w_value)], axis=1)
        for at in range(GROUPS)
    ]
    inner = w_in.reshape(rows, OWNERS, PARTS, SHARE).transpose(2, 0, 1, 3).reshape(PARTS, rows, width)
    outer = w_out.reshape(-1, PARTS, SHARE, width).transpose(1, 0, 2, 3).reshape(PARTS, rows, width)
    parts = [one for at in range(PARTS) for one in (inner[at], outer[at])]
    return jnp.stack(groups + [w_output] + parts)


def small_of(rows, gain_attn, gain_ffn, rel_table):
    entries = jnp.pad(rel_table.reshape(-1, TABLE_SHARE), ((0, 0), (0, SHARE - TABLE_SHARE))).reshape(rows)
    return jnp.pad(jnp.stack([gain_attn, gain_ffn, entries], axis=1), ((0, 0), (0, SMALL - 3)))


def shards(
    hidden_in, out_grad, pooled_gradient, gain_attn, w_query, w_key, w_value, w_output, rel_table, gain_ffn, w_in, w_out,
    pair_flags, instruction_mask, *, fast,
):
    width = hidden_in.shape[1]
    own = (w_query, w_key, w_value, w_output, w_in, w_out)
    if fast:
        shares = ordered(w_query.shape[0], *own)
        small = small_of(w_query.shape[0], gain_attn, gain_ffn, rel_table)[None]
    else:
        gather = lambda one: lax.all_gather(one, "fsdp", axis=0, tiled=True)
        shares = ordered(width, *map(gather, own)).reshape(-1, DEPTH, WIDE, CORES, SHARE, width)
        small = small_of(width, *map(gather, (gain_attn, gain_ffn, rel_table))).reshape(1, DEPTH, WIDE, CORES, SHARE, SMALL)
    flags = pair_flags.reshape(-1, 1, LENGTH)
    instr = instruction_mask.reshape(-1, 1, LENGTH)
    qkv, p, inv, mix, mid, n2, bg, gains, *rest = attend(
        hidden_in, out_grad, pooled_gradient, flags, instr, shares, small, fast
    )
    early = rest[0] if fast else shares
    output, pooled, gm, dmix, parts, *rest = feed(
        n2, bg, mid, flags, instr, pooled_gradient, gains, out_grad, mix, early, shares, fast
    )
    early_sums = rest[0] if fast else None
    input_grad, group_parts, small_parts, *rest = back(hidden_in, gm, gains, early, qkv, p, inv, mix, dmix, parts, fast)
    if fast:
        last = rest[1][:GROUPS].transpose(1, 0, 2).reshape(1, SHARE, width)
        sums = jnp.concatenate([early_sums, rest[0], last])
        table = rest[1][GROUPS, :TABLE_SHARE, 0]
        rows = SHARE
    else:
        sums = jnp.concatenate([parts, group_parts]).reshape(-1, width, width)
        table = small_parts.reshape(OWNERS, SHARE, SMALL)[:, :TABLE_SHARE, 0].reshape(-1)
        rows = width
    groups = [sums[2 * PARTS + 1 + at] for at in range(GROUPS)]
    grad_query, grad_key, grad_value = (
        jnp.concatenate([one[:, at * GROUP_ROWS : (at + 1) * GROUP_ROWS] for one in groups], axis=1) for at in range(3)
    )
    grad_output = sums[2 * PARTS]
    grad_in = sums[0 : 2 * PARTS : 2].reshape(PARTS, rows, OWNERS, SHARE).transpose(1, 2, 0, 3).reshape(rows, -1)
    grad_out = sums[1 : 2 * PARTS : 2].reshape(PARTS, -1, SHARE, width).transpose(1, 0, 2, 3).reshape(-1, width)
    if not fast:
        scatter = lambda one: lax.psum(lax.psum_scatter(one, "fsdp", scatter_dimension=0, tiled=True), "grp").astype(F32)
        grad_query, grad_key, grad_value, grad_output, grad_in, grad_out, table = map(
            scatter, (grad_query, grad_key, grad_value, grad_output, grad_in, grad_out, table)
        )
    weigh = lambda weight, grad: jnp.sum(weight.astype(F32) * grad, axis=1)
    grad_gain = weigh(w_query, grad_query) + weigh(w_key, grad_key) + weigh(w_value, grad_value)
    return (
        output, pooled, input_grad, grad_gain / gain_attn.astype(F32),
        grad_query, grad_key, grad_value, grad_output, table.astype(F32),
        weigh(w_in, grad_in) / gain_ffn.astype(F32), grad_in, grad_out,
    )


def solution(mesh):
    tokens, square, line = P(("grp", "fsdp"), None), P("fsdp", None), P("fsdp")
    cube, flat = P(("grp", "fsdp"), None, None), P(("grp", "fsdp"))
    fast = mesh.shape["fsdp"] == OWNERS and mesh.shape["grp"] == 2
    return jax.shard_map(
        partial(shards, fast=fast),
        mesh=mesh,
        in_specs=(tokens, tokens, cube, line, square, square, square, square, line, line, square, square, flat, flat),
        out_specs=(tokens, cube, tokens, line, square, square, square, square, line, line, square, square),
        check_vma=False,
    )
```

time: 1490 us -> 333 us (0.22)
  local copies, waits for them, and re-layouts: 519 us -> 22.1 us
  matrix products: 435 us -> 0 us
  Pallas kernels: 0 us -> 305 us
  waiting for transfers between devices: 292 us -> 0 us
  other arithmetic: 110 us -> 4.27 us
  blocking collectives: 101 us -> 0 us
  between operations: 17.2 us -> 1.04 us
    dot_general x106 -> x0, matrix products: 435 us -> none  [the longest x24 77.6 us: head_scores(): jnp.einsum('sid,sjd->sij', head_query, head_key, preferred_element_type=j...]
    pallas_call x0 -> x3, Pallas kernels: none -> 305 us  [the longest x1 112 us: feed(): pl.pallas_call(partial(feed_kernel, fast=fast), name='feed', grid=(PARTS...]
    reduce_scatter x6 -> x0, waiting for transfers between devices: 239 us -> none  [the longest x1 114 us: shards(): lax.psum_scatter(grad_outer, 'fsdp', scatter_dimension=0, tiled=True)]
    reshape x42 -> x5, local copies, waits for them, and re-layouts: 141 us -> 4.53 us  [the longest x2 2.6 us: shards(): sums[0:2 * PARTS:2].reshape(PARTS, rows, OWNERS, SHARE)]
    unnamed x2 -> x0, blocking collectives: 96.4 us -> none
    another operation x52 -> x4, local copies, waits for them, and re-layouts: 77.3 us -> 0.82 us  [the longest x2 0.8 us: small_of(): jnp.stack([gain_attn, gain_ffn, entries], axis=1)]
    slice x96 -> x12, local copies, waits for them, and re-layouts: 77.1 us -> 5.04 us  [the longest x2 1.66 us: ordered(): one[:, at * GROUP_ROWS:(at + 1) * GROUP_ROWS]]
    rev x12 -> x0, local copies, waits for them, and re-layouts: 63.1 us -> none  [diagonal_sums(): padded = jnp.pad(jnp.flip(matrix, axis=1), ((0, 0), (0, length)))]
  transfers between devices with their start and end apart: 13 -> 0, of which waited for: 5 -> 0; matrix products, arithmetic and copies ran while one was open for 64% -> 0% of each run, Pallas kernels for 0% -> 0%
where the time goes in v2:
time: 333 us; the launch traced here: 332 us
  Pallas kernels  305 us (92%)
  local copies, waits for them, and re-layouts  22.1 us (7%)
  other arithmetic  4.27 us (1%)
    pallas_call x1, Pallas kernels, feed(): pl.pallas_call(partial(feed_kernel, fast=fast), name='feed', grid=(PARTS...  112 us
    pallas_call x1, Pallas kernels, back(): pl.pallas_call(kernel, name='back', grid=(GROUPS + 1, seqs), in_specs=[x_...  101 us
    pallas_call x1, Pallas kernels, attend(): pl.pallas_call(kernel, name='attend', grid=(GROUPS, seqs), in_specs=in_sp...  91.9 us
    unnamed x41, local copies, waits for them, and re-layouts  7.32 us

profile of v2, /device:TPU:0, one launch (start us, length us, event | category | flops | bytes accessed | tf_op | source)
XLA Modules:
  0.0 332.4 jit_solution(9559758444326589679)
XLA Ops:
  0.7 0.7 pad_bitcast_fusion.1
  1.3 0.7 pad_maximum_fusion.3
  2.1 0.6 pad_bitcast_fusion.small_hbm
  2.8 0.8 fusion.10
  3.5 0.9 fusion.8
  4.4 1.7 reshape.56
  7.5 0.9 copy-done
  8.4 91.9 %attend.1 = (bf16[3,4,768,512]{3,2,1,0:T(8,128)(2,1)}, bf16[3,4,4,512,512]{4,3,2,1,0:T(8,128)(2,1)}, f32[3,4,4,1,512]{4,3,2,1,0:T(1,128)}, bf16[3,4,256,512]{3,2...) custom-call(bf16[2048,768]{1,0:T(8,128)(2,1)} %x_ref.3, ...), custom_call_target="tpu_custom_call" | custom-call | tf_op jit(solution)/shard_map/attend/pallas_call | solution.py:535
  100.3 112.1 %feed.1 = (bf16[2048,768]{1,0:T(8,128)(2,1)}, f32[4,2,768]{2,1,0:T(2,128)}, f32[2048,768]{1,0:T(8,128)}, bf16[3,4,256,512]{3,2,1,0:T(8,128)(2,1)}, bf16[9,4,2,2,...) custom-call(bf16[2048,768]{1,0:T(8,128)(2,1)} %get-tuple-element.30.n2_ref, ...), custom_call_target="tpu_custom_call" | custom-call | tf_op jit(solution)/shard_map/feed/pallas_call | solution.py:712
  212.4 100.9 %back.1 = (bf16[2048,768]{1,0:T(8,128)(2,1)}, bf16[3,4,2,2,48,768]{5,4,3,2,1,0:T(8,128)(2,1)}, bf16[4,2,2,48,256]{4,3,2,1,0:T(8,128)(2,1)}, f32[6,48,768]{2,1,0:T(8,128)}, f32[4,48,256]{2,1,0:T(8,128)}) custom-call(bf16[2048,768]{1,0:T(8,128)(2,1)} %x_ref.3, f32[2048,768]{1,0:T(8,128)} %get-tuple-element.38.gm_ref, f32[8,768]{1,0:T(8,128)} %get-tuple-element.33.gains_ref, ...), custom_call_target="tpu_custom_call" | custom-call | tf_op jit(solution)/shard_map/back/pallas_call | solution.py:921
  313.4 1.5 slice_reduce_fusion
  314.8 0.9 slice_bitcast_fusion.4
  316.0 1.7 slice_bitcast_fusion
  317.8 0.8 multiply_reduce_fusion.2
  318.6 0.8 multiply_reduce_fusion.1
  319.4 0.8 multiply_reduce_fusion.3
  320.9 0.9 fusion.3
  321.8 0.8 reshape.59
  322.6 1.0 copy.42
  323.6 1.8 reshape.60
  325.6 0.5 convert_divide_fusion
  326.2 3.9 %copy.62 = bf16[2048,768]{1,0:T(8,128)(2,1)} copy(bf16[2048,768]{1,0:T(8,128)(2,1)} %get-tuple-element.98) | data formatting | bytes 6291456
  330.1 0.6 copy.63
  330.7 1.7 copy.64
  (57 shorter events, 2.4 us)
Async XLA Ops:
  0.6 6.7 %copy-start.10 = (bf16[48,768]{1,0:T(8,128)(2,1)S(1)}, bf16[48,768]{1,0:T(8,128)(2,1)}, u32[]{:S(2)}) copy-start(bf16[48,768]{1,0:T(8,128)(2,1)} %param.21) | copy-start | bytes 221188
  3.5 3.8 %copy-start.6 = (bf16[192,768]{1,0:T(8,128)(2,1)S(1)}, bf16[192,768]{1,0:T(8,128)(2,1)}, u32[]{:S(2)}) copy-start(bf16[192,768]{1,0:T(8,128)(2,1)} %param.25) | copy-start | bytes 884740
  7.5 0.9 copy-start
  313.3 4.5 %copy-start.8 = (bf16[48,768]{1,0:T(8,128)(2,1)S(1)}, bf16[48,768]{1,0:T(8,128)(2,1)}, u32[]{:S(2)}) copy-start(bf16[48,768]{1,0:T(8,128)(2,1)} %param.19) | copy-start | bytes 221188
  313.3 5.3 %copy-start.7 = (bf16[48,768]{1,0:T(8,128)(2,1)S(1)}, bf16[48,768]{1,0:T(8,128)(2,1)}, u32[]{:S(2)}) copy-start(bf16[48,768]{1,0:T(8,128)(2,1)} %param.20) | copy-start | bytes 221188
  313.3 6.1 %copy-start.9 = (bf16[48,768]{1,0:T(8,128)(2,1)S(1)}, bf16[48,768]{1,0:T(8,128)(2,1)}, u32[]{:S(2)}) copy-start(bf16[48,768]{1,0:T(8,128)(2,1)} %param.18) | copy-start | bytes 221188
  313.4 6.8 %copy-start.12 = (bf16[48]{0:T(256)(128)(2,1)S(1)}, bf16[48]{0:T(256)(128)(2,1)}, u32[]{:S(2)}) copy-start(bf16[48]{0:T(256)(128)(2,1)} %param.17) | copy-start | bytes 292
  313.4 7.4 %copy-start.5 = (f32[5,48,768]{2,1,0:T(8,128)S(1)}, f32[5,48,768]{2,1,0:T(8,128)}, u32[]{:S(2)}) copy-start(f32[5,48,768]{2,1,0:T(8,128)} %get-tuple-element.47) | copy-start | bytes 2211844
  313.4 7.4 %copy-start.3 = (f32[6,48,768]{2,1,0:T(8,128)S(1)}, f32[6,48,768]{2,1,0:T(8,128)}, u32[]{:S(2)}) copy-start(f32[6,48,768]{2,1,0:T(8,128)} %get-tuple-element.45) | copy-start | bytes 2654212
  322.6 2.9 copy-start.4
  322.6 3.0 copy-start.13
  325.4 4.6 %copy-start.2 = (f32[48,3072]{1,0:T(8,128)}, f32[48,3072]{1,0:T(8,128)S(1)}, u32[]{:S(2)}) copy-start(f32[48,3072]{1,0:T(8,128)S(1)} %reshape.60) | copy-start | bytes 1769476
  326.2 3.9 %copy-start.11 = (f32[4,2,768]{2,1,0:T(2,128)S(1)}, f32[4,2,768]{2,1,0:T(2,128)}, u32[]{:S(2)}) copy-start(f32[4,2,768]{2,1,0:T(2,128)} %get-tuple-element.99) | copy-start | bytes 73732
  326.2 4.5 %copy-start.1 = (bf16[2048,768]{1,0:T(8,128)(2,1)S(1)}, bf16[2048,768]{1,0:T(8,128)(2,1)}, u32[]{:S(2)}) copy-start(bf16[2048,768]{1,0:T(8,128)(2,1)} %get-tuple-element.100) | copy-start | bytes 9437188

commit v3 on v2

--- a/solution.py
+++ b/solution.py
@@ -101,10 +101,14 @@
     return scale * (scaled - unit * inner), jnp.sum(cotangent * unit, axis=0, keepdims=True)
 
 
-def table_places():
+def owners_of():
     at = iota((1, OWNERS * SHARE), 1)
     owner = sum((at >= SHARE * one).astype(jnp.int32) for one in range(1, OWNERS))
-    inside = at - SHARE * owner
+    return owner, at - SHARE * owner
+
+
+def table_places():
+    owner, inside = owners_of()
     entry = owner * TABLE_SHARE + inside
     bucket = sum((entry >= HEADS * one).astype(jnp.int32) for one in range(1, BUCKETS))
     return entry - HEADS * bucket, jnp.where(inside < TABLE_SHARE, bucket, -1)
@@ -122,7 +126,7 @@
         return (grp, z * (WIDE * CORES) + x * CORES + core)
 
     return dict(
-        z=z, x=x, core=core,
+        at=at, y=grp, z=z, x=x, core=core,
         over_y=device(1 - grp, z, x, core),
         over_x=device(grp, z, 1 - x, core),
         over_core=device(grp, z, x, 1 - core),
@@ -139,8 +143,27 @@
     pl.semaphore_wait(barrier, DEPTH + 2)
 
 
-def gather_phase(phase, sem, here, share_ref, whole_ref, sent, got, own_sem):
+def others(here):
+    at = here["at"]
+    for one in range(1, OWNERS):
+        yield one, (here["y"], lax.rem(at + one, OWNERS)), lax.rem(at + OWNERS - one, OWNERS)
+
+
+def greet_all(here):
+    barrier = pltpu.get_barrier_semaphore()
+    pl.semaphore_signal(barrier, inc=1, device_id=here["over_y"], device_id_type=MESH_ID)
+    for _, device, _ in others(here):
+        pl.semaphore_signal(barrier, inc=1, device_id=device, device_id_type=MESH_ID)
+    pl.semaphore_wait(barrier, OWNERS)
+
+
+def gather_phase(phase, sem, here, share_ref, whole_ref, sent, got, own_sem, shared=False):
     z, x, core = here["z"], here["x"], here["core"]
+    every = slice(None)
+    half = share_ref.shape[-1] // 2
+    lanes = pl.ds(pl.multiple_of(here["y"] * half, half), half) if shared else every
+    other = pl.ds(pl.multiple_of((1 - here["y"]) * half, half), half) if shared else every
+    mine = share_ref.at[:, lanes] if shared else share_ref
 
     def copy(source, where, channel, device):
         return pltpu.make_async_remote_copy(
@@ -148,14 +171,18 @@
             device_id=device, device_id_type=MESH_ID,
         )
 
-    own = lambda: pltpu.make_async_copy(share_ref, whole_ref.at[z, x, core], own_sem.at[sem])
-    every = slice(None)
-    line_out = lambda one: copy(share_ref, (z, x, core), one, here["over_z"][one])
-    line_in = lambda one: copy(share_ref, (here["behind"][one], x, core), one, here["over_z"][one])
-    side_out = lambda: copy(whole_ref.at[every, x, core], (every, x, core), 3, here["over_x"])
-    side_in = lambda: copy(whole_ref.at[every, x, core], (every, 1 - x, core), 3, here["over_x"])
-    core_out = lambda: copy(whole_ref.at[every, every, core], (every, every, core), 4, here["over_core"])
-    core_in = lambda: copy(whole_ref.at[every, every, core], (every, every, 1 - core), 4, here["over_core"])
+    def same(where, channel, device):
+        return copy(whole_ref.at[where], where, channel, device)
+
+    own = lambda: pltpu.make_async_copy(mine, whole_ref.at[z, x, core, every, lanes], own_sem.at[sem])
+    line_out = lambda one: copy(mine, (z, x, core, every, lanes), one, here["over_z"][one])
+    line_in = lambda one: copy(mine, (here["behind"][one], x, core, every, lanes), one, here["over_z"][one])
+    side_out = lambda: same((every, x, core, every, lanes), 3, here["over_x"])
+    side_in = lambda: same((every, 1 - x, core, every, lanes), 3, here["over_x"])
+    group_out = lambda: same((every, every, core, every, lanes), 5, here["over_y"])
+    group_in = lambda: same((every, every, core, every, other), 5, here["over_y"])
+    core_out = lambda: same((every, every, core), 4, here["over_core"])
+    core_in = lambda: same((every, every, 1 - core), 4, here["over_core"])
     if phase == 0:
         own().start()
         for one in range(DEPTH - 1):
@@ -167,18 +194,26 @@
         side_out().start()
     elif phase == 2:
         side_in().wait_recv()
+        group_out().start()
+    elif phase == 3:
+        if shared:
+            group_in().wait_recv()
+        else:
+            side_in().wait_recv()
         core_out().start()
     else:
         for one in range(DEPTH - 1):
             line_out(one).wait_send()
         side_out().wait_send()
+        if shared:
+            group_out().wait_send()
         core_out().wait_send()
         core_in().wait_recv()
 
 
 def scatter_phase(phase, piece, here, part_ref, out_ref, own, fromc, fromx, fromz, last, sent, got, own_sem):
     z, x, core = here["z"], here["x"], here["core"]
-    slot = lax.rem(piece, 2)
+    slot = lax.rem(piece, own.shape[0])
 
     def remote(source, target, channel, device):
         return pltpu.make_async_remote_copy(
@@ -205,8 +240,7 @@
 
         def one(at, _):
             for side in range(WIDE):
-                mine = own[slot, at, side].astype(F32) + fromc[piece, at, side].astype(F32)
-                fromc[piece, at, side] = mine.astype(BF16)
+                fromc[piece, at, side] = own[slot, at, side] + fromc[piece, at, side]
             return 0
 
         lax.fori_loop(0, DEPTH, one, 0)
@@ -215,8 +249,7 @@
         over_x().wait()
 
         def one(at, _):
-            mine = fromc[piece, at, x].astype(F32) + fromx[piece, at].astype(F32)
-            fromc[piece, at, x] = mine.astype(BF16)
+            fromc[piece, at, x] = fromc[piece, at, x] + fromx[piece, at]
             return 0
 
         lax.fori_loop(0, DEPTH, one, 0)
@@ -262,33 +295,26 @@
 
 
 def gather_sems(pieces):
-    return [pltpu.SemaphoreType.DMA((5, pieces)), pltpu.SemaphoreType.DMA((5, pieces)), pltpu.SemaphoreType.DMA((pieces,))]
-
-
-def scatter_scratch(pieces, rows, columns):
+    return [pltpu.SemaphoreType.DMA((6, pieces)), pltpu.SemaphoreType.DMA((6, pieces)), pltpu.SemaphoreType.DMA((pieces,))]
+
+
+def scatter_scratch(pieces, rows, columns, places=2):
     return [
-        pltpu.VMEM((2, DEPTH, WIDE, rows, columns), BF16),
+        pltpu.VMEM((places, DEPTH, WIDE, rows, columns), BF16),
         pltpu.VMEM((pieces, DEPTH, WIDE, rows, columns), BF16),
         pltpu.VMEM((pieces, DEPTH, rows, columns), BF16),
         pltpu.VMEM((pieces, DEPTH, rows, columns), BF16),
         pltpu.VMEM((pieces, rows, columns), BF16),
         pltpu.SemaphoreType.DMA((6, pieces)),
         pltpu.SemaphoreType.DMA((6, pieces)),
-        pltpu.SemaphoreType.DMA((2,)),
+        pltpu.SemaphoreType.DMA((places,)),
     ]
 
 
 ATTEND_PIECES, FEED_PIECES = 8, 4
-ATTEND_TABLE = {
-    1: (None, 0, 3, 5),
-    2: (0, 4, 8, 10),
-    3: (3, 8, 12, 14),
-    4: (6, 11, 15, 17),
-    5: (9, 14, 18, 20),
-    6: (12, 17, 21, 23),
-    7: (15, 20, 24, 25),
-}
-FEED_GATHER = {0: (0, 5, 10, 12), 1: (3, 8, 13, 15), 2: (6, 11, 16, 18), 3: (9, 14, 19, 21)}
+ATTEND_DIRECT = {1: (None, 0, None, 3, 5), 3: (2, 7, None, 12, 14), 6: (8, 13, None, 18, 20)}
+ATTEND_SHARED = {2: (0, 4, 7, 11, 13), 4: (4, 8, 12, 16, 18), 5: (6, 10, 15, 19, 21), 7: (11, 15, 19, 23, 25)}
+FEED_GATHER = {0: (0, 5, None, 10, 12), 1: (3, 8, None, 13, 15), 2: (6, 11, None, 16, 18), 3: (9, 14, None, 19, 21)}
 FEED_SUMS = 5
 FEED_SCATTER = {
     0: (8, 10, 15, 20, 23), 1: (11, 13, 18, 23, 26), 2: (16, 18, 23, 28, 31), 3: (19, 21, 26, 31, 34), 4: (24, 26, 31, 36, 39),
@@ -299,28 +325,37 @@
     4: (12, 14, 19, 24, 27), 5: (16, 18, 23, 27, 29),
 }
 TAIL_SUMS = 4
-TAIL_SCATTER = {0: (24, 25, 26, 27, 28), 1: (25, 26, 27, 28, 29), 2: (26, 27, 28, 29, 30), 3: (27, 28, 29, 30, 31)}
+TAIL_SCATTER = {0: (None, 24, 26, 28, 30), 1: (None, 25, 27, 29, 31), 2: (None, 26, 28, 30, 32), 3: (24, 27, 29, 31, 33)}
 
 
 def attend_kernel(
-    x_ref, og_ref, pg_ref, flags_ref, instr_ref, shares_hbm, small_hbm,
-    qkv_ref, p_ref, inv_ref, mix_ref, mid_ref, n2_ref, bg_ref, gains_ref, weights_hbm, smalls_hbm,
-    band_ref, aux_ref, normed_ref, wg_ref, wo_ref, small_ref, table_ref, cur_ref, nxt_ref, sa_ref, sb_ref, sems,
-    *comm, fast,
+    x_hbm, og_hbm, pg_ref, flags_ref, instr_ref, shares_hbm, small_hbm,
+    qkv_ref, p_ref, inv_ref, mix_ref, mid_ref, n2_ref, bg_hbm, gains_ref, weights_hbm,
+    x_ref, bg_ref, mixed_ref, band_ref, aux_ref, normed_ref, wg_ref, wo_ref, small_ref, table_ref, cur_ref, nxt_ref, sa_ref, sb_ref,
+    sems, *comm, fast,
 ):
     group, seq = pl.program_id(0), pl.program_id(1)
     seqs = pl.num_programs(1)
     step = group * seqs + seq
     width = x_ref.shape[1]
     if fast:
-        main_sems, first_sems, small_sems = comm[0:3], comm[3:6], comm[6:9]
+        main_sems, first_sems, small_sent, small_got = comm[0:3], comm[3:6], comm[6], comm[7]
         here = place()
 
-        def main(phase, piece):
-            gather_phase(phase, piece, here, shares_hbm.at[piece], weights_hbm.at[piece], *main_sems)
-
-        def small(phase):
-            gather_phase(phase, 0, here, small_hbm.at[0], smalls_hbm.at[0], *small_sems)
+        def main(phase, piece, shared=False):
+            gather_phase(phase, piece, here, shares_hbm.at[piece], weights_hbm.at[piece], *main_sems, shared=shared)
+
+        def small(start):
+            for one, device, source in others(here):
+                copy = lambda where: pltpu.make_async_remote_copy(
+                    src_ref=small_hbm, dst_ref=small_ref.at[where], send_sem=small_sent.at[one], recv_sem=small_got.at[one],
+                    device_id=device, device_id_type=MESH_ID,
+                )
+                if start:
+                    copy(here["at"]).start()
+                else:
+                    copy(source).wait_recv()
+                    copy(here["at"]).wait_send()
 
         def first(phase, which):
             lanes = pl.ds(which * GROUP_ROWS, GROUP_ROWS)
@@ -330,12 +365,17 @@
             )
 
         def travel(slot):
-            run_slot(slot, ATTEND_TABLE, main)
+            run_slot(slot, ATTEND_DIRECT, main)
+            run_slot(slot, ATTEND_SHARED, partial(main, shared=True))
 
         point = lambda at: travel(2 * step + at)
     else:
         point = lambda at: None
-    load_small = lambda: pltpu.make_async_copy(smalls_hbm.at[0], small_ref, sems.at[0])
+    small_own = small_ref.at[here["at"]] if fast else small_ref
+    load_small = lambda: pltpu.make_async_copy(small_hbm, small_own, sems.at[0])
+    load_hidden = lambda: pltpu.make_async_copy(x_hbm, x_ref, sems.at[3])
+    load_grad = lambda: pltpu.make_async_copy(og_hbm, bg_ref, sems.at[4])
+    keep_grad = lambda: pltpu.make_async_copy(bg_ref, bg_hbm, sems.at[4])
     load_group = lambda at: pltpu.make_async_copy(weights_hbm.at[at], wg_ref, sems.at[1])
     load_output = lambda: pltpu.make_async_copy(weights_hbm.at[GROUPS], wo_ref, sems.at[2])
     square = lambda ref: ref[...].reshape(width, width)
@@ -344,15 +384,24 @@
         flags = flags_ref[at]
         chosen, counts = pool_terms(flags, instr_ref[at])
         rows = pl.ds(pl.multiple_of(at * LENGTH, LENGTH), LENGTH)
-        grad_result = og_ref[rows, :].astype(F32) + pool_gradient(chosen, counts, pg_ref[at])
-        bg_ref[rows, :] = grad_result.astype(BF16)
+        bg_ref[rows, :] = (bg_ref[rows, :].astype(F32) + pool_gradient(chosen, counts, pg_ref[at])).astype(BF16)
         row = iota((16, LENGTH), 0)
         aux_ref[0, at] = jnp.where(row == 0, 1 - flags, jnp.where(row == 1, flags, 0)).astype(F32).astype(BF16)
         other = jnp.where(row == 0, flags, jnp.where(row == 1, 1 - flags, 0)).astype(F32) * NEG
         aux_ref[1, at] = other.astype(BF16)
+
+    def normalize(at):
+        rows = pl.ds(pl.multiple_of(at * LENGTH, LENGTH), LENGTH)
         hidden = x_ref[rows, :].astype(F32)
         scale = lax.rsqrt(jnp.mean(hidden * hidden, axis=1, keepdims=True) + EPS)
         normed_ref[at] = (hidden * scale * gains_ref[0:1, :]).astype(BF16)
+
+    def every_seq(act):
+        def one_seq(at, _):
+            act(at)
+            return 0
+
+        lax.fori_loop(0, seqs, one_seq, 0)
 
     def project(at, target):
         target[...] = dot_tt(square(wg_ref), normed_ref[at]).astype(BF16)
@@ -378,19 +427,28 @@
         mixed = dot(values, exponent)
         inverse = 1.0 / mixed[HEAD_DIM : HEAD_DIM + 1, :]
         inv_ref[0, 0, head] = inverse
-        mix_ref[group, seq, head * HEAD_DIM : (head + 1) * HEAD_DIM, :] = (mixed[0:HEAD_DIM, :] * inverse).astype(BF16)
+        mixed = (mixed[0:HEAD_DIM, :] * inverse).astype(BF16)
+        mix_ref[0, 0, head * HEAD_DIM : (head + 1) * HEAD_DIM, :] = mixed
+        mixed_ref[seq, pl.ds(pl.multiple_of(group * GROUP_ROWS + head * HEAD_DIM, HEAD_DIM), HEAD_DIM), :] = mixed
 
     def read_small():
-        load_small().start()
-        load_small().wait()
-        flipped = small_ref[...].reshape(width, SMALL)[:, 0:BLOCK].astype(F32).T
-        gains_ref[...] = flipped[0:8, :]
+        owner, inside = owners_of()
+        spread = (iota((BLOCK, width), 0) == inside).astype(F32).astype(BF16)
+        shares = small_ref[...].astype(F32)
+
+        def line(which):
+            placed = dot(shares[:, which, :].astype(BF16), spread)
+            return jnp.sum(jnp.where(iota((OWNERS, width), 0) == owner, placed, 0.0), axis=0, keepdims=True)
+
+        row = iota((8, width), 0)
+        gains_ref[...] = jnp.where(row == 0, line(0), line(1))
+        table_row = line(2)
         heads, buckets = table_places()
-        entries = jnp.where((iota((16, width), 0) == heads) & (buckets >= 0), flipped[2:3, :], 0.0).astype(BF16)
+        entries = jnp.where((iota((16, width), 0) == heads) & (buckets >= 0), table_row, 0.0).astype(BF16)
         onehot = (bucket_of(iota((OFFSETS, 1), 0) - BLOCKS * BLOCK) == buckets).astype(F32).astype(BF16)
         table_ref[...] = dot_nt(entries, onehot)
 
-    def make_bands():
+    def make_bands(at_group):
         def one_head(head, _):
             table = table_ref[...]
             line = jnp.sum(jnp.where(iota(table.shape, 0) == head, table, 0.0), axis=0, keepdims=True)
@@ -398,41 +456,47 @@
             band_ref[head] = turned[:, BLOCK:].T
             return 0
 
-        lax.fori_loop(0, HEADS, one_head, 0)
-
-    def prepare_all():
-        def one_seq(at, _):
-            prepare(at)
-            return 0
-
-        lax.fori_loop(0, seqs, one_seq, 0)
+        lax.fori_loop(at_group * GROUP, (at_group + 1) * GROUP, one_head, 0)
 
     @pl.when(step == 0)
     def _():
+        load_grad().start()
+        load_hidden().start()
+        load_small().start()
         if fast:
-            greet(here)
-            small(0)
+            greet_all(here)
+            small(True)
             for which in range(3):
                 first(0, which)
-            small(1)
+        load_grad().wait()
+        every_seq(prepare)
+        keep_grad().start()
+        load_hidden().wait()
+        load_small().wait()
+        if fast:
+            small(False)
             first(1, 0)
-            small(2)
+            read_small()
             first(1, 1)
-            small(3)
-            read_small()
+            normalize(0)
+            normalize(1)
             first(1, 2)
             main(0, 1)
-            first(2, 0)
-            prepare_all()
-            first(2, 1)
-            make_bands()
-            first(2, 2)
+            normalize(2)
+            normalize(3)
+            first(3, 0)
+            make_bands(0)
+            first(3, 1)
+            make_bands(1)
+            first(3, 2)
+            make_bands(2)
             for which in range(3):
-                first(3, which)
+                first(4, which)
         else:
             read_small()
-            prepare_all()
-            make_bands()
+            every_seq(normalize)
+            for one in range(GROUPS):
+                make_bands(one)
         load_group(0).start()
         load_group(0).wait()
         project(0, nxt_ref)
@@ -474,19 +538,16 @@
     @pl.when(group == GROUPS - 1)
     def _():
         rows = pl.ds(pl.multiple_of(seq * LENGTH, LENGTH), LENGTH)
-        middle = x_ref[rows, :].astype(F32)
-        output = square(wo_ref)
-        for one in range(GROUPS):
-            middle = middle + dot_tn(mix_ref[one, seq], output[one * GROUP_ROWS : (one + 1) * GROUP_ROWS, :])
+        middle = x_ref[rows, :].astype(F32) + dot_tn(mixed_ref[seq], square(wo_ref))
         mid_ref[...] = middle
         scale = lax.rsqrt(jnp.mean(middle * middle, axis=1, keepdims=True) + EPS)
         n2_ref[...] = (middle * scale * gains_ref[1:2, :]).astype(BF16)
 
-    if fast:
-
-        @pl.when(step == GROUPS * seqs - 1)
-        def _():
-            run_rest(2 * GROUPS * (x_ref.shape[0] // LENGTH), [ATTEND_TABLE], travel)
+    @pl.when(step == GROUPS * seqs - 1)
+    def _():
+        keep_grad().wait()
+        if fast:
+            run_rest(2 * GROUPS * (x_ref.shape[0] // LENGTH), [ATTEND_DIRECT, ATTEND_SHARED], travel)
 
 
 def attend(x, og, pg, flags, instr, shares, small, fast):
@@ -498,7 +559,7 @@
         pl.BlockSpec((1, 1, width, LENGTH), lambda g, s: (g, s, 0, 0)),
         pl.BlockSpec((1, 1, GROUP, LENGTH, LENGTH), lambda g, s: (g, s, 0, 0, 0)),
         pl.BlockSpec((1, 1, GROUP, 1, LENGTH), lambda g, s: (g, s, 0, 0, 0)),
-        whole((GROUPS, seqs, GROUP_ROWS, LENGTH)), last_rows, last_rows, whole((tokens, width)), whole((8, width)),
+        pl.BlockSpec((1, 1, GROUP_ROWS, LENGTH), lambda g, s: (g, s, 0, 0)), last_rows, last_rows, ANY, whole((8, width)),
     ]
     out_shape = [
         jax.ShapeDtypeStruct((GROUPS, seqs, width, LENGTH), BF16),
@@ -508,29 +569,26 @@
         jax.ShapeDtypeStruct((tokens, width), F32), low, low, jax.ShapeDtypeStruct((8, width), F32),
     ]
     scratch = [
+        pltpu.VMEM((tokens, width), BF16), pltpu.VMEM((tokens, width), BF16), pltpu.VMEM((seqs, width, LENGTH), BF16),
         pltpu.VMEM((HEADS, BAND, BLOCK), F32), pltpu.VMEM((2, seqs, 16, LENGTH), BF16),
         pltpu.VMEM((seqs, LENGTH, width), BF16), pltpu.VMEM((DEPTH, WIDE, CORES, SHARE, width), BF16),
-        pltpu.VMEM((DEPTH, WIDE, CORES, SHARE, width), BF16), pltpu.VMEM((DEPTH, WIDE, CORES, SHARE, SMALL), BF16), pltpu.VMEM((16, OFFSETS), F32),
+        pltpu.VMEM((DEPTH, WIDE, CORES, SHARE, width), BF16), pltpu.VMEM((OWNERS, 16, BLOCK), BF16), pltpu.VMEM((16, OFFSETS), F32),
         pltpu.VMEM((width, LENGTH), BF16), pltpu.VMEM((width, LENGTH), BF16),
-        pltpu.VMEM((LENGTH, LENGTH), F32), pltpu.VMEM((LENGTH, LENGTH), F32), pltpu.SemaphoreType.DMA((3,)),
+        pltpu.VMEM((LENGTH, LENGTH), F32), pltpu.VMEM((LENGTH, LENGTH), F32), pltpu.SemaphoreType.DMA((5,)),
     ]
     in_specs = [
-        whole((tokens, width)), whole((tokens, width)), whole((seqs, 2, width)), whole((seqs, 1, LENGTH)),
-        whole((seqs, 1, LENGTH)), ANY, ANY,
+        ANY, ANY, whole((seqs, 2, width)), whole((seqs, 1, LENGTH)), whole((seqs, 1, LENGTH)), ANY, ANY,
     ]
     if fast:
         kernel = partial(attend_kernel, fast=True)
-        out_specs += [ANY, ANY]
-        out_shape += [
-            jax.ShapeDtypeStruct((ATTEND_PIECES, DEPTH, WIDE, CORES, SHARE, width), BF16),
-            jax.ShapeDtypeStruct((1, DEPTH, WIDE, CORES, SHARE, SMALL), BF16),
-        ]
-        scratch += gather_sems(ATTEND_PIECES) + gather_sems(3) + gather_sems(1)
+        out_specs += [ANY]
+        out_shape += [jax.ShapeDtypeStruct((ATTEND_PIECES, DEPTH, WIDE, CORES, SHARE, width), BF16)]
+        scratch += gather_sems(ATTEND_PIECES) + gather_sems(3) + [pltpu.SemaphoreType.DMA((OWNERS,)), pltpu.SemaphoreType.DMA((OWNERS,))]
     else:
 
         def kernel(*refs):
             inputs, outputs, rest = refs[:7], refs[7:15], refs[15:]
-            attend_kernel(*inputs, *outputs, inputs[5], inputs[6], *rest, fast=False)
+            attend_kernel(*inputs, *outputs, inputs[5], *rest, fast=False)
 
     return pl.pallas_call(
         kernel,
@@ -547,20 +605,20 @@
 
 
 def feed_kernel(
-    n2_ref, bg_ref, mid_hbm, flags_ref, instr_ref, pg_ref, gains_ref, og_ref, mid_ref, mix_ref, early_hbm, late_hbm,
+    n2_hbm, bg_hbm, mid_hbm, flags_ref, instr_ref, gains_ref, mid_ref, mix_ref, early_hbm, late_hbm,
     out_ref, pooled_ref, gm_ref, dmix_ref, parts_hbm, *rest, fast,
 ):
     if fast:
         sums_ref, gathered_hbm = rest[0:2]
         rest = rest[2:]
-    res_ref, dn2_ref, act_ref, dinner_ref, win_ref, wout_ref, wo_ref, dwo_ref, staged_ref, sems = rest[:10]
+    n2_ref, bg_ref, res_ref, dn2_ref, act_ref, dinner_ref, win_ref, wout_ref, wo_ref, dwo_ref, staged_ref, sems, block_sems = rest[:13]
     part, block = pl.program_id(0), pl.program_id(1)
     blocks = pl.num_programs(1)
     step = part * blocks + block
-    width = n2_ref.shape[1]
+    width = res_ref.shape[1]
     rows = pl.ds(pl.multiple_of(block * LENGTH, LENGTH), LENGTH)
     if fast:
-        sems_of, scratch = rest[10:13], rest[13:]
+        sems_of, scratch = rest[13:16], rest[16:]
         here = place()
 
         def travel(slot):
@@ -592,21 +650,31 @@
         else:
             both(early_hbm, 4)
 
-    load_middle = lambda: pltpu.make_async_copy(mid_hbm, res_ref, sems.at[0, 2])
+
+    def load_block(at, start):
+        mine = pl.ds(pl.multiple_of(at * LENGTH, LENGTH), LENGTH)
+        for which, (source, target) in enumerate(((n2_hbm, n2_ref), (bg_hbm, bg_ref), (mid_hbm, res_ref))):
+            copy = pltpu.make_async_copy(source.at[mine], target.at[mine], block_sems.at[which, at])
+            copy.start() if start else copy.wait()
+
     load_output = lambda: pltpu.make_async_copy(early_hbm.at[GROUPS], wo_ref, sems.at[1, 2])
     keep = lambda at, which: pltpu.make_async_copy(staged_ref.at[which], parts_hbm.at[2 * at + which], sems.at[which, 3])
 
     @pl.when(step == 0)
     def _():
-        load_middle().start()
+        weights(0, True)
+        for at in range(res_ref.shape[0] // LENGTH):
+            load_block(at, True)
         load_output().start()
-        weights(0, True)
         if fast:
             greet(here)
-        dn2_ref[...] = jnp.zeros_like(dn2_ref)
         dwo_ref[...] = jnp.zeros_like(dwo_ref)
-        load_middle().wait()
         load_output().wait()
+
+    @pl.when(part == 0)
+    def _():
+        dn2_ref[rows, :] = jnp.zeros((LENGTH, width), F32)
+        load_block(block, False)
 
     @pl.when((part < PARTS) & (block == 0))
     def _():
@@ -666,11 +734,9 @@
         total = dot(picks, high) + dot(picks, low)
         total = total / jnp.where(iota((8, 1), 0) == 0, counts[0], counts[1])
         pooled_ref[block] = total[0:2, :]
-        grad_result = og_ref[...].astype(F32) + pool_gradient(chosen, counts, pg_ref[block])
         change, _ = norm_back(mid_ref[...], gains_ref[1:2, :], dn2_ref[rows, :])
-        grad_middle = grad_result + change
-        gm_ref[...] = grad_middle
-        out_low = grad_middle.astype(BF16)
+        out_low = (bg_ref[rows, :].astype(F32) + change).astype(BF16)
+        gm_ref[...] = out_low
         output = square(wo_ref)
         for group in range(GROUPS):
             mine = slice(group * GROUP_ROWS, (group + 1) * GROUP_ROWS)
@@ -685,7 +751,7 @@
         keep(PARTS, 0).wait()
 
 
-def feed(n2, bg, mid, flags, instr, pg, gains, og, mix, early, late, fast):
+def feed(n2, bg, mid, flags, instr, gains, mix, early, late, fast):
     tokens, width = n2.shape
     seqs = tokens // LENGTH
     rows = pl.BlockSpec((LENGTH, width), lambda c, m: (jnp.where(c == PARTS, m, 0), 0))
@@ -695,13 +761,15 @@
     out_specs = [rows, whole((seqs, 2, width)), rows, heads, ANY]
     out_shape = [
         jax.ShapeDtypeStruct((tokens, width), BF16), jax.ShapeDtypeStruct((seqs, 2, width), F32),
-        jax.ShapeDtypeStruct((tokens, width), F32), jax.ShapeDtypeStruct((GROUPS, seqs, GROUP_ROWS, LENGTH), BF16),
+        jax.ShapeDtypeStruct((tokens, width), BF16), jax.ShapeDtypeStruct((GROUPS, seqs, GROUP_ROWS, LENGTH), BF16),
         jax.ShapeDtypeStruct((2 * PARTS + 1, *piece), BF16),
     ]
     scratch = [
+        pltpu.VMEM((tokens, width), BF16), pltpu.VMEM((tokens, width), BF16),
         pltpu.VMEM((tokens, width), F32), pltpu.VMEM((tokens, width), F32), pltpu.VMEM((tokens, width), BF16),
         pltpu.VMEM((tokens, width), BF16), pltpu.VMEM((2, *piece), BF16), pltpu.VMEM((2, *piece), BF16),
         pltpu.VMEM(piece, BF16), pltpu.VMEM((width, width), F32), pltpu.VMEM((2, *piece), BF16), pltpu.SemaphoreType.DMA((2, 4)),
+        pltpu.SemaphoreType.DMA((3, seqs)),
     ]
     if fast:
         out_specs += [whole((sums, SHARE, width)), ANY]
@@ -714,8 +782,7 @@
         name="feed",
         grid=(PARTS + 1, seqs),
         in_specs=[
-            whole((tokens, width)), whole((tokens, width)), ANY, whole((seqs, 1, LENGTH)), whole((seqs, 1, LENGTH)),
-            whole((seqs, 2, width)), whole((8, width)), rows, rows, heads, ANY, ANY,
+            ANY, ANY, ANY, whole((seqs, 1, LENGTH)), whole((seqs, 1, LENGTH)), whole((8, width)), rows, heads, ANY, ANY,
         ],
         out_specs=out_specs,
         out_shape=out_shape,
@@ -723,24 +790,24 @@
         compiler_params=pltpu.CompilerParams(
             vmem_limit_bytes=VMEM_LIMIT, collective_id=2 if fast else None, has_side_effects=fast
         ),
-    )(n2, bg, mid, flags, instr, pg, gains, og, mid, mix, early, late)
+    )(n2, bg, mid, flags, instr, gains, mid, mix, early, late)
 
 
 def back_kernel(
-    x_ref, gm_ref, gains_ref, wg_ref, qkv_ref, p_ref, inv_ref, mix_ref, dmix_ref, early_hbm,
+    x_ref, gm_ref, gains_ref, weights_hbm, qkv_ref, p_ref, inv_ref, mix_ref, dmix_ref, early_hbm,
     ig_ref, parts_hbm, small_ref, *rest, fast,
 ):
     if fast:
         sums_ref, tail_ref = rest[0:2]
         rest = rest[2:]
-    band_ref, flipped_ref, grads_ref, normal_ref, diag_ref, staged_ref, ds_ref, sem = rest[:8]
+    band_ref, flipped_ref, grads_ref, wg_ref, diag_ref, staged_ref, ds_ref, sem, weight_sem = rest[:9]
     group, seq = pl.program_id(0), pl.program_id(1)
     seqs = pl.num_programs(1)
     step = group * seqs + seq
     width = x_ref.shape[1]
     if fast:
         extra = len(scatter_scratch(1, SHARE, width))
-        scratch, tail_scratch = rest[8 : 8 + extra], rest[8 + extra :]
+        scratch, tail_scratch = rest[9 : 9 + extra], rest[9 + extra :]
         here = place()
 
         def main(phase, piece):
@@ -760,24 +827,18 @@
             if phase > 0:
                 scatter_phase(phase, piece, here, small_ref, tail_ref, *tail_scratch)
                 return
-            for which in range(3):
-
-                @pl.when(piece == which)
-                def _(which=which):
-                    lanes = slice(which * SMALL, (which + 1) * SMALL)
-                    scatter_phase(phase, which, here, staged_ref.at[:, :, :, :, lanes], tail_ref, *tail_scratch)
-
-            @pl.when(piece == 3)
-            def _():
-                scatter_phase(phase, 3, here, small_ref, tail_ref, *tail_scratch)
+            scatter_phase(phase, GROUPS, here, small_ref, tail_ref, *tail_scratch)
+
+        def tail_start(which):
+            mine = slice(which * SMALL, (which + 1) * SMALL)
+            scatter_phase(0, which, here, staged_ref.at[:, :, :, :, mine], tail_ref, *tail_scratch)
 
         def travel(slot):
             run_slot(slot, BACK_SCATTER, main)
             run_slot(slot, TAIL_SCATTER, tail)
 
         def point(at):
-            ends = 2 * GROUPS * seqs
-            travel(jnp.where(group < GROUPS, 2 * step + at, ends + seq + at * 10000))
+            travel(2 * step + at)
     else:
         point = lambda at: None
     keep = lambda: pltpu.make_async_copy(staged_ref, parts_hbm.at[group], sem)
@@ -788,6 +849,12 @@
         scale = lax.rsqrt(jnp.mean(hidden * hidden, axis=1, keepdims=True) + EPS)
         return hidden, scale
 
+    load_weights = lambda: pltpu.make_async_copy(weights_hbm.at[0:GROUPS], wg_ref, weight_sem)
+
+    @pl.when(step == 0)
+    def _():
+        load_weights().start()
+
     if fast:
 
         @pl.when(step == 0)
@@ -798,7 +865,6 @@
     def _():
         hidden, scale = hidden_terms()
         flipped_ref[:, lanes] = (hidden * scale * gains_ref[0:1, :]).astype(BF16).T
-        normal_ref[seq] = jnp.zeros((width, LENGTH), F32)
 
     @pl.when((seq == 0) & (group < GROUPS))
     def _():
@@ -819,9 +885,9 @@
                 band_ref[head, span(row - column + BLOCKS - 1, row - column + BLOCKS), :] += value
                 ds_ref[head % 2, seen, mine] = value.astype(BF16)
         scores = ds_ref[head % 2]
-        grads_ref[at : at + HEAD_DIM, lanes] = dot(rows(1), scores).astype(BF16)
-        grads_ref[GROUP_ROWS + at : GROUP_ROWS + at + HEAD_DIM, lanes] = dot_nt(rows(0), scores).astype(BF16)
-        grads_ref[2 * GROUP_ROWS + at : 2 * GROUP_ROWS + at + HEAD_DIM, lanes] = dot_nt(grads, p_ref[0, 0, head]).astype(BF16)
+        grads_ref[group, at : at + HEAD_DIM, lanes] = dot(rows(1), scores).astype(BF16)
+        grads_ref[group, GROUP_ROWS + at : GROUP_ROWS + at + HEAD_DIM, lanes] = dot_nt(rows(0), scores).astype(BF16)
+        grads_ref[group, 2 * GROUP_ROWS + at : 2 * GROUP_ROWS + at + HEAD_DIM, lanes] = dot_nt(grads, p_ref[0, 0, head]).astype(BF16)
 
     point(0)
 
@@ -830,22 +896,35 @@
         one_head(0)
         one_head(1)
 
-    point(1)
+    @pl.when(group < GROUPS)
+    def _():
+        point(1)
 
     @pl.when(group < GROUPS)
     def _():
         one_head(2)
         one_head(3)
-        normal_ref[seq] += dot(wg_ref[...].reshape(width, width), grads_ref[:, lanes])
 
     @pl.when((seq == seqs - 1) & (group < GROUPS))
     def _():
         for first in range(0, width, 256):
-            value = dot_nt(flipped_ref[...], grads_ref[first : first + 256, :]).astype(BF16)
+            value = dot_nt(flipped_ref[...], grads_ref[group, first : first + 256, :]).astype(BF16)
             for owner in range(OWNERS):
                 z, x, core = owner // 4, owner // 2 % 2, owner % 2
                 staged_ref[z, x, core, :, first : first + 256] = value[SHARE * owner : SHARE * (owner + 1), :]
-        keep().start()
+        last_fast = fast & (group == GROUPS - 1)
+
+        @pl.when(jnp.logical_not(last_fast))
+        def _():
+            keep().start()
+
+        if fast:
+
+            @pl.when(last_fast)
+            def _():
+                for which in range(3):
+                    tail_start(which)
+
         for head in range(GROUP):
             turned = band_ref[head].T
             total = jnp.zeros((8, OFFSETS), F32)
@@ -857,7 +936,9 @@
             for row in range(1, 8):
                 moved = jnp.where(line == row, pltpu.roll(total, OFFSETS - row, 1), moved)
             diag_ref[pl.ds(group * GROUP + head, 1)] = jnp.sum(moved, axis=0, keepdims=True)[None]
-        keep().wait()
+        @pl.when(jnp.logical_not(last_fast))
+        def _():
+            keep().wait()
 
     @pl.when((seq == seqs - 1) & (group == GROUPS - 1))
     def _():
@@ -876,20 +957,29 @@
             small_ref[z, x, core, :, 0:BLOCK] = mine
             small_ref[z, x, core, :, BLOCK:SMALL] = mine
 
+    @pl.when((group == GROUPS) & (seq == 0))
+    def _():
+        load_weights().wait()
+
     @pl.when(group == GROUPS)
     def _():
         hidden, scale = hidden_terms()
-        cotangent = normal_ref[seq].T
+        flat = wg_ref[...].reshape(GROUPS, width, width)
+        cotangent = sum(dot(flat[one], grads_ref[one, :, lanes]) for one in range(GROUPS)).T
         scaled = cotangent * gains_ref[0:1, :]
         unit = hidden * scale
         inner = jnp.mean(scaled * unit, axis=1, keepdims=True)
-        ig_ref[...] = (gm_ref[...] + scale * (scaled - unit * inner)).astype(BF16)
+        ig_ref[...] = (gm_ref[...].astype(F32) + scale * (scaled - unit * inner)).astype(BF16)
+
+    @pl.when(group == GROUPS)
+    def _():
+        point(1)
 
     if fast:
 
         @pl.when(step == (GROUPS + 1) * seqs - 1)
         def _():
-            run_rest((2 * GROUPS + 1) * (flipped_ref.shape[1] // LENGTH), [BACK_SCATTER, TAIL_SCATTER], travel)
+            run_rest((2 * GROUPS + 2) * (flipped_ref.shape[1] // LENGTH), [BACK_SCATTER, TAIL_SCATTER], travel)
 
 
 def back(x, gm, gains, weights, qkv, p, inv, mix, dmix, early, fast):
@@ -908,23 +998,24 @@
         jax.ShapeDtypeStruct((DEPTH, WIDE, CORES, SHARE, SMALL), BF16),
     ]
     scratch = [
-        pltpu.VMEM((GROUP, BAND, BLOCK), F32), pltpu.VMEM((width, tokens), BF16), pltpu.VMEM((width, tokens), BF16),
-        pltpu.VMEM((seqs, width, LENGTH), F32), pltpu.VMEM((HEADS, 1, OFFSETS), F32), pltpu.VMEM(piece, BF16),
+        pltpu.VMEM((GROUP, BAND, BLOCK), F32), pltpu.VMEM((width, tokens), BF16), pltpu.VMEM((GROUPS, width, tokens), BF16),
+        pltpu.VMEM((GROUPS, *piece), BF16), pltpu.VMEM((HEADS, 1, OFFSETS), F32), pltpu.VMEM(piece, BF16),
         pltpu.VMEM((2, LENGTH, LENGTH), BF16), pltpu.SemaphoreType.DMA,
+        pltpu.SemaphoreType.DMA,
     ]
     kernel = partial(back_kernel, fast=fast)
     if fast:
         sums = BACK_SUMS
         out_specs += [whole((sums, SHARE, width)), whole((TAIL_SUMS, SHARE, SMALL))]
         out_shape += [jax.ShapeDtypeStruct((sums, SHARE, width), F32), jax.ShapeDtypeStruct((TAIL_SUMS, SHARE, SMALL), F32)]
-        scratch += scatter_scratch(sums, SHARE, width) + scatter_scratch(TAIL_SUMS, SHARE, SMALL)
+        scratch += scatter_scratch(sums, SHARE, width) + scatter_scratch(TAIL_SUMS, SHARE, SMALL, TAIL_SUMS)
     return pl.pallas_call(
         kernel,
         name="back",
         grid=(GROUPS + 1, seqs),
         in_specs=[
             x_rows, end_rows, whole((8, width)),
-            pl.BlockSpec((1, *piece), lambda g, s: (group_at(g), 0, 0, 0, 0, 0)), four(width),
+            ANY, four(width),
             pl.BlockSpec((1, 1, GROUP, LENGTH, LENGTH), lambda g, s: (group_at(g), seq_at(g, s), 0, 0, 0)),
             pl.BlockSpec((1, 1, GROUP, 1, LENGTH), lambda g, s: (group_at(g), seq_at(g, s), 0, 0, 0)),
             four(GROUP_ROWS), four(GROUP_ROWS), ANY,
@@ -950,9 +1041,10 @@
     return jnp.stack(groups + [w_output] + parts)
 
 
-def small_of(rows, gain_attn, gain_ffn, rel_table):
-    entries = jnp.pad(rel_table.reshape(-1, TABLE_SHARE), ((0, 0), (0, SHARE - TABLE_SHARE))).reshape(rows)
-    return jnp.pad(jnp.stack([gain_attn, gain_ffn, entries], axis=1), ((0, 0), (0, SMALL - 3)))
+def small_of(gain_attn, gain_ffn, rel_table):
+    lines = [one.reshape(-1, 1, share) for one, share in ((gain_attn, SHARE), (gain_ffn, SHARE), (rel_table, TABLE_SHARE))]
+    padded = [jnp.pad(one, ((0, 0), (0, 0), (0, BLOCK - one.shape[2]))) for one in lines]
+    return jnp.pad(jnp.concatenate(padded, axis=1), ((0, 0), (0, 13), (0, 0)))
 
 
 def shards(
@@ -963,11 +1055,11 @@
     own = (w_query, w_key, w_value, w_output, w_in, w_out)
     if fast:
         shares = ordered(w_query.shape[0], *own)
-        small = small_of(w_query.shape[0], gain_attn, gain_ffn, rel_table)[None]
+        small = small_of(gain_attn, gain_ffn, rel_table)[0]
     else:
         gather = lambda one: lax.all_gather(one, "fsdp", axis=0, tiled=True)
         shares = ordered(width, *map(gather, own)).reshape(-1, DEPTH, WIDE, CORES, SHARE, width)
-        small = small_of(width, *map(gather, (gain_attn, gain_ffn, rel_table))).reshape(1, DEPTH, WIDE, CORES, SHARE, SMALL)
+        small = small_of(*map(gather, (gain_attn, gain_ffn, rel_table)))
     flags = pair_flags.reshape(-1, 1, LENGTH)
     instr = instruction_mask.reshape(-1, 1, LENGTH)
     qkv, p, inv, mix, mid, n2, bg, gains, *rest = attend(
@@ -975,7 +1067,7 @@
     )
     early = rest[0] if fast else shares
     output, pooled, gm, dmix, parts, *rest = feed(
-        n2, bg, mid, flags, instr, pooled_gradient, gains, out_grad, mix, early, shares, fast
+        n2, bg, mid, flags, instr, gains, mix, early, shares, fast
     )
     early_sums = rest[0] if fast else None
     input_grad, group_parts, small_parts, *rest = back(hidden_in, gm, gains, early, qkv, p, inv, mix, dmix, parts, fast)

time: 333 us -> 305 us (0.916)
  Pallas kernels: 305 us -> 277 us
    pallas_call x1, Pallas kernels: 101 us -> 87.8 us  [back(): pl.pallas_call(kernel, name='back', grid=(GROUPS + 1, seqs), in_specs=[x_...]
    pallas_call x1, Pallas kernels: 91.9 us -> 81.2 us  [attend(): pl.pallas_call(kernel, name='attend', grid=(GROUPS, seqs), in_specs=in_sp...]
    pallas_call x1, Pallas kernels: 112 us -> 108 us  [feed(): pl.pallas_call(partial(feed_kernel, fast=fast), name='feed', grid=(PARTS...]
where the time goes in v3:
time: 305 us; the launch traced here: 304 us
  Pallas kernels  277 us (91%)
  local copies, waits for them, and re-layouts  21.3 us (7%)
  other arithmetic  4.32 us (1%)
    pallas_call x1, Pallas kernels, feed(): pl.pallas_call(partial(feed_kernel, fast=fast), name='feed', grid=(PARTS...  108 us
    pallas_call x1, Pallas kernels, back(): pl.pallas_call(kernel, name='back', grid=(GROUPS + 1, seqs), in_specs=[x_...  87.8 us
    pallas_call x1, Pallas kernels, attend(): pl.pallas_call(kernel, name='attend', grid=(GROUPS, seqs), in_specs=in_sp...  81.2 us
    unnamed x41, local copies, waits for them, and re-layouts  7.32 us

profile of v3, /device:TPU:0, one launch (start us, length us, event | category | flops | bytes accessed | tf_op | source)
XLA Modules:
  0.0 304.1 jit_solution(15462702114071404258)
XLA Ops:
  0.7 0.7 fusion.8
  1.4 0.6 pad_bitcast_fusion.small_hbm
  2.0 0.8 fusion.16
  2.8 0.9 fusion.14
  3.6 1.7 reshape.62
  6.7 0.9 copy-done
  7.6 81.2 %attend.1 = (bf16[3,4,768,512]{3,2,1,0:T(8,128)(2,1)}, bf16[3,4,4,512,512]{4,3,2,1,0:T(8,128)(2,1)}, f32[3,4,4,1,512]{4,3,2,1,0:T(1,128)}, bf16[3,4,256,512]{3,2...) custom-call(bf16[2048,768]{1,0:T(8,128)(2,1)} %x_ref.1, ...), custom_call_target="tpu_custom_call" | custom-call | tf_op jit(solution)/shard_map/attend/pallas_call | solution.py:593
  88.8 108.4 %feed.1 = (bf16[2048,768]{1,0:T(8,128)(2,1)}, f32[4,2,768]{2,1,0:T(2,128)}, bf16[2048,768]{1,0:T(8,128)(2,1)}, bf16[3,4,256,512]{3,2,1,0:T(8,128)(2,1)}, bf16[9,...) custom-call(bf16[2048,768]{1,0:T(8,128)(2,1)} %get-tuple-element.30.n2_hbm, ...), custom_call_target="tpu_custom_call" | custom-call | tf_op jit(solution)/shard_map/feed/pallas_call | solution.py:780
  197.3 87.8 %back.1 = (bf16[2048,768]{1,0:T(8,128)(2,1)}, bf16[3,4,2,2,48,768]{5,4,3,2,1,0:T(8,128)(2,1)}, bf16[4,2,2,48,256]{4,3,2,1,0:T(8,128)(2,1)}, f32[6,48,768]{2,1,0:T(8,128)}, f32[4,48,256]{2,1,0:T(8,128)}) custom-call(bf16[2048,768]{1,0:T(8,128)(2,1)} %x_ref.1, bf16[2048,768]{1,0:T(8,128)(2,1)} %get-tuple-element.38.gm_ref, ...), custom_call_target="tpu_custom_call" | custom-call | tf_op jit(solution)/shard_map/back/pallas_call | solution.py:1012
  285.1 1.5 slice_reduce_fusion
  286.6 0.9 slice_bitcast_fusion.4
  287.8 1.7 slice_bitcast_fusion
  289.6 0.8 multiply_reduce_fusion.2
  290.4 0.8 multiply_reduce_fusion.1
  291.2 0.8 multiply_reduce_fusion.3
  292.0 0.5 convert_divide_fusion.1
  292.6 0.9 fusion.9
  293.5 0.8 reshape.67
  294.4 1.0 copy.31
  295.4 1.8 reshape.68
  297.4 0.5 convert_divide_fusion
  297.9 3.9 %copy.51 = bf16[2048,768]{1,0:T(8,128)(2,1)} copy(bf16[2048,768]{1,0:T(8,128)(2,1)} %get-tuple-element.98) | data formatting | bytes 6291456
  301.8 0.6 copy.52
  302.4 1.7 copy.53
  (55 shorter events, 1.8 us)
Async XLA Ops:
  0.6 5.9 %copy-start.10 = (bf16[48,768]{1,0:T(8,128)(2,1)S(1)}, bf16[48,768]{1,0:T(8,128)(2,1)}, u32[]{:S(2)}) copy-start(bf16[48,768]{1,0:T(8,128)(2,1)} %param.21) | copy-start | bytes 221188
  2.8 3.8 %copy-start.6 = (bf16[192,768]{1,0:T(8,128)(2,1)S(1)}, bf16[192,768]{1,0:T(8,128)(2,1)}, u32[]{:S(2)}) copy-start(bf16[192,768]{1,0:T(8,128)(2,1)} %param.25) | copy-start | bytes 884740
  6.7 0.9 copy-start
  285.1 4.5 %copy-start.8 = (bf16[48,768]{1,0:T(8,128)(2,1)S(1)}, bf16[48,768]{1,0:T(8,128)(2,1)}, u32[]{:S(2)}) copy-start(bf16[48,768]{1,0:T(8,128)(2,1)} %param.19) | copy-start | bytes 221188
  285.1 5.3 %copy-start.7 = (bf16[48,768]{1,0:T(8,128)(2,1)S(1)}, bf16[48,768]{1,0:T(8,128)(2,1)}, u32[]{:S(2)}) copy-start(bf16[48,768]{1,0:T(8,128)(2,1)} %param.20) | copy-start | bytes 221188
  285.1 6.1 %copy-start.9 = (bf16[48,768]{1,0:T(8,128)(2,1)S(1)}, bf16[48,768]{1,0:T(8,128)(2,1)}, u32[]{:S(2)}) copy-start(bf16[48,768]{1,0:T(8,128)(2,1)} %param.18) | copy-start | bytes 221188
  285.1 6.8 %copy-start.12 = (bf16[48]{0:T(256)(128)(2,1)S(1)}, bf16[48]{0:T(256)(128)(2,1)}, u32[]{:S(2)}) copy-start(bf16[48]{0:T(256)(128)(2,1)} %param.17) | copy-start | bytes 292
  285.1 7.4 %copy-start.5 = (f32[5,48,768]{2,1,0:T(8,128)S(1)}, f32[5,48,768]{2,1,0:T(8,128)}, u32[]{:S(2)}) copy-start(f32[5,48,768]{2,1,0:T(8,128)} %get-tuple-element.47) | copy-start | bytes 2211844
  285.1 7.4 %copy-start.3 = (f32[6,48,768]{2,1,0:T(8,128)S(1)}, f32[6,48,768]{2,1,0:T(8,128)}, u32[]{:S(2)}) copy-start(f32[6,48,768]{2,1,0:T(8,128)} %get-tuple-element.45) | copy-start | bytes 2654212
  294.3 2.9 copy-start.4
  294.3 3.0 %copy-start.13 = (bf16[48]{0:T(256)(128)(2,1)S(1)}, bf16[48]{0:T(256)(128)(2,1)}, u32[]{:S(2)}) copy-start(bf16[48]{0:T(256)(128)(2,1)} %param.23) | copy-start | bytes 292
  297.2 4.6 %copy-start.2 = (f32[48,3072]{1,0:T(8,128)}, f32[48,3072]{1,0:T(8,128)S(1)}, u32[]{:S(2)}) copy-start(f32[48,3072]{1,0:T(8,128)S(1)} %reshape.68) | copy-start | bytes 1769476
  297.9 3.9 %copy-start.11 = (f32[4,2,768]{2,1,0:T(2,128)S(1)}, f32[4,2,768]{2,1,0:T(2,128)}, u32[]{:S(2)}) copy-start(f32[4,2,768]{2,1,0:T(2,128)} %get-tuple-element.99) | copy-start | bytes 73732
  297.9 4.5 %copy-start.1 = (bf16[2048,768]{1,0:T(8,128)(2,1)S(1)}, bf16[2048,768]{1,0:T(8,128)(2,1)}, u32[]{:S(2)}) copy-start(bf16[2048,768]{1,0:T(8,128)(2,1)} %get-tuple-element.100) | copy-start | bytes 9437188

commit v4 on v3

--- a/solution.py
+++ b/solution.py
@@ -326,6 +326,30 @@
 }
 TAIL_SUMS = 4
 TAIL_SCATTER = {0: (None, 24, 26, 28, 30), 1: (None, 25, 27, 29, 31), 2: (None, 26, 28, 30, 32), 3: (24, 27, 29, 31, 33)}
+
+
+def arrange_kernel(wq_ref, wk_ref, wv_ref, wo_ref, win_ref, wout_ref, shares_ref, line_ref):
+    for group in range(GROUPS):
+        mine = slice(group * GROUP_ROWS, (group + 1) * GROUP_ROWS)
+        for which, one in enumerate((wq_ref, wk_ref, wv_ref)):
+            shares_ref[group, :, which * GROUP_ROWS : (which + 1) * GROUP_ROWS] = one[:, mine]
+    shares_ref[GROUPS] = wo_ref[...]
+    for part in range(PARTS):
+        for owner in range(OWNERS):
+            at = (owner * PARTS + part) * SHARE
+            line_ref[:, owner * SHARE : (owner + 1) * SHARE] = win_ref[:, at : at + SHARE].astype(F32)
+        shares_ref[GROUPS + 1 + 2 * part] = line_ref[...].astype(BF16)
+        shares_ref[GROUPS + 2 + 2 * part] = wout_ref[part * SHARE : (part + 1) * SHARE, :]
+
+
+def arrange(*weights):
+    width = weights[0].shape[1]
+    return pl.pallas_call(
+        arrange_kernel,
+        name="arrange",
+        out_shape=jax.ShapeDtypeStruct((GROUPS + 1 + 2 * PARTS, SHARE, width), BF16),
+        scratch_shapes=[pltpu.VMEM((SHARE, width), F32)],
+    )(*weights)
 
 
 def attend_kernel(
@@ -669,6 +693,9 @@
         if fast:
             greet(here)
         dwo_ref[...] = jnp.zeros_like(dwo_ref)
+
+    @pl.when((part == PARTS) & (block == 0))
+    def _():
         load_output().wait()
 
     @pl.when(part == 0)
@@ -691,13 +718,14 @@
     def _():
         slot = lax.rem(part, 2)
         inner = dot(n2_ref[rows, :], square(win_ref.at[slot]))
+        grad_active = dot_nt(bg_ref[rows, :], square(wout_ref.at[slot]))
         squared = inner * inner
         half = 0.5 * jnp.tanh(inner * (ROOT + (ROOT * CUBE) * squared)) + 0.5
         active = inner * half
         slope = half + active * (1.0 - half) * (2.0 * ROOT + (6.0 * ROOT * CUBE) * squared)
         active = active.astype(BF16)
         act_ref[rows, :] = active
-        dinner = (dot_nt(bg_ref[rows, :], square(wout_ref.at[slot])) * slope).astype(BF16)
+        dinner = (grad_active * slope).astype(BF16)
         dinner_ref[rows, :] = dinner
         res_ref[rows, :] += dot(active, square(wout_ref.at[slot]))
         dn2_ref[rows, :] += dot_nt(dinner, square(win_ref.at[slot]))
@@ -1029,6 +1057,80 @@
     )(x, gm, gains, weights, qkv, p, inv, mix, dmix, early)
 
 
+def finish_kernel(
+    out_ref, ig_ref, early_ref, late_ref, tail_ref, wq_ref, wk_ref, wv_ref, win_ref, gains_ref,
+    output_ref, input_grad_ref, gq_ref, gk_ref, gv_ref, go_ref, gin_ref, gout_ref, gains_out_ref, table_ref,
+):
+    output_ref[...] = out_ref[...]
+    input_grad_ref[...] = ig_ref[...]
+    step = pl.program_id(0)
+
+    @pl.when(step == 0)
+    def _():
+        for which, target in enumerate((gq_ref, gk_ref, gv_ref)):
+            mine = slice(which * GROUP_ROWS, (which + 1) * GROUP_ROWS)
+            for group in range(GROUPS):
+                value = tail_ref[which] if group == GROUPS - 1 else late_ref[BACK_BEFORE + group, :, mine]
+                target[:, group * GROUP_ROWS : (group + 1) * GROUP_ROWS] = value
+        go_ref[...] = late_ref[2 * PARTS - FEED_SUMS]
+
+    @pl.when(step == 1)
+    def _():
+        for part in range(PARTS):
+            piece = 2 * part + 1
+            gout_ref[part * SHARE : (part + 1) * SHARE, :] = (
+                early_ref[piece] if piece < FEED_SUMS else late_ref[piece - FEED_SUMS]
+            )
+
+    @pl.when(step == 2)
+    def _():
+        for part in range(PARTS):
+            piece = 2 * part
+            value = early_ref[piece] if piece < FEED_SUMS else late_ref[piece - FEED_SUMS]
+            for owner in range(OWNERS):
+                at = (owner * PARTS + part) * SHARE
+                gin_ref[:, at : at + SHARE] = value[:, owner * SHARE : (owner + 1) * SHARE]
+
+    @pl.when(step == pl.num_programs(0) - 1)
+    def _():
+        def weigh(weight_ref, grad_ref):
+            return jnp.sum(weight_ref[...].astype(F32) * grad_ref[...], axis=1, keepdims=True)
+
+        first = weigh(wq_ref, gq_ref) + weigh(wk_ref, gk_ref) + weigh(wv_ref, gv_ref)
+        second = weigh(win_ref, gin_ref)
+        column = iota((SHARE, BLOCK), 1)
+        lines = jnp.where(column == 0, first, jnp.where(column == 1, second, tail_ref[GROUPS, :, 0:BLOCK])).T
+        gains_out_ref[...] = lines[0:2, 0:SHARE] / gains_ref[0:2, 0:SHARE].astype(F32)
+        table_ref[...] = lines[2:3, 0:TABLE_SHARE]
+
+
+def finish(out, ig, early, late, tail, wq, wk, wv, win, gains):
+    tokens, width = out.shape
+    ff = win.shape[1]
+    rows = pl.BlockSpec((LENGTH, width), lambda s: (s, 0))
+    low = jax.ShapeDtypeStruct((tokens, width), BF16)
+    square = whole((SHARE, width))
+    table = lambda *shape: jax.ShapeDtypeStruct(shape, F32)
+    return pl.pallas_call(
+        finish_kernel,
+        name="finish",
+        grid=(tokens // LENGTH,),
+        in_specs=[
+            rows, rows, whole(early.shape), whole(late.shape), whole(tail.shape), square, square, square, whole((SHARE, ff)),
+            whole(gains.shape),
+        ],
+        out_specs=[
+            rows, rows, square, square, square, square, whole((SHARE, ff)), whole((ff // OWNERS, width)), whole((2, SHARE)),
+            whole((1, TABLE_SHARE)),
+        ],
+        out_shape=[
+            low, low, table(SHARE, width), table(SHARE, width), table(SHARE, width), table(SHARE, width), table(SHARE, ff),
+            table(ff // OWNERS, width), table(2, SHARE), table(1, TABLE_SHARE),
+        ],
+        compiler_params=pltpu.CompilerParams(vmem_limit_bytes=VMEM_LIMIT),
+    )(out, ig, early, late, tail, wq, wk, wv, win, gains)
+
+
 def ordered(rows, w_query, w_key, w_value, w_output, w_in, w_out):
     width = w_query.shape[1]
     groups = [
@@ -1054,7 +1156,7 @@
     width = hidden_in.shape[1]
     own = (w_query, w_key, w_value, w_output, w_in, w_out)
     if fast:
-        shares = ordered(w_query.shape[0], *own)
+        shares = arrange(*own)
         small = small_of(gain_attn, gain_ffn, rel_table)[0]
     else:
         gather = lambda one: lax.all_gather(one, "fsdp", axis=0, tiled=True)
@@ -1069,17 +1171,16 @@
     output, pooled, gm, dmix, parts, *rest = feed(
         n2, bg, mid, flags, instr, gains, mix, early, shares, fast
     )
-    early_sums = rest[0] if fast else None
+    early_sums = rest
     input_grad, group_parts, small_parts, *rest = back(hidden_in, gm, gains, early, qkv, p, inv, mix, dmix, parts, fast)
     if fast:
-        last = rest[1][:GROUPS].transpose(1, 0, 2).reshape(1, SHARE, width)
-        sums = jnp.concatenate([early_sums, rest[0], last])
-        table = rest[1][GROUPS, :TABLE_SHARE, 0]
-        rows = SHARE
-    else:
-        sums = jnp.concatenate([parts, group_parts]).reshape(-1, width, width)
-        table = small_parts.reshape(OWNERS, SHARE, SMALL)[:, :TABLE_SHARE, 0].reshape(-1)
-        rows = width
+        output, input_grad, *grads, gains, table = finish(
+            output, input_grad, early_sums[0], *rest, w_query, w_key, w_value, w_in, small
+        )
+        return (output, pooled, input_grad, gains[0], *grads[:4], table[0], gains[1], *grads[4:])
+    sums = jnp.concatenate([parts, group_parts]).reshape(-1, width, width)
+    table = small_parts.reshape(OWNERS, SHARE, SMALL)[:, :TABLE_SHARE, 0].reshape(-1)
+    rows = width
     groups = [sums[2 * PARTS + 1 + at] for at in range(GROUPS)]
     grad_query, grad_key, grad_value = (
         jnp.concatenate([one[:, at * GROUP_ROWS : (at + 1) * GROUP_ROWS] for one in groups], axis=1) for at in range(3)
@@ -1087,11 +1188,10 @@
     grad_output = sums[2 * PARTS]
     grad_in = sums[0 : 2 * PARTS : 2].reshape(PARTS, rows, OWNERS, SHARE).transpose(1, 2, 0, 3).reshape(rows, -1)
     grad_out = sums[1 : 2 * PARTS : 2].reshape(PARTS, -1, SHARE, width).transpose(1, 0, 2, 3).reshape(-1, width)
-    if not fast:
-        scatter = lambda one: lax.psum(lax.psum_scatter(one, "fsdp", scatter_dimension=0, tiled=True), "grp").astype(F32)
-        grad_query, grad_key, grad_value, grad_output, grad_in, grad_out, table = map(
-            scatter, (grad_query, grad_key, grad_value, grad_output, grad_in, grad_out, table)
-        )
+    scatter = lambda one: lax.psum(lax.psum_scatter(one, "fsdp", scatter_dimension=0, tiled=True), "grp").astype(F32)
+    grad_query, grad_key, grad_value, grad_output, grad_in, grad_out, table = map(
+        scatter, (grad_query, grad_key, grad_value, grad_output, grad_in, grad_out, table)
+    )
     weigh = lambda weight, grad: jnp.sum(weight.astype(F32) * grad, axis=1)
     grad_gain = weigh(w_query, grad_query) + weigh(w_key, grad_key) + weigh(w_value, grad_value)
     return (

time: 305 us -> 291 us (0.954)
  local copies, waits for them, and re-layouts: 21.3 us -> 2.44 us
  Pallas kernels: 277 us -> 286 us
  other arithmetic: 4.32 us -> 0.7 us
    pallas_call x0 -> x2, Pallas kernels: none -> 10.2 us  [the longest x1 7.71 us: finish(): pl.pallas_call(finish_kernel, name='finish', grid=(tokens // LENGTH,), in...]
    unnamed x41 -> x3, local copies, waits for them, and re-layouts: 7.32 us -> 0.61 us
    slice x12 -> x0, local copies, waits for them, and re-layouts: 5.04 us -> none  [the longest x2 1.66 us: ordered(): one[:, at * GROUP_ROWS:(at + 1) * GROUP_ROWS]]
    reshape x5 -> x0, local copies, waits for them, and re-layouts: 4.53 us -> none  [the longest x2 2.6 us: shards(): sums[0:2 * PARTS:2].reshape(PARTS, rows, OWNERS, SHARE)]
where the time goes in v4:
time: 291 us; the launch traced here: 290 us
  Pallas kernels  286 us (98%)
    pallas_call x1, Pallas kernels, feed(): pl.pallas_call(partial(feed_kernel, fast=fast), name='feed', grid=(PARTS...  107 us
    pallas_call x1, Pallas kernels, back(): pl.pallas_call(kernel, name='back', grid=(GROUPS + 1, seqs), in_specs=[x_...  87.7 us
    pallas_call x1, Pallas kernels, attend(): pl.pallas_call(kernel, name='attend', grid=(GROUPS, seqs), in_specs=in_sp...  81.3 us
    pallas_call x1, Pallas kernels, finish(): pl.pallas_call(finish_kernel, name='finish', grid=(tokens // LENGTH,), in...  7.71 us

profile of v4, /device:TPU:0, one launch (start us, length us, event | category | flops | bytes accessed | tf_op | source)
XLA Modules:
  0.0 290.1 jit_solution(6645362158815447783)
XLA Ops:
  0.6 0.7 fusion.5
  1.3 0.6 pad_bitcast_fusion.small_hbm.gains_ref
  1.9 2.5 arrange.1.shares_hbm.late_hbm
  4.4 81.3 %attend.1 = (bf16[3,4,768,512]{3,2,1,0:T(8,128)(2,1)}, bf16[3,4,4,512,512]{4,3,2,1,0:T(8,128)(2,1)}, f32[3,4,4,1,512]{4,3,2,1,0:T(1,128)}, bf16[3,4,256,512]{3,2...) custom-call(bf16[2048,768]{1,0:T(8,128)(2,1)} %x_ref.1, ...), custom_call_target="tpu_custom_call" | custom-call | tf_op jit(solution)/shard_map/attend/pallas_call | solution.py:617
  85.7 107.1 %feed.1 = (bf16[2048,768]{1,0:T(8,128)(2,1)}, f32[4,2,768]{2,1,0:T(2,128)}, bf16[2048,768]{1,0:T(8,128)(2,1)}, bf16[3,4,256,512]{3,2,1,0:T(8,128)(2,1)}, bf16[9,...) custom-call(bf16[2048,768]{1,0:T(8,128)(2,1)} %get-tuple-element.40.n2_hbm, ...), custom_call_target="tpu_custom_call" | custom-call | tf_op jit(solution)/shard_map/feed/pallas_call | solution.py:808
  192.9 87.7 %back.1 = (bf16[2048,768]{1,0:T(8,128)(2,1)}, bf16[3,4,2,2,48,768]{5,4,3,2,1,0:T(8,128)(2,1)}, bf16[4,2,2,48,256]{4,3,2,1,0:T(8,128)(2,1)}, f32[6,48,768]{2,1,0:T(8,128)}, f32[4,48,256]{2,1,0:T(8,128)}) custom-call(bf16[2048,768]{1,0:T(8,128)(2,1)} %x_ref.1, bf16[2048,768]{1,0:T(8,128)(2,1)} %get-tuple-element.47.gm_ref, ...), custom_call_target="tpu_custom_call" | custom-call | tf_op jit(solution)/shard_map/back/pallas_call | solution.py:1040
  280.6 0.0 copy-start
  280.6 7.7 %finish.1 = (bf16[2048,768]{1,0:T(8,128)(2,1)}, bf16[2048,768]{1,0:T(8,128)(2,1)}, f32[48,768]{1,0:T(8,128)}, f32[48,768]{1,0:T(8,128)}, f32[48,768]{1,0:T(8,128...) custom-call(bf16[2048,768]{1,0:T(8,128)(2,1)} %get-tuple-element.46.o, ...), custom_call_target="tpu_custom_call" | custom-call | tf_op jit(solution)/shard_map/finish/pallas_call | solution.py:1114
  288.3 1.2 slice_bitcast_fusion
  289.5 0.0 copy-done
  289.5 0.6 copy.27
Async XLA Ops:
  280.6 9.0 %copy-start = (f32[4,2,768]{2,1,0:T(2,128)S(1)}, f32[4,2,768]{2,1,0:T(2,128)}, u32[]{:S(2)}) copy-start(f32[4,2,768]{2,1,0:T(2,128)} %get-tuple-element.83) | copy-start | bytes 73732

commit v5 on v4

--- a/solution.py
+++ b/solution.py
@@ -312,13 +312,12 @@
 
 
 ATTEND_PIECES, FEED_PIECES = 8, 4
-ATTEND_DIRECT = {1: (None, 0, None, 3, 5), 3: (2, 7, None, 12, 14), 6: (8, 13, None, 18, 20)}
-ATTEND_SHARED = {2: (0, 4, 7, 11, 13), 4: (4, 8, 12, 16, 18), 5: (6, 10, 15, 19, 21), 7: (11, 15, 19, 23, 25)}
-FEED_GATHER = {0: (0, 5, None, 10, 12), 1: (3, 8, None, 13, 15), 2: (6, 11, None, 16, 18), 3: (9, 14, None, 19, 21)}
+ATTEND_DIRECT = {2: (0, 6, None, 12, 14), 3: (3, 9, None, 15, 17), 5: (9, 14, None, 20, 22), 7: (14, 19, None, 25, 26)}
+ATTEND_SHARED = {1: (None, None, 0, 5, 7), 4: (7, 12, 16, 21, 23), 6: (12, 17, 21, 24, 25)}
+FEED_DIRECT = {1: (1, 7, None, 12, 15), 3: (6, 12, None, 18, 20)}
+FEED_SHARED = {0: (0, 4, 7, 11, 14), 2: (5, 8, 15, 19, 21)}
 FEED_SUMS = 5
-FEED_SCATTER = {
-    0: (8, 10, 15, 20, 23), 1: (11, 13, 18, 23, 26), 2: (16, 18, 23, 28, 31), 3: (19, 21, 26, 31, 34), 4: (24, 26, 31, 36, 39),
-}
+FEED_SCATTER = {0: (8, 13, 18, 24, 26), 1: (11, 15, 21, 26, 28), 2: (16, 18, 24, 31, 32), 3: (19, 21, 27, 32, 35), 4: (24, 26, 31, 37, 40)}
 BACK_BEFORE, BACK_SUMS = 4, 6
 BACK_SCATTER = {
     0: (0, 2, 7, 12, 15), 1: (3, 5, 10, 15, 18), 2: (6, 8, 13, 18, 21), 3: (9, 11, 16, 21, 24),
@@ -500,17 +499,18 @@
         if fast:
             small(False)
             first(1, 0)
+            main(0, 1, shared=True)
             read_small()
             first(1, 1)
             normalize(0)
             normalize(1)
             first(1, 2)
-            main(0, 1)
             normalize(2)
             normalize(3)
             first(3, 0)
             make_bands(0)
             first(3, 1)
+            main(1, 1, shared=True)
             make_bands(1)
             first(3, 2)
             make_bands(2)
@@ -529,20 +529,11 @@
     last_seq = seq == seqs - 1
     more = step + 1 < GROUPS * seqs
     cur_ref[...] = nxt_ref[...]
-    qkv_ref[0, 0] = nxt_ref[...]
-
-    @pl.when(last_seq & more)
-    def _():
-        load_group(group + 1).start()
-
-    @pl.when((seq == 0) & (group == GROUPS - 1))
-    def _():
-        load_output().start()
-        load_output().wait()
 
     next_seq = jnp.where(last_seq, 0, seq + 1)
     next_group = jnp.where(last_seq, jnp.minimum(group + 1, GROUPS - 1), group)
     point(0)
+    qkv_ref[0, 0] = cur_ref[...]
     score(cur_ref, group, seq, 1, sb_ref)
     soften(0, sa_ref)
     score(cur_ref, group, seq, 2, sa_ref)
@@ -553,11 +544,17 @@
 
     @pl.when(last_seq & more)
     def _():
+        load_group(group + 1).start()
         load_group(group + 1).wait()
 
     project(next_seq, nxt_ref)
     score(nxt_ref, next_group, next_seq, 0, sa_ref)
     soften(3, sb_ref)
+
+    @pl.when((seq == 0) & (group == GROUPS - 1))
+    def _():
+        load_output().start()
+        load_output().wait()
 
     @pl.when(group == GROUPS - 1)
     def _():
@@ -646,14 +643,15 @@
         here = place()
 
         def travel(slot):
-            def bring(phase, piece):
+            def bring(phase, piece, shared=False):
                 share = late_hbm.at[ATTEND_PIECES + piece]
-                gather_phase(phase, piece, here, share, gathered_hbm.at[piece], *sems_of)
+                gather_phase(phase, piece, here, share, gathered_hbm.at[piece], *sems_of, shared=shared)
 
             def add(phase, piece):
                 scatter_phase(phase, piece, here, parts_hbm.at[piece], sums_ref, *scratch)
 
-            run_slot(slot, FEED_GATHER, bring)
+            run_slot(slot, FEED_DIRECT, bring)
+            run_slot(slot, FEED_SHARED, partial(bring, shared=True))
             run_slot(slot, FEED_SCATTER, add)
 
         point = lambda at: travel(2 * step + at)
@@ -776,6 +774,8 @@
         for first in range(0, width, 256):
             stage(0, first, dwo_ref[:, first : first + 256].astype(BF16))
         keep(PARTS, 0).start()
+        if fast:
+            run_rest(2 * (PARTS + 1) * (res_ref.shape[0] // LENGTH), [FEED_DIRECT, FEED_SHARED, FEED_SCATTER], travel)
         keep(PARTS, 0).wait()
 
 
@@ -1058,11 +1058,12 @@
 
 
 def finish_kernel(
-    out_ref, ig_ref, early_ref, late_ref, tail_ref, wq_ref, wk_ref, wv_ref, win_ref, gains_ref,
-    output_ref, input_grad_ref, gq_ref, gk_ref, gv_ref, go_ref, gin_ref, gout_ref, gains_out_ref, table_ref,
+    out_ref, ig_ref, mean_ref, early_ref, late_ref, tail_ref, wq_ref, wk_ref, wv_ref, win_ref, gains_ref,
+    output_ref, input_grad_ref, pooled_ref, gq_ref, gk_ref, gv_ref, go_ref, gin_ref, gout_ref, first_ref, second_ref, table_ref,
 ):
     output_ref[...] = out_ref[...]
     input_grad_ref[...] = ig_ref[...]
+    pooled_ref[...] = mean_ref[...]
     step = pl.program_id(0)
 
     @pl.when(step == 0)
@@ -1100,14 +1101,17 @@
         second = weigh(win_ref, gin_ref)
         column = iota((SHARE, BLOCK), 1)
         lines = jnp.where(column == 0, first, jnp.where(column == 1, second, tail_ref[GROUPS, :, 0:BLOCK])).T
-        gains_out_ref[...] = lines[0:2, 0:SHARE] / gains_ref[0:2, 0:SHARE].astype(F32)
+        gains = lines[0:2, 0:SHARE] / gains_ref[0:2, 0:SHARE].astype(F32)
+        first_ref[...] = gains[0:1, :]
+        second_ref[...] = gains[1:2, :]
         table_ref[...] = lines[2:3, 0:TABLE_SHARE]
 
 
-def finish(out, ig, early, late, tail, wq, wk, wv, win, gains):
+def finish(out, ig, mean, early, late, tail, wq, wk, wv, win, gains):
     tokens, width = out.shape
     ff = win.shape[1]
     rows = pl.BlockSpec((LENGTH, width), lambda s: (s, 0))
+    means = pl.BlockSpec((1, 2, width), lambda s: (s, 0, 0))
     low = jax.ShapeDtypeStruct((tokens, width), BF16)
     square = whole((SHARE, width))
     table = lambda *shape: jax.ShapeDtypeStruct(shape, F32)
@@ -1116,19 +1120,20 @@
         name="finish",
         grid=(tokens // LENGTH,),
         in_specs=[
-            rows, rows, whole(early.shape), whole(late.shape), whole(tail.shape), square, square, square, whole((SHARE, ff)),
+            rows, rows, means, whole(early.shape), whole(late.shape), whole(tail.shape), square, square, square, whole((SHARE, ff)),
             whole(gains.shape),
         ],
         out_specs=[
-            rows, rows, square, square, square, square, whole((SHARE, ff)), whole((ff // OWNERS, width)), whole((2, SHARE)),
+            rows, rows, means, square, square, square, square, whole((SHARE, ff)), whole((ff // OWNERS, width)),
+            whole((1, SHARE)), whole((1, SHARE)),
             whole((1, TABLE_SHARE)),
         ],
         out_shape=[
-            low, low, table(SHARE, width), table(SHARE, width), table(SHARE, width), table(SHARE, width), table(SHARE, ff),
-            table(ff // OWNERS, width), table(2, SHARE), table(1, TABLE_SHARE),
+            low, low, table(*mean.shape), table(SHARE, width), table(SHARE, width), table(SHARE, width), table(SHARE, width), table(SHARE, ff),
+            table(ff // OWNERS, width), table(1, SHARE), table(1, SHARE), table(1, TABLE_SHARE),
         ],
         compiler_params=pltpu.CompilerParams(vmem_limit_bytes=VMEM_LIMIT),
-    )(out, ig, early, late, tail, wq, wk, wv, win, gains)
+    )(out, ig, mean, early, late, tail, wq, wk, wv, win, gains)
 
 
 def ordered(rows, w_query, w_key, w_value, w_output, w_in, w_out):
@@ -1174,10 +1179,11 @@
     early_sums = rest
     input_grad, group_parts, small_parts, *rest = back(hidden_in, gm, gains, early, qkv, p, inv, mix, dmix, parts, fast)
     if fast:
-        output, input_grad, *grads, gains, table = finish(
-            output, input_grad, early_sums[0], *rest, w_query, w_key, w_value, w_in, small
+        *results, grad_in, grad_out, first, second, table = finish(
+            output, input_grad, pooled, early_sums[0], *rest, w_query, w_key, w_value, w_in, small
         )
-        return (output, pooled, input_grad, gains[0], *grads[:4], table[0], gains[1], *grads[4:])
+        output, pooled, input_grad = results[0], results[2], results[1]
+        return (output, pooled, input_grad, first[0], *results[3:], table[0], second[0], grad_in, grad_out)
     sums = jnp.concatenate([parts, group_parts]).reshape(-1, width, width)
     table = small_parts.reshape(OWNERS, SHARE, SMALL)[:, :TABLE_SHARE, 0].reshape(-1)
     rows = width

time: 291 us -> 286 us (0.983)
    pallas_call x1, Pallas kernels: 107 us -> 103 us  [feed(): pl.pallas_call(partial(feed_kernel, fast=fast), name='feed', grid=(PARTS...]
    pallas_call x1, Pallas kernels: 87.7 us -> 91.2 us  [back(): pl.pallas_call(kernel, name='back', grid=(GROUPS + 1, seqs), in_specs=[x_...]
where the time goes in v5:
time: 286 us
  Pallas kernels  284 us (99%)
    pallas_call x1, Pallas kernels, feed(): pl.pallas_call(partial(feed_kernel, fast=fast), name='feed', grid=(PARTS...  103 us
    pallas_call x1, Pallas kernels, back(): pl.pallas_call(kernel, name='back', grid=(GROUPS + 1, seqs), in_specs=[x_...  91.2 us
    pallas_call x1, Pallas kernels, attend(): pl.pallas_call(kernel, name='attend', grid=(GROUPS, seqs), in_specs=in_sp...  79.1 us
    pallas_call x1, Pallas kernels, finish(): pl.pallas_call(finish_kernel, name='finish', grid=(tokens // LENGTH,), in...  7.92 us

profile of v5, /device:TPU:0, one launch (start us, length us, event | category | flops | bytes accessed | tf_op | source)
XLA Modules:
  0.0 286.1 jit_solution(7151407368467081516)
XLA Ops:
  0.6 0.7 fusion.5
  1.3 0.6 pad_bitcast_fusion.small_hbm.gains_ref
  1.9 2.5 arrange.1.shares_hbm.late_hbm
  4.4 79.1 %attend.1 = (bf16[3,4,768,512]{3,2,1,0:T(8,128)(2,1)}, bf16[3,4,4,512,512]{4,3,2,1,0:T(8,128)(2,1)}, f32[3,4,4,1,512]{4,3,2,1,0:T(1,128)}, bf16[3,4,256,512]{3,2...) custom-call(bf16[2048,768]{1,0:T(8,128)(2,1)} %x_ref.1, ...), custom_call_target="tpu_custom_call" | custom-call | tf_op jit(solution)/shard_map/attend/pallas_call | solution.py:614
  83.5 103.3 %feed.1 = (bf16[2048,768]{1,0:T(8,128)(2,1)}, f32[4,2,768]{2,1,0:T(2,128)}, bf16[2048,768]{1,0:T(8,128)(2,1)}, bf16[3,4,256,512]{3,2,1,0:T(8,128)(2,1)}, bf16[9,...) custom-call(bf16[2048,768]{1,0:T(8,128)(2,1)} %get-tuple-element.42.n2_hbm, ...), custom_call_target="tpu_custom_call" | custom-call | tf_op jit(solution)/shard_map/feed/pallas_call | solution.py:808
  186.8 91.2 %back.1 = (bf16[2048,768]{1,0:T(8,128)(2,1)}, bf16[3,4,2,2,48,768]{5,4,3,2,1,0:T(8,128)(2,1)}, bf16[4,2,2,48,256]{4,3,2,1,0:T(8,128)(2,1)}, f32[6,48,768]{2,1,0:T(8,128)}, f32[4,48,256]{2,1,0:T(8,128)}) custom-call(bf16[2048,768]{1,0:T(8,128)(2,1)} %x_ref.1, bf16[2048,768]{1,0:T(8,128)(2,1)} %get-tuple-element.49.gm_ref, ...), custom_call_target="tpu_custom_call" | custom-call | tf_op jit(solution)/shard_map/back/pallas_call | solution.py:1040
  278.0 7.9 %finish.1 = (bf16[2048,768]{1,0:T(8,128)(2,1)}, bf16[2048,768]{1,0:T(8,128)(2,1)}, f32[4,2,768]{2,1,0:T(2,128)}, f32[48,768]{1,0:T(8,128)}, f32[48,768]{1,0:T(8,...) custom-call(bf16[2048,768]{1,0:T(8,128)(2,1)} %get-tuple-element.48., ...), custom_call_target="tpu_custom_call" | custom-call | tf_op jit(solution)/shard_map/finish/pallas_call | solution.py:1118

commit v6 on v5

--- a/solution.py
+++ b/solution.py
@@ -140,7 +140,10 @@
     barrier = pltpu.get_barrier_semaphore()
     for device in (here["over_y"], here["over_x"], here["over_core"], *here["over_z"]):
         pl.semaphore_signal(barrier, inc=1, device_id=device, device_id_type=MESH_ID)
-    pl.semaphore_wait(barrier, DEPTH + 2)
+
+
+def await_greetings():
+    pl.semaphore_wait(pltpu.get_barrier_semaphore(), DEPTH + 2)
 
 
 def others(here):
@@ -320,7 +323,7 @@
 FEED_SCATTER = {0: (8, 13, 18, 24, 26), 1: (11, 15, 21, 26, 28), 2: (16, 18, 24, 31, 32), 3: (19, 21, 27, 32, 35), 4: (24, 26, 31, 37, 40)}
 BACK_BEFORE, BACK_SUMS = 4, 6
 BACK_SCATTER = {
-    0: (0, 2, 7, 12, 15), 1: (3, 5, 10, 15, 18), 2: (6, 8, 13, 18, 21), 3: (9, 11, 16, 21, 24),
+    0: (2, 4, 8, 13, 15), 1: (4, 6, 11, 16, 18), 2: (6, 9, 14, 19, 21), 3: (9, 12, 17, 22, 24),
     4: (12, 14, 19, 24, 27), 5: (16, 18, 23, 27, 29),
 }
 TAIL_SUMS = 4
@@ -690,6 +693,7 @@
         load_output().start()
         if fast:
             greet(here)
+            await_greetings()
         dwo_ref[...] = jnp.zeros_like(dwo_ref)
 
     @pl.when((part == PARTS) & (block == 0))
@@ -888,6 +892,10 @@
         @pl.when(step == 0)
         def _():
             greet(here)
+
+        @pl.when(step == 1)
+        def _():
+            await_greetings()
 
     @pl.when(group == 0)
     def _():

time: 286 us -> 285 us (level)
  no operation moved by 1% of the time
where the time goes in v6:
time: 285 us; the launch traced here: 284 us
  Pallas kernels  282 us (99%)
    pallas_call x1, Pallas kernels, feed(): pl.pallas_call(partial(feed_kernel, fast=fast), name='feed', grid=(PARTS...  103 us
    pallas_call x1, Pallas kernels, back(): pl.pallas_call(kernel, name='back', grid=(GROUPS + 1, seqs), in_specs=[x_...  89.2 us
    pallas_call x1, Pallas kernels, attend(): pl.pallas_call(kernel, name='attend', grid=(GROUPS, seqs), in_specs=in_sp...  79.1 us
    pallas_call x1, Pallas kernels, finish(): pl.pallas_call(finish_kernel, name='finish', grid=(tokens // LENGTH,), in...  7.92 us

profile of v6, /device:TPU:0, one launch (start us, length us, event | category | flops | bytes accessed | tf_op | source)
XLA Modules:
  0.0 284.1 jit_solution(12366515666352850877)
XLA Ops:
  0.6 0.7 fusion.5
  1.3 0.6 pad_bitcast_fusion.small_hbm.gains_ref
  1.9 2.5 arrange.1.shares_hbm.late_hbm
  4.4 79.1 %attend.1 = (bf16[3,4,768,512]{3,2,1,0:T(8,128)(2,1)}, bf16[3,4,4,512,512]{4,3,2,1,0:T(8,128)(2,1)}, f32[3,4,4,1,512]{4,3,2,1,0:T(1,128)}, bf16[3,4,256,512]{3,2...) custom-call(bf16[2048,768]{1,0:T(8,128)(2,1)} %x_ref.1, ...), custom_call_target="tpu_custom_call" | custom-call | tf_op jit(solution)/shard_map/attend/pallas_call | solution.py:617
  83.5 103.3 %feed.1 = (bf16[2048,768]{1,0:T(8,128)(2,1)}, f32[4,2,768]{2,1,0:T(2,128)}, bf16[2048,768]{1,0:T(8,128)(2,1)}, bf16[3,4,256,512]{3,2,1,0:T(8,128)(2,1)}, bf16[9,...) custom-call(bf16[2048,768]{1,0:T(8,128)(2,1)} %get-tuple-element.42.n2_hbm, ...), custom_call_target="tpu_custom_call" | custom-call | tf_op jit(solution)/shard_map/feed/pallas_call | solution.py:812
  186.8 89.2 %back.1 = (bf16[2048,768]{1,0:T(8,128)(2,1)}, bf16[3,4,2,2,48,768]{5,4,3,2,1,0:T(8,128)(2,1)}, bf16[4,2,2,48,256]{4,3,2,1,0:T(8,128)(2,1)}, f32[6,48,768]{2,1,0:T(8,128)}, f32[4,48,256]{2,1,0:T(8,128)}) custom-call(bf16[2048,768]{1,0:T(8,128)(2,1)} %x_ref.1, bf16[2048,768]{1,0:T(8,128)(2,1)} %get-tuple-element.49.gm_ref, ...), custom_call_target="tpu_custom_call" | custom-call | tf_op jit(solution)/shard_map/back/pallas_call | solution.py:1048
  276.0 7.9 %finish.1 = (bf16[2048,768]{1,0:T(8,128)(2,1)}, bf16[2048,768]{1,0:T(8,128)(2,1)}, f32[4,2,768]{2,1,0:T(2,128)}, f32[48,768]{1,0:T(8,128)}, f32[48,768]{1,0:T(8,...) custom-call(bf16[2048,768]{1,0:T(8,128)(2,1)} %get-tuple-element.48., ...), custom_call_target="tpu_custom_call" | custom-call | tf_op jit(solution)/shard_map/finish/pallas_call | solution.py:1126

commit v7 on v6

--- a/solution.py
+++ b/solution.py
@@ -687,13 +687,12 @@
 
     @pl.when(step == 0)
     def _():
+        if fast:
+            greet(here)
         weights(0, True)
         for at in range(res_ref.shape[0] // LENGTH):
             load_block(at, True)
         load_output().start()
-        if fast:
-            greet(here)
-            await_greetings()
         dwo_ref[...] = jnp.zeros_like(dwo_ref)
 
     @pl.when((part == PARTS) & (block == 0))
@@ -713,6 +712,12 @@
     def _():
         keep(part - 1, 0).wait()
         keep(part - 1, 1).wait()
+
+    if fast:
+
+        @pl.when(step == 0)
+        def _():
+            await_greetings()
 
     point(0)
 

time: 285 us -> 285 us (level)
  no operation moved by 1% of the time
where the time goes in v7:
time: 285 us; the launch traced here: 284 us
  Pallas kernels  282 us (99%)
    pallas_call x1, Pallas kernels, feed(): pl.pallas_call(partial(feed_kernel, fast=fast), name='feed', grid=(PARTS...  103 us
    pallas_call x1, Pallas kernels, back(): pl.pallas_call(kernel, name='back', grid=(GROUPS + 1, seqs), in_specs=[x_...  89.6 us
    pallas_call x1, Pallas kernels, attend(): pl.pallas_call(kernel, name='attend', grid=(GROUPS, seqs), in_specs=in_sp...  79.1 us
    pallas_call x1, Pallas kernels, finish(): pl.pallas_call(finish_kernel, name='finish', grid=(tokens // LENGTH,), in...  7.92 us

profile of v7, /device:TPU:0, one launch (start us, length us, event | category | flops | bytes accessed | tf_op | source)
XLA Modules:
  0.0 284.1 jit_solution(9420321275410663637)
XLA Ops:
  0.6 0.7 fusion.5
  1.3 0.6 pad_bitcast_fusion.small_hbm.gains_ref
  1.9 2.5 arrange.1.shares_hbm.late_hbm
  4.4 79.1 %attend.1 = (bf16[3,4,768,512]{3,2,1,0:T(8,128)(2,1)}, bf16[3,4,4,512,512]{4,3,2,1,0:T(8,128)(2,1)}, f32[3,4,4,1,512]{4,3,2,1,0:T(1,128)}, bf16[3,4,256,512]{3,2...) custom-call(bf16[2048,768]{1,0:T(8,128)(2,1)} %x_ref.1, ...), custom_call_target="tpu_custom_call" | custom-call | tf_op jit(solution)/shard_map/attend/pallas_call | solution.py:617
  83.5 102.9 %feed.1 = (bf16[2048,768]{1,0:T(8,128)(2,1)}, f32[4,2,768]{2,1,0:T(2,128)}, bf16[2048,768]{1,0:T(8,128)(2,1)}, bf16[3,4,256,512]{3,2,1,0:T(8,128)(2,1)}, bf16[9,...) custom-call(bf16[2048,768]{1,0:T(8,128)(2,1)} %get-tuple-element.42.n2_hbm, ...), custom_call_target="tpu_custom_call" | custom-call | tf_op jit(solution)/shard_map/feed/pallas_call | solution.py:817
  186.4 89.6 %back.1 = (bf16[2048,768]{1,0:T(8,128)(2,1)}, bf16[3,4,2,2,48,768]{5,4,3,2,1,0:T(8,128)(2,1)}, bf16[4,2,2,48,256]{4,3,2,1,0:T(8,128)(2,1)}, f32[6,48,768]{2,1,0:T(8,128)}, f32[4,48,256]{2,1,0:T(8,128)}) custom-call(bf16[2048,768]{1,0:T(8,128)(2,1)} %x_ref.1, bf16[2048,768]{1,0:T(8,128)(2,1)} %get-tuple-element.49.gm_ref, ...), custom_call_target="tpu_custom_call" | custom-call | tf_op jit(solution)/shard_map/back/pallas_call | solution.py:1053
  276.0 7.9 %finish.1 = (bf16[2048,768]{1,0:T(8,128)(2,1)}, bf16[2048,768]{1,0:T(8,128)(2,1)}, f32[4,2,768]{2,1,0:T(2,128)}, f32[48,768]{1,0:T(8,128)}, f32[48,768]{1,0:T(8,...) custom-call(bf16[2048,768]{1,0:T(8,128)(2,1)} %get-tuple-element.48., ...), custom_call_target="tpu_custom_call" | custom-call | tf_op jit(solution)/shard_map/finish/pallas_call | solution.py:1131
